TPU v7x, 32 devices: a whole 2x2x4 slice. The times are simulated.
32 devices in a mesh: seq: 16 (over z, x, core), head: 2 (over y).
Axes of the slice: x: 2, y: 2, z: 4, core: 2. Of those that a mesh axis runs over, the one named last changes fastest.
Arguments:
- q_rot: bfloat16 [12288, 1024], P('seq', 'head'), may hold values from -6 to 6
- k_rot: bfloat16 [12288, 256], P('seq', 'head'), may hold values from -6 to 6
- values: bfloat16 [12288, 256], P('seq', 'head'), may hold values from -6 to 6
- attn_out: bfloat16 [12288, 1024], P('seq', 'head'), may hold values from -4 to 4
- out_grad: bfloat16 [12288, 1024], P('seq', 'head'), may hold values from -6 to 6
- log_norm: float32 [8, 12288], P('head', 'seq')
- stretch_ids: int32 [16, 2], replicated, may hold values from 0 to 31, as said below
- q_weight: bfloat16 [4096, 1024], P(None, 'head'), may hold values from -0.09375 to 0.09375
- k_weight: bfloat16 [4096, 256], P(None, 'head'), may hold values from -0.09375 to 0.09375
- v_weight: bfloat16 [4096, 256], P(None, 'head'), may hold values from -0.09375 to 0.09375
Outputs:
- d_input: bfloat16 [12288, 4096], P(('seq', 'head'))
- key_grad: bfloat16 [12288, 256], P('seq', 'head')
- value_grad: bfloat16 [12288, 256], P('seq', 'head')
Inputs may be any that keep to these rules, and one draw needn't show every extreme that they name: `stretch_ids`: row j lists the two blocks of 384 consecutive positions whose tokens index j of seq holds, in its row order; every block appears once and the two entries of a row add up to 31.
All inputs are finite; a program needn't handle non-finite values.
Results may differ from a plain program's by a relative error of at most 0.0057.
Values may be sent and summed in bfloat16 or wider, within the bound.
A program may use at most 128 MiB of HBM per device.

v0:
```python
import math

import jax
import jax.numpy as jnp
from jax import lax
from jax.sharding import PartitionSpec as P

STOPS = 3


def shifted(x, axis, by):
    devices = lax.axis_size(axis)
    return lax.ppermute(x, axis, [(i, (i + by) % devices) for i in range(devices)])


def rotary_tables(positions, head_dim):
    half_dim = head_dim // 2
    inverse = jnp.exp(
        jnp.arange(half_dim, dtype=jnp.float32) * (-2.0 * math.log(500000.0) / head_dim)
    )
    angles = positions.astype(jnp.float32)[:, None] * inverse[None, :]
    cosine_table = jnp.cos(angles)
    sine_table = jnp.sin(angles)
    return (
        jnp.concatenate([cosine_table, cosine_table], axis=1),
        jnp.concatenate([sine_table, sine_table], axis=1),
    )


def unrotate(gradient, cosine_table, sine_table):
    half_dim = gradient.shape[-1] // 2
    rotated = gradient * sine_table
    return gradient * cosine_table + jnp.concatenate(
        [rotated[..., half_dim:], -rotated[..., :half_dim]], axis=-1
    )


def block_terms(
    query_rows,
    dout_rows,
    norm_rows,
    delta_rows,
    query_pos,
    key_block,
    value_block,
    key_pos,
    score_scale,
):
    scores = (
        jnp.einsum("thd,kd->htk", query_rows, key_block, preferred_element_type=jnp.float32)
        * score_scale
    )
    visible = key_pos[None, :] <= query_pos[:, None]
    attn_probs = jnp.where(visible[None, :, :], jnp.exp(scores - norm_rows[:, :, None]), 0.0)
    dprobs = jnp.einsum("thd,kd->htk", dout_rows, value_block, preferred_element_type=jnp.float32)
    dscores = (attn_probs * (dprobs - delta_rows[:, :, None])).astype(jnp.bfloat16)
    probs_low = attn_probs.astype(jnp.bfloat16)
    value_part = jnp.einsum("htk,thd->kd", probs_low, dout_rows, preferred_element_type=jnp.float32)
    query_part = jnp.einsum("htk,kd->thd", dscores, key_block, preferred_element_type=jnp.float32)
    key_part = jnp.einsum("htk,thd->kd", dscores, query_rows, preferred_element_type=jnp.float32)
    return (query_part, key_part, value_part)


def local(
    q_rot, k_rot, values, attn_out, out_grad, log_norm, stretch_ids, q_weight, k_weight, v_weight
):
    seq_count = lax.axis_size("seq")
    tok_rows, col_width = q_rot.shape
    head_dim = k_rot.shape[1]
    head_count = col_width // head_dim
    half_rows = tok_rows // 2
    score_scale = 1.0 / math.sqrt(head_dim)
    my_index = lax.axis_index("seq")
    offsets = jnp.arange(half_rows, dtype=jnp.int32)

    def block_positions(first_id, second_id):
        return jnp.concatenate([first_id * half_rows + offsets, second_id * half_rows + offsets])

    def owned(index):
        return lax.dynamic_index_in_dim(stretch_ids, jnp.mod(index, seq_count), 0, keepdims=False)

    own_ids = owned(my_index)
    query_pos = block_positions(own_ids[0], own_ids[1])
    queries = q_rot.reshape(tok_rows, head_count, head_dim)
    grads_out = out_grad.reshape(tok_rows, head_count, head_dim)
    outputs = attn_out.reshape(tok_rows, head_count, head_dim)
    delta_rows = jnp.sum(grads_out.astype(jnp.float32) * outputs.astype(jnp.float32), axis=2).T

    def stop_terms(key_block, value_block, key_pos):
        return block_terms(
            queries,
            grads_out,
            log_norm,
            delta_rows,
            query_pos,
            key_block,
            value_block,
            key_pos,
            score_scale,
        )

    key_block, value_block = (k_rot, values)
    query_acc, key_sum, value_sum = stop_terms(key_block, value_block, query_pos)
    for stop in range(1, STOPS):
        key_block, value_block = shifted((key_block, value_block), "seq", 1)
        key_sum, value_sum = shifted((key_sum, value_sum), "seq", 1)
        anchor_ids = owned(my_index - stop)
        query_part, key_part, value_part = stop_terms(
            key_block, value_block, block_positions(anchor_ids[0], anchor_ids[1])
        )
        query_acc = query_acc + query_part
        key_sum = key_sum + key_part
        value_sum = value_sum + value_part
    key_home, value_home = shifted((key_sum, value_sum), "seq", 1 - STOPS)
    cosine_table, sine_table = rotary_tables(query_pos, head_dim)
    query_grad = unrotate(query_acc * score_scale, cosine_table[:, None, :], sine_table[:, None, :])
    query_grad = query_grad.astype(jnp.bfloat16).reshape(tok_rows, col_width)
    key_grad = unrotate(key_home * score_scale, cosine_table, sine_table).astype(jnp.bfloat16)
    value_grad = value_home.astype(jnp.bfloat16)
    contract = (((1,), (1,)), ((), ()))
    query_part = query_grad
    key_part = key_grad
    value_part = value_grad
    total = lax.dot_general(query_part, q_weight, contract, preferred_element_type=jnp.float32)
    total = total + lax.dot_general(
        key_part, k_weight, contract, preferred_element_type=jnp.float32
    )
    d_input = lax.psum_scatter(
        total + lax.dot_general(value_part, v_weight, contract, preferred_element_type=jnp.float32),
        "head",
        scatter_dimension=0,
        tiled=True,
    ).astype(jnp.bfloat16)
    return (d_input, key_grad, value_grad)


def solution(mesh):
    in_specs = (
        P("seq", "head"),
        P("seq", "head"),
        P("seq", "head"),
        P("seq", "head"),
        P("seq", "head"),
        P("head", "seq"),
        P(),
        P(None, "head"),
        P(None, "head"),
        P(None, "head"),
    )
    out_specs = (P(("seq", "head"), None), P("seq", "head"), P("seq", "head"))
    return jax.shard_map(local, mesh=mesh, in_specs=in_specs, out_specs=out_specs, check_vma=False)
```

profile of v0, /device:TPU:0, one launch (start us, length us, event | category | flops | bytes accessed | tf_op | source)
XLA Modules:
  0.0 261.7 jit_solution(15527294594403661135)
XLA Ops:
  7.7 2.6 collective-permute-start
  16.1 1.8 reshape.142
  17.9 1.7 reshape.144
  19.6 1.6 multiply_reduce_fusion
  22.5 2.6 %fusion.51 = f32[768,768,4]{1,0,2:T(8,128)S(1)} fusion(bf16[768,128]{1,0:T(8,128)(2,1)} %param.11, bf16[768,512]{1,0:T(8,128)(2,1)} %param.10), kind=kOutput, calls=%fused_computation.57 | convolution fusion | flops 603979776 | bytes 10420224 | tf_op jit(solution)/shard_map/thd,kd->htk/dot_general | solution.py:50
  26.4 3.4 %fusion.9 = bf16[4,768,768]{1,2,0:T(8,128)(2,1)S(1)} fusion(f32[768,768,4]{1,0,2:T(8,128)S(1)} %fusion.51, f32[4,768]{1,0:T(4,128)S(1)} %copy.35, f32[4,768]{1,0:T(4,128)S(1)} %copy-done.9, pred[768,768]{0,1:T(8,128)(4,1)S(1)} %get-tuple-element.16, bf16[768,128]{1,0:T(8,128)(2,1)S(1)} %copy-done.8, bf16[768,512]{1,0:T(8,128)(2,1)S(1)} %copy-done.4), kind=kOutput, calls=%fused_computation.15 | convolution fusion | flops 618135552 | bytes 15753216 | tf_op jit(solution)/shard_map/thd,kd->htk/dot_general | solution.py:55
  31.3 1.8 fusion.25
  33.1 1.6 collective-permute-start.7
  35.6 2.4 multiply_cosine_fusion
  38.1 2.3 fusion.49
  42.1 4.3 %fusion.5 = bf16[4,768,768]{1,2,0:T(8,128)(2,1)S(1)} fusion(f32[768,768,4]{1,0,2:T(8,128)S(1)} %fusion.49, f32[4,768]{1,0:T(4,128)S(1)} %copy.35, f32[4,768]{1,0:T(4,128)S(1)} %copy-done.9, pred[768,768]{0,1:T(8,128)(4,1)S(1)} %get-tuple-element.17, bf16[768,128]{1,0:T(8,128)(2,1)} %collective-permute-done.1, bf16[768,512]{1,0:T(8,128)(2,1)S(1)} %copy-done.4), kind=kOutput, calls=%fused_computation.9 | convolution fusion | flops 618135552 | bytes 15753216 | tf_op jit(solution)/shard_map/thd,kd->htk/dot_general | solution.py:55
  46.4 1.8 fusion.72
  49.7 2.0 fusion.34
  51.6 1.9 collective-permute-start.8
  54.9 1.8 fusion.31
  56.7 3.4 %fusion.1 = bf16[4,768,768]{1,2,0:T(8,128)(2,1)S(1)} fusion(f32[768,768,4]{1,0,2:T(8,128)S(1)} %fusion.47, f32[4,768]{1,0:T(4,128)S(1)} %copy.35, f32[4,768]{1,0:T(4,128)S(1)} %copy-done.9, pred[768,768]{0,1:T(8,128)(4,1)S(1)} %get-tuple-element.15, bf16[768,128]{1,0:T(8,128)(2,1)S(1)} %collective-permute-done.3, bf16[768,512]{1,0:T(8,128)(2,1)S(1)} %copy-done.4), kind=kOutput, calls=%fused_computation.3 | convolution fusion | flops 618135552 | bytes 15753216 | tf_op jit(solution)/shard_map/thd,kd->htk/dot_general | solution.py:55
  61.6 3.2 %collective-permute-start.6 = (f32[768,128]{1,0:T(8,128)S(1)}, f32[768,128]{1,0:T(8,128)S(1)}, u32[]{:S(2)}, u32[]{:S(2)}) collective-permute-start(f32[768,128]{1,0:T(8,128)S(1)} %add.118), channel_id=1, source_target_pairs={{0,28},{2,30},{4,0},{6,2},{8,4},{10,6},{12,8},{14,10},{16,12},{18,... | collective-permute-start | bytes 1179656 | tf_op jit(solution)/shard_map/ppermute | solution.py:13
  66.9 7.4 %collective-permute-done.6 = f32[768,128]{1,0:T(8,128)S(1)} collective-permute-done((f32[768,128]{1,0:T(8,128)S(1)}, f32[768,128]{1,0:T(8,128)S(1)}, u32[]{:S(2)}, u32[]{:S(2)}) %collective-permute-start.6) | collective-permute-done | bytes 393248 | tf_op jit(solution)/shard_map/ppermute | solution.py:13
  76.6 2.3 fusion.53
  82.2 6.4 %fusion.91 = f32[768,4096]{1,0:T(8,128)} fusion(bf16[768,512]{0,1:T(8,128)(2,1)S(1)} %bitcast.191, bf16[4096,512]{1,0:T(8,128)(2,1)S(1)} %copy-done.7), kind=kOutput, calls=%fused_computation.118 | convolution fusion | flops 3221225472 | bytes 17563648 | tf_op jit(solution)/shard_map/dot_general | solution.py:124
  88.6 1.8 fusion.92
  90.4 11.3 %add_add_fusion = f32[768,4096]{1,0:T(8,128)} fusion(f32[768,4096]{1,0:T(8,128)} %fusion.91, f32[768,4096]{1,0:T(8,128)S(1)} %fusion.92, bf16[768,128]{1,0:T(8,128)(2,1)} %collective-permute-done.9, bf16[4096,128]{1,0:T(8,128)(2,1)S(1)} %copy-done.3), kind=kOutput, calls=%fused_computation | convolution fusion | flops 811597824 | bytes 38993920 | tf_op jit(solution)/shard_map/dot_general | solution.py:129
  101.8 146.5 %reduce-scatter.2.cloned.1.call-done = f32[384,4096]{1,0:T(8,128)} async-done(((f32[768,4096]{1,0:T(8,128)}), f32[384,4096]{1,0:T(8,128)}) %reduce-scatter.2.cloned.1.call-update) | async-done | bytes 6291472 | tf_op jit(solution)/shard_map/reduce_scatter | solution.py:128
  248.3 4.9 %convert_element_type.59 = bf16[384,4096]{1,0:T(8,128)(2,1)} convert(f32[384,4096]{1,0:T(8,128)} %reduce-scatter.2.cloned.1.call-done) | non-fusion elementwise | flops 1572864 | bytes 9437184 | tf_op jit(solution)/shard_map/convert_element_type | solution.py:133
  (67 shorter events, 22.6 us)
Async XLA Ops:
  7.2 81.4 %copy-start = (bf16[4096,128]{1,0:T(8,128)(2,1)S(1)}, bf16[4096,128]{1,0:T(8,128)(2,1)}, u32[]{:S(2)}) copy-start(bf16[4096,128]{1,0:T(8,128)(2,1)} %param.18) | copy-start | bytes 3145732
  7.2 241.1 %reduce-scatter.2.cloned.1.call-start = ((), (), s32[]{:S(2)}) async-start(), calls=%async_computation.1 | async-start | bytes 18874368 | tf_op jit(solution)/shard_map/reduce_scatter | solution.py:128
  7.2 33.2 %collective-permute-start.1 = (bf16[768,128]{1,0:T(8,128)(2,1)}, bf16[768,128]{1,0:T(8,128)(2,1)}, u32[]{:S(2)}, u32[]{:S(2)}) collective-permute-start(bf16[768,128]{1,0:T(8,128)(2,1)} %param.12), channel_id=1, source_target_pairs={{0,2},{2,4},{4,6},{6,8},{8,10},{10,12},{12,14},{14,16},{16,18},{18... | collective-permute-start | bytes 589832 | tf_op jit(solution)/shard_map/ppermute | solution.py:13
  7.7 30.3 %collective-permute-start = (bf16[768,128]{1,0:T(8,128)(2,1)}, bf16[768,128]{1,0:T(8,128)(2,1)}, u32[]{:S(2)}, u32[]{:S(2)}) collective-permute-start(bf16[768,128]{1,0:T(8,128)(2,1)} %param.11), channel_id=1, source_target_pairs={{0,2},{2,4},{4,6},{6,8},{8,10},{10,12},{12,14},{14,16},{16,18},{18... | collective-permute-start | bytes 589832 | tf_op jit(solution)/shard_map/ppermute | solution.py:13
  16.1 10.2 %copy-start.9 = (f32[4,768]{1,0:T(4,128)S(1)}, f32[4,768]{1,0:T(4,128)}, u32[]{:S(2)}) copy-start(f32[4,768]{1,0:T(4,128)} %param.15) | copy-start | bytes 36868
  21.3 5.1 %copy-start.4 = (bf16[768,512]{1,0:T(8,128)(2,1)S(1)}, bf16[768,512]{1,0:T(8,128)(2,1)}, u32[]{:S(2)}) copy-start(bf16[768,512]{1,0:T(8,128)(2,1)} %param.14) | copy-start | bytes 2359300
  21.3 5.1 %copy-start.8 = (bf16[768,128]{1,0:T(8,128)(2,1)S(1)}, bf16[768,128]{1,0:T(8,128)(2,1)}, u32[]{:S(2)}) copy-start(bf16[768,128]{1,0:T(8,128)(2,1)} %param.12) | copy-start | bytes 589828
  26.3 3.5 %copy-start.1 = (bf16[768,512]{1,0:T(8,128)(2,1)S(1)}, bf16[768,512]{1,0:T(8,128)(2,1)}, u32[]{:S(2)}) copy-start(bf16[768,512]{1,0:T(8,128)(2,1)} %param.10) | copy-start | bytes 2359300
  31.2 3.6 %copy-start.6 = (bf16[768,128]{1,0:T(8,128)(2,1)S(1)}, bf16[768,128]{1,0:T(8,128)(2,1)}, u32[]{:S(2)}) copy-start(bf16[768,128]{1,0:T(8,128)(2,1)} %param.11) | copy-start | bytes 589828
  31.2 16.9 %collective-permute-start.4 = (f32[768,128]{1,0:T(8,128)S(1)}, f32[768,128]{1,0:T(8,128)S(1)}, u32[]{:S(2)}, u32[]{:S(2)}) collective-permute-start(f32[768,128]{1,0:T(8,128)S(1)} %convolution_bitcast_fusion.2), channel_id=1, source_target_pairs={{0,2},{2,4},{4,6},{6,8},{8,10},{10,12},{12,14},{14,16},{16,18},{18... | collective-permute-start | bytes 1179656 | tf_op jit(solution)/shard_map/ppermute | solution.py:13
  33.1 16.5 %collective-permute-start.7 = (f32[768,128]{1,0:T(8,128)S(1)}, f32[768,128]{1,0:T(8,128)S(1)}, u32[]{:S(2)}, u32[]{:S(2)}) collective-permute-start(f32[768,128]{1,0:T(8,128)S(1)} %fusion.25), channel_id=1, source_target_pairs={{0,2},{2,4},{4,6},{6,8},{8,10},{10,12},{12,14},{14,16},{16,18},{18... | collective-permute-start | bytes 1179656 | tf_op jit(solution)/shard_map/ppermute | solution.py:13
  38.0 15.5 %collective-permute-start.2 = (bf16[768,128]{1,0:T(8,128)(2,1)}, bf16[768,128]{1,0:T(8,128)(2,1)S(1)}, u32[]{:S(2)}, u32[]{:S(2)}) collective-permute-start(bf16[768,128]{1,0:T(8,128)(2,1)} %collective-permute-done), channel_id=1, source_target_pairs={{0,2},{2,4},{4,6},{6,8},{8,10},{10,12},{12,14},{14,16},{16,18},{18... | collective-permute-start | bytes 589832 | tf_op jit(solution)/shard_map/ppermute | solution.py:13
  40.4 16.3 %collective-permute-start.3 = (bf16[768,128]{1,0:T(8,128)(2,1)}, bf16[768,128]{1,0:T(8,128)(2,1)S(1)}, u32[]{:S(2)}, u32[]{:S(2)}) collective-permute-start(bf16[768,128]{1,0:T(8,128)(2,1)} %collective-permute-done.1), channel_id=1, source_target_pairs={{0,2},{2,4},{4,6},{6,8},{8,10},{10,12},{12,14},{14,16},{16,18},{18... | collective-permute-start | bytes 589832 | tf_op jit(solution)/shard_map/ppermute | solution.py:13
  49.5 12.0 %collective-permute-start.5 = (f32[768,128]{1,0:T(8,128)S(1)}, f32[768,128]{1,0:T(8,128)S(1)}, u32[]{:S(2)}, u32[]{:S(2)}) collective-permute-start(f32[768,128]{1,0:T(8,128)S(1)} %fusion.37), channel_id=1, source_target_pairs={{0,2},{2,4},{4,6},{6,8},{8,10},{10,12},{12,14},{14,16},{16,18},{18... | collective-permute-start | bytes 1179656 | tf_op jit(solution)/shard_map/ppermute | solution.py:13
  51.6 14.0 %collective-permute-start.8 = (f32[768,128]{1,0:T(8,128)S(1)}, f32[768,128]{1,0:T(8,128)S(1)}, u32[]{:S(2)}, u32[]{:S(2)}) collective-permute-start(f32[768,128]{1,0:T(8,128)S(1)} %fusion.34), channel_id=1, source_target_pairs={{0,2},{2,4},{4,6},{6,8},{8,10},{10,12},{12,14},{14,16},{16,18},{18... | collective-permute-start | bytes 1179656 | tf_op jit(solution)/shard_map/ppermute | solution.py:13
  61.6 12.7 %collective-permute-start.6 = (f32[768,128]{1,0:T(8,128)S(1)}, f32[768,128]{1,0:T(8,128)S(1)}, u32[]{:S(2)}, u32[]{:S(2)}) collective-permute-start(f32[768,128]{1,0:T(8,128)S(1)} %add.118), channel_id=1, source_target_pairs={{0,28},{2,30},{4,0},{6,2},{8,4},{10,6},{12,8},{14,10},{16,12},{18,... | collective-permute-start | bytes 1179656 | tf_op jit(solution)/shard_map/ppermute | solution.py:13
  66.4 24.0 %collective-permute-start.9 = (bf16[768,128]{1,0:T(8,128)(2,1)}, bf16[768,128]{1,0:T(8,128)(2,1)}, u32[]{:S(2)}, u32[]{:S(2)}) collective-permute-start(bf16[768,128]{1,0:T(8,128)(2,1)} %add.122), channel_id=1, source_target_pairs={{0,28},{2,30},{4,0},{6,2},{8,4},{10,6},{12,8},{14,10},{16,12},{18,... | collective-permute-start | bytes 589832 | tf_op jit(solution)/shard_map/ppermute | solution.py:13
  74.3 0.9 copy-start.2
  80.0 2.2 copy-start.7
  80.6 8.0 %copy-start.5 = (bf16[768,128]{1,0:T(8,128)(2,1)S(1)}, bf16[768,128]{1,0:T(8,128)(2,1)}, u32[]{:S(2)}) copy-start(bf16[768,128]{1,0:T(8,128)(2,1)} %get-tuple-element.35) | copy-start | bytes 589828
  88.6 1.8 copy-start.3
Sparse Core Ops, SparseCore 0:
  101.9 146.3 reduce-scatter.1
where the time goes:
time: 262 us
  waiting for transfers between devices  154 us (59%)
  matrix products  50.1 us (19%)
  between operations  18.2 us (7%)
  other arithmetic  14.9 us (6%)
  starting transfers between devices  12.3 us (5%)
  local copies, waits for them, and re-layouts  12.2 us (5%)
    reduce_scatter x1, waiting for transfers between devices, local(): lax.psum_scatter(total + lax.dot_general(value_part, v_weight, contract,...  147 us
    ppermute x10, starting transfers between devices, shifted(): lax.ppermute(x, axis, [(i, (i + by) % devices) for i in range(devices)])  12.3 us
    dot_general x1, matrix products, local(): lax.dot_general(value_part, v_weight, contract, preferred_element_type=jn...  11.3 us
    dot_general x3, matrix products, block_terms(): jnp.einsum('thd,kd->htk', dout_rows, value_block, preferred_element_type=...  11.2 us
    ppermute x10, waiting for transfers between devices, shifted(): lax.ppermute(x, axis, [(i, (i + by) % devices) for i in range(devices)])  7.39 us
    dot_general x1, matrix products, local(): lax.dot_general(query_part, q_weight, contract, preferred_element_type=jn...  6.38 us
    dot_general x3, matrix products, block_terms(): jnp.einsum('thd,kd->htk', query_rows, key_block, preferred_element_type=j...  6.35 us
    dot_general x3, matrix products, block_terms(): jnp.einsum('htk,thd->kd', probs_low, dout_rows, preferred_element_type=jn...  5.55 us
  transfers between devices with their start and end apart: 11, of which 2 were waited for; matrix products, arithmetic and copies ran while one was open for 22% of the time, Pallas kernels for 0%

commit v1 on v0

v1 whole, which is shorter than its diff:
```python
import functools
import math

import jax
import jax.numpy as jnp
from jax import lax
from jax.experimental import pallas as pl
from jax.experimental.pallas import tpu as pltpu
from jax.sharding import PartitionSpec as P

STOPS = 3
LOG2E = math.log2(math.e)
F32 = jnp.float32
BF16 = jnp.bfloat16
NT = (((1,), (1,)), ((), ()))
NN = (((1,), (0,)), ((), ()))
VMEM_LIMIT = 48 * 1024 * 1024


def dot(a, b, dims):
    return lax.dot_general(a, b, dims, preferred_element_type=F32)


def rotary_tables(positions, head_dim):
    half_dim = head_dim // 2
    inverse = jnp.exp(
        jnp.arange(half_dim, dtype=F32) * (-2.0 * math.log(500000.0) / head_dim)
    )
    angles = inverse[:, None] * positions.astype(F32)[None, :]
    return jnp.stack([jnp.cos(angles), jnp.sin(angles)])


def lo_half(ids_ref, row):
    first, second = ids_ref[row, 0], ids_ref[row, 1]
    swap = (second < first).astype(jnp.int32)
    return swap, jnp.minimum(first, second)


def attend(q_ref, do_ref, norm_ref, delta_ref, dq_ref, kv_block, k_acc, q_half, k_half, masked):
    half = norm_ref.shape[2]
    heads = norm_ref.shape[1]
    keys, vals = kv_block(k_half)
    hd = keys.shape[1]
    scale = LOG2E / math.sqrt(hd)
    keys_t = keys.T
    rows = pl.ds(pl.multiple_of(q_half * half, half), half)
    dk = jnp.zeros((half, hd), F32)
    dv = jnp.zeros((half, hd), F32)
    if masked:
        visible = lax.broadcasted_iota(jnp.int32, (half, half), 0) <= lax.broadcasted_iota(
            jnp.int32, (half, half), 1
        )
    for h in range(heads):
        cols = slice(h * hd, (h + 1) * hd)
        q = q_ref[rows, cols]
        do = do_ref[rows, cols]
        probs = jnp.exp2(dot(keys, q, NT) * scale - norm_ref[q_half, h : h + 1, :])
        if masked:
            probs = jnp.where(visible, probs, 0.0)
        ds = (probs * (dot(vals, do, NT) - delta_ref[q_half, h : h + 1, :])).astype(BF16)
        dv = dv + dot(probs.astype(BF16), do, NN)
        dk = dk + dot(ds, q, NN)
        dq_ref[q_half, cols, :] += dot(keys_t, ds, NN)
    k_acc[k_half, :, :hd] += dk
    k_acc[k_half, :, hd:] += dv


def own_kernel(seq_count, ids_ref, q_ref, k_ref, v_ref, o_ref, do_ref, ln_ref, dq_ref, kv_ref, norm_ref, delta_ref):
    me = lax.axis_index("seq")
    heads, half = norm_ref.shape[1:]
    hd = k_ref.shape[1]
    for h in range(heads):
        cols = slice(h * hd, (h + 1) * hd)
        prod = do_ref[:, cols].astype(F32) * o_ref[:, cols].astype(F32)
        delta = jnp.sum(prod.T, axis=0, keepdims=True)
        for a in range(2):
            delta_ref[a, h : h + 1, :] = delta[:, a * half : (a + 1) * half]
    for a in range(2):
        norm_ref[a] = ln_ref[:, a * half : (a + 1) * half] * LOG2E
    dq_ref[...] = jnp.zeros_like(dq_ref)
    kv_ref[...] = jnp.zeros_like(kv_ref)

    def kv_block(b):
        rows = pl.ds(pl.multiple_of(b * half, half), half)
        return k_ref[rows, :], v_ref[rows, :]

    run = functools.partial(attend, q_ref, do_ref, norm_ref, delta_ref, dq_ref, kv_block, kv_ref)
    run(0, 0, True)
    run(1, 1, True)
    lo, _ = lo_half(ids_ref, me)
    run(1 - lo, lo, False)


def far_kernel(seq_count, ids_ref, q_ref, do_ref, norm_ref, delta_ref, dq0_ref, tab_ref, *rest):
    stops = STOPS - 1
    kv_refs, qg_ref, home_refs = rest[:stops], rest[stops], rest[stops + 1 : 2 * stops + 1]
    dq_ref, acc_ref = rest[2 * stops + 1 :]
    me = lax.axis_index("seq")
    heads, half = norm_ref.shape[1:]
    hd = kv_refs[0].shape[1] // 2
    dq_ref[...] = dq0_ref[...]
    lo, low_id = lo_half(ids_ref, me)
    for i in range(stops):
        kv_ref, acc = kv_refs[i], acc_ref.at[i]
        acc[...] = jnp.zeros_like(acc)
        row = lax.rem(me - (i + 1) + seq_count, seq_count)
        k_lo, k_low_id = lo_half(ids_ref, row)

        def kv_block(b, kv_ref=kv_ref):
            rows = pl.ds(pl.multiple_of(b * half, half), half)
            return kv_ref[rows, :hd], kv_ref[rows, hd:]

        run = functools.partial(attend, q_ref, do_ref, norm_ref, delta_ref, dq_ref, kv_block, acc)
        run(1 - lo, k_lo, False)
        lows = k_low_id < low_id
        run(jnp.where(lows, lo, 1 - lo), jnp.where(lows, k_lo, 1 - k_lo), False)
        for b in range(2):
            home_refs[i][b * half : (b + 1) * half, :] = acc[b].astype(BF16)
    scale = 1.0 / math.sqrt(hd)
    hh = hd // 2
    for a in range(2):
        cos = tab_ref[0, :, a * half : (a + 1) * half] * scale
        sin = tab_ref[1, :, a * half : (a + 1) * half] * scale
        for h in range(heads):
            first = dq_ref[a, h * hd : h * hd + hh, :]
            second = dq_ref[a, h * hd + hh : (h + 1) * hd, :]
            turned = jnp.concatenate(
                [first * cos + second * sin, second * cos - first * sin], axis=0
            )
            qg_ref[a * half : (a + 1) * half, h * hd : (h + 1) * hd] = turned.T.astype(BF16)


def finish_kernel(tab_ref, kv0_ref, *rest):
    home_refs, (kg_ref, vg_ref) = rest[:-2], rest[-2:]
    half = kv0_ref.shape[1]
    hd = kg_ref.shape[1]
    hh = hd // 2
    scale = 1.0 / math.sqrt(hd)
    for a in range(2):
        rows = slice(a * half, (a + 1) * half)
        total = kv0_ref[a]
        for ref in home_refs:
            total = total + ref[rows, :].astype(F32)
        cos = tab_ref[0, :, rows]
        sin = tab_ref[1, :, rows]
        cos = jnp.concatenate([cos, cos], axis=0).T * scale
        sin = jnp.concatenate([sin, -sin], axis=0).T * scale
        dk = total[:, :hd]
        swapped = jnp.concatenate([dk[:, hh:], dk[:, :hh]], axis=1)
        kg_ref[rows, :] = (dk * cos + swapped * sin).astype(BF16)
        vg_ref[rows, :] = total[:, hd:].astype(BF16)


def project_kernel(others, slots, r_ref, qg, kg, vg, qo, kvo, wq, wk, wv, p0, p1, p2, p3, out_ref, buf, sem):
    j = pl.program_id(0)
    pieces = (p0, p1, p2, p3)
    qw, kw = qg.shape[1], kg.shape[1]

    def copy(i):
        return pltpu.make_async_copy(pieces[i], buf.at[i % slots], sem.at[i])

    for i in range(4):
        @pl.when(j == max(0, i - slots + 1))
        def _(i=i):
            copy(i).start()

    total = dot(qg[...], wq[...], NT) + dot(kg[...], wk[...], NT) + dot(vg[...], wv[...], NT)
    for i in range(4):
        @pl.when(j == i)
        def _(i=i):
            copy(i).wait()

    slot = lax.rem(j, slots)
    width = qw + 2 * kw
    for s in range(others):
        total = total + dot(
            qo[:, s * qw : (s + 1) * qw], buf[slot, :, s * width : s * width + qw], NT
        )
        total = total + dot(
            kvo[:, s * 2 * kw : (s + 1) * 2 * kw],
            buf[slot, :, s * width + qw : (s + 1) * width],
            NT,
        )
    out_ref[...] = total.astype(BF16)


def params(**kw):
    return pltpu.CompilerParams(vmem_limit_bytes=VMEM_LIMIT, **kw)


def local(
    q_rot, k_rot, values, attn_out, out_grad, log_norm, stretch_ids, q_weight, k_weight, v_weight
):
    seq_count = lax.axis_size("seq")
    head_axis = lax.axis_size("head")
    tok, col_width = q_rot.shape
    hd = k_rot.shape[1]
    heads = col_width // hd
    half = tok // 2
    d_model = q_weight.shape[0]
    me = lax.axis_index("seq")
    my_head = lax.axis_index("head")
    quarter = d_model // 4
    part = lax.rem(me, 4)

    def shift_seq(x, by):
        return lax.ppermute(x, "seq", [(i, (i + by) % seq_count) for i in range(seq_count)])

    def swap_seq(x, bit):
        return lax.ppermute(x, "seq", [(i, i ^ bit) for i in range(seq_count)])

    def from_head(x, by):
        return lax.ppermute(x, "head", [(i, (i - by) % head_axis) for i in range(head_axis)])

    kv = jnp.concatenate([k_rot, values], axis=1)
    kvs = [shift_seq(kv, stop) for stop in range(1, STOPS)]

    def rows_of(w):
        return lax.dynamic_slice_in_dim(w, part * quarter, quarter, 0)

    mine = jnp.concatenate([rows_of(q_weight), rows_of(k_weight), rows_of(v_weight)], axis=1)
    got = [from_head(mine, s) for s in range(1, head_axis)]
    piece0 = got[0] if len(got) == 1 else jnp.concatenate(got, axis=1)
    piece2 = swap_seq(piece0, 2)
    piece1 = swap_seq(piece0, 1)
    piece3 = swap_seq(piece2, 1)

    own_ids = lax.dynamic_index_in_dim(stretch_ids, me, 0, keepdims=False)
    offsets = jnp.arange(half, dtype=jnp.int32)
    positions = (own_ids[:, None] * half + offsets[None, :]).reshape(tok)
    tables = rotary_tables(positions, hd)

    smem = pl.BlockSpec(memory_space=pltpu.SMEM)
    vmem = pl.BlockSpec(memory_space=pltpu.VMEM)
    unit = 10 * heads * half * half * hd
    dq0, kv0, norm, delta = pl.pallas_call(
        functools.partial(own_kernel, seq_count),
        out_shape=(
            jax.ShapeDtypeStruct((2, col_width, half), F32),
            jax.ShapeDtypeStruct((2, half, 2 * hd), F32),
            jax.ShapeDtypeStruct((2, heads, half), F32),
            jax.ShapeDtypeStruct((2, heads, half), F32),
        ),
        in_specs=[smem] + [vmem] * 6,
        out_specs=(vmem,) * 4,
        compiler_params=params(),
        cost_estimate=pl.CostEstimate(
            flops=3 * unit, bytes_accessed=5 * 2**20, transcendentals=3 * heads * half * half
        ),
        name="own_stop",
    )(stretch_ids, q_rot, k_rot, values, attn_out, out_grad, log_norm)

    query_grad, *homes = pl.pallas_call(
        functools.partial(far_kernel, seq_count),
        out_shape=(jax.ShapeDtypeStruct((tok, col_width), BF16),)
        + (jax.ShapeDtypeStruct((tok, 2 * hd), BF16),) * (STOPS - 1),
        in_specs=[smem] + [vmem] * (6 + STOPS - 1),
        out_specs=(vmem,) * STOPS,
        scratch_shapes=[
            pltpu.VMEM((2, col_width, half), F32),
            pltpu.VMEM((STOPS - 1, 2, half, 2 * hd), F32),
        ],
        compiler_params=params(),
        cost_estimate=pl.CostEstimate(
            flops=4 * unit, bytes_accessed=6 * 2**20, transcendentals=4 * heads * half * half
        ),
        name="far_stops",
    )(stretch_ids, q_rot, out_grad, norm, delta, dq0, tables, *kvs)

    homes = [shift_seq(x, -(i + 1)) for i, x in enumerate(homes)]
    out_rows = tok // head_axis

    def rows_for(x, h):
        return lax.dynamic_slice_in_dim(x, lax.rem(h, head_axis) * out_rows, out_rows, 0)

    def exchange(x):
        got = [
            from_head(rows_for(x, my_head + head_axis - s), s) for s in range(1, head_axis)
        ]
        return got[0] if len(got) == 1 else jnp.concatenate(got, axis=1)

    q_other = exchange(query_grad)
    key_grad, value_grad = pl.pallas_call(
        finish_kernel,
        out_shape=(jax.ShapeDtypeStruct((tok, hd), BF16),) * 2,
        in_specs=[vmem] * (1 + STOPS),
        out_specs=(vmem,) * 2,
        compiler_params=params(),
        name="finish_keys",
    )(tables, kv0, *homes)
    kv_other = exchange(jnp.concatenate([key_grad, value_grad], axis=1))

    others = head_axis - 1
    slots = 4 if others == 1 else 2
    full = lambda shape: pl.BlockSpec(shape, lambda j, r: (0, 0))
    wspec = lambda cols: pl.BlockSpec((quarter, cols), lambda j, r: (r[0] ^ j, 0))
    hbm = pl.BlockSpec(memory_space=pl.ANY)
    d_input = pl.pallas_call(
        functools.partial(project_kernel, others, slots),
        out_shape=jax.ShapeDtypeStruct((out_rows, d_model), BF16),
        grid_spec=pltpu.PrefetchScalarGridSpec(
            num_scalar_prefetch=1,
            grid=(4,),
            in_specs=[
                full((out_rows, col_width)),
                full((out_rows, hd)),
                full((out_rows, hd)),
                full((out_rows, col_width * others)),
                full((out_rows, 2 * hd * others)),
                wspec(col_width),
                wspec(hd),
                wspec(hd),
                hbm,
                hbm,
                hbm,
                hbm,
            ],
            out_specs=pl.BlockSpec((out_rows, quarter), lambda j, r: (0, r[0] ^ j)),
            scratch_shapes=[
                pltpu.VMEM((slots, quarter, (col_width + 2 * hd) * others), BF16),
                pltpu.SemaphoreType.DMA((4,)),
            ],
        ),
        compiler_params=params(),
        name="project",
    )(
        part.reshape(1),
        rows_for(query_grad, my_head),
        rows_for(key_grad, my_head),
        rows_for(value_grad, my_head),
        q_other,
        kv_other,
        q_weight,
        k_weight,
        v_weight,
        piece0,
        piece1,
        piece2,
        piece3,
    )
    return (d_input, key_grad, value_grad)


def solution(mesh):
    in_specs = (
        P("seq", "head"),
        P("seq", "head"),
        P("seq", "head"),
        P("seq", "head"),
        P("seq", "head"),
        P("head", "seq"),
        P(),
        P(None, "head"),
        P(None, "head"),
        P(None, "head"),
    )
    out_specs = (P(("seq", "head"), None), P("seq", "head"), P("seq", "head"))
    return jax.shard_map(local, mesh=mesh, in_specs=in_specs, out_specs=out_specs, check_vma=False)
```

time: 262 us -> 145 us (0.55)
  waiting for transfers between devices: 154 us -> 88.3 us
  matrix products: 50.1 us -> 0 us
  Pallas kernels: 0 us -> 26.9 us
  between operations: 18.2 us -> 0.97 us
  other arithmetic: 14.9 us -> 2.15 us
  starting transfers between devices: 12.3 us -> 15.9 us
    reduce_scatter x1 -> x0, waiting for transfers between devices: 147 us -> none  [local(): lax.psum_scatter(total + lax.dot_general(value_part, v_weight, contract,...]
    ppermute x10, waiting for transfers between devices: 7.39 us -> 88.3 us  [the longest x3 42.3 us: swap_seq(): return lax.ppermute(x, 'seq', [(i, i ^ bit) for i in range(seq_count)])]
    dot_general x18 -> x0, matrix products: 50.1 us -> none  [the longest x1 11.3 us: local(): lax.dot_general(value_part, v_weight, contract, preferred_element_type=jn...]
    pallas_call x0 -> x4, Pallas kernels: none -> 26.9 us  [the longest x1 9.55 us: local(): pl.pallas_call(functools.partial(project_kernel, others, slots), out_shap...]
    convert_element_type x4 -> x1, other arithmetic: 7.55 us -> 0.08 us  [rotary_tables(): angles = inverse[:, None] * positions.astype(F32)[None, :]]
    ppermute x10, starting transfers between devices: 12.3 us -> 15.9 us  [the longest x3 6.18 us: from_head(): lax.ppermute(x, 'head', [(i, (i - by) % head_axis) for i in range(head_ax...]
    unnamed x21 -> x26, local copies, waits for them, and re-layouts: 3.23 us -> 6.39 us
    dynamic_slice x1 -> x4, local copies, waits for them, and re-layouts: 0.86 us -> 3.59 us  [the longest x2 2.12 us: rows_for(): lax.dynamic_slice_in_dim(x, lax.rem(h, head_axis) * out_rows, out_rows, 0)]
  transfers between devices with their start and end apart: 11 -> 10, of which waited for: 2 -> 5; matrix products, arithmetic and copies ran while one was open for 22% -> 4% of each run, Pallas kernels for 0% -> 12%
where the time goes in v1:
time: 145 us
  waiting for transfers between devices  88.3 us (61%)
  Pallas kernels  26.9 us (19%)
  starting transfers between devices  15.9 us (11%)
  local copies, waits for them, and re-layouts  10.7 us (7%)
  other arithmetic  2.15 us (1%)
    ppermute x3, waiting for transfers between devices, swap_seq(): return lax.ppermute(x, 'seq', [(i, i ^ bit) for i in range(seq_count)])  42.3 us
    ppermute x3, waiting for transfers between devices, from_head(): lax.ppermute(x, 'head', [(i, (i - by) % head_axis) for i in range(head_ax...  37.7 us
    pallas_call x1, Pallas kernels, local(): pl.pallas_call(functools.partial(project_kernel, others, slots), out_shap...  9.55 us
    pallas_call x1, Pallas kernels, local(): pl.pallas_call(functools.partial(far_kernel, seq_count), out_shape=(jax.S...  9.45 us
    ppermute x4, waiting for transfers between devices, shift_seq(): lax.ppermute(x, 'seq', [(i, (i + by) % seq_count) for i in range(seq_coun...  8.26 us
    unnamed x26, local copies, waits for them, and re-layouts  6.39 us
    ppermute x3, starting transfers between devices, from_head(): lax.ppermute(x, 'head', [(i, (i - by) % head_axis) for i in range(head_ax...  6.18 us
    pallas_call x1, Pallas kernels, local(): pl.pallas_call(functools.partial(own_kernel, seq_count), out_shape=(jax.S...  5.75 us
  transfers between devices with their start and end apart: 10, of which 5 were waited for; matrix products, arithmetic and copies ran while one was open for 4% of the time, Pallas kernels for 12%

profile of v1, /device:TPU:0, one launch (start us, length us, event | category | flops | bytes accessed | tf_op | source)
XLA Modules:
  0.0 144.9 jit_solution(11922632247196721401)
XLA Ops:
  0.7 1.4 constant_dynamic-slice_fusion.2
  2.7 3.0 %collective-permute-start.6 = (bf16[1024,768]{1,0:T(8,128)(2,1)S(1)}, bf16[1024,768]{1,0:T(8,128)(2,1)}, u32[]{:S(2)}, u32[]{:S(2)}) collective-permute-start(bf16[1024,768]{1,0:T(8,128)(2,1)S(1)} %pad_maximum_fusion), channel_id=1, source_target_pairs={{0,1},{1,0},{2,3},{3,2},{4,5},{5,4},{6,7},{7,6},{8,9},{9,8},{10,11... | collective-permute-start | bytes 4718600 | tf_op jit(solution)/shard_map/ppermute | solution.py:213
  5.7 34.5 %collective-permute-done.6.p0 = bf16[1024,768]{1,0:T(8,128)(2,1)} collective-permute-done((bf16[1024,768]{1,0:T(8,128)(2,1)S(1)}, bf16[1024,768]{1,0:T(8,128)(2,1)}, u32[]{:S(2)}, u32[]{:S(2)}) %collective-permute-start.6) | collective-permute-done | bytes 1572896 | tf_op jit(solution)/shard_map/ppermute | solution.py:213
  40.2 1.7 %collective-permute-start.8 = (bf16[1024,768]{1,0:T(8,128)(2,1)}, bf16[1024,768]{1,0:T(8,128)(2,1)}, u32[]{:S(2)}, u32[]{:S(2)}) collective-permute-start(bf16[1024,768]{1,0:T(8,128)(2,1)} %collective-permute-done.6.p0), channel_id=1, source_target_pairs={{0,4},{2,6},{4,0},{6,2},{8,12},{10,14},{12,8},{14,10},{16,20},{18,... | collective-permute-start | bytes 4718600 | tf_op jit(solution)/shard_map/ppermute | solution.py:210
  44.0 2.5 %collective-permute-start.7 = (bf16[1024,768]{1,0:T(8,128)(2,1)}, bf16[1024,768]{1,0:T(8,128)(2,1)}, u32[]{:S(2)}, u32[]{:S(2)}) collective-permute-start(bf16[1024,768]{1,0:T(8,128)(2,1)} %collective-permute-done.6.p0), channel_id=1, source_target_pairs={{0,2},{2,0},{4,6},{6,4},{8,10},{10,8},{12,14},{14,12},{16,18},{18,... | collective-permute-start | bytes 4718600 | tf_op jit(solution)/shard_map/ppermute | solution.py:210
  46.5 42.3 %collective-permute-done.8.p2 = bf16[1024,768]{1,0:T(8,128)(2,1)} collective-permute-done((bf16[1024,768]{1,0:T(8,128)(2,1)}, bf16[1024,768]{1,0:T(8,128)(2,1)}, u32[]{:S(2)}, u32[]{:S(2)}) %collective-permute-start.8) | collective-permute-done | bytes 1572896 | tf_op jit(solution)/shard_map/ppermute | solution.py:210
  89.7 0.9 copy-done.5
  90.6 1.1 copy-done.6
  91.8 1.1 copy-done.7
  92.9 1.1 copy-done.8
  94.0 5.8 %own_stop.1 = (f32[2,512,384]{2,1,0:T(8,128)S(1)}, f32[2,384,256]{2,1,0:T(8,128)S(1)}, f32[2,4,384]{2,1,0:T(4,128)S(1)}, f32[2,4,384]{2,1,0:T(4,128)S(1)}) custom-call(s32[16,2]{1,0:T(8,128)S(1)} %copy.14.ids_ref, bf16[768,512]{1,0:T(8,128)(2,1)S(1)} %copy-done.7, bf16[768,128]{1,0:T(8,128)(2,1)S(1)} %copy-done.3, bf16[768,128]{1,0:T(8,128)(2,1)S(1)} %copy-done.5, ...), custom_call_target="tpu_custom_call" | custom-call | flops 2264924160 | bytes 5242880 | tf_op jit(solution)/shard_map/own_stop/pallas_call | solution.py:236
  99.8 9.4 %far_stops.1 = (bf16[768,512]{1,0:T(8,128)(2,1)S(1)}, bf16[768,256]{1,0:T(8,128)(2,1)}, bf16[768,256]{1,0:T(8,128)(2,1)}) custom-call(s32[16,2]{1,0:T(8,128)S(1)} %copy.14.ids_ref, bf16[768,512]{1,0:T(8,128)(2,1)S(1)} %copy-done.7, bf16[768,512]{1,0:T(8,128)(2,1)S(1)} %copy-done.9, f32[2,4,384]{2,1,0:T(4,128)S(1)} %get-tuple-element.12.norm_ref, ...), custom_call_target="tpu_custom_call" | custom-call | flops 3019898880 | bytes 6291456 | tf_op jit(solution)/shard_map/far_stops/pallas_call | solution.py:253
  110.2 2.6 %collective-permute-start.2 = (bf16[768,256]{1,0:T(8,128)(2,1)}, bf16[768,256]{1,0:T(8,128)(2,1)}, u32[]{:S(2)}, u32[]{:S(2)}) collective-permute-start(bf16[768,256]{1,0:T(8,128)(2,1)} %get-tuple-element.17), channel_id=1, source_target_pairs={{0,30},{2,0},{4,2},{6,4},{8,6},{10,8},{12,10},{14,12},{16,14},{18,... | collective-permute-start | bytes 1179656 | tf_op jit(solution)/shard_map/ppermute | solution.py:207
  112.7 2.5 %collective-permute-start.3 = (bf16[768,256]{1,0:T(8,128)(2,1)}, bf16[768,256]{1,0:T(8,128)(2,1)}, u32[]{:S(2)}, u32[]{:S(2)}) collective-permute-start(bf16[768,256]{1,0:T(8,128)(2,1)} %get-tuple-element.18), channel_id=1, source_target_pairs={{0,28},{2,30},{4,0},{6,2},{8,4},{10,6},{12,8},{14,10},{16,12},{18,... | collective-permute-start | bytes 1179656 | tf_op jit(solution)/shard_map/ppermute | solution.py:207
  115.2 1.2 constant_dynamic-slice_fusion.3
  116.4 1.6 %collective-permute-start.4 = (bf16[384,512]{1,0:T(8,128)(2,1)S(1)}, bf16[384,512]{1,0:T(8,128)(2,1)S(1)}, u32[]{:S(2)}, u32[]{:S(2)}) collective-permute-start(bf16[384,512]{1,0:T(8,128)(2,1)S(1)} %get-tuple-element.21), channel_id=1, source_target_pairs={{0,1},{1,0},{2,3},{3,2},{4,5},{5,4},{6,7},{7,6},{8,9},{9,8},{10,11... | collective-permute-start | bytes 1179656 | tf_op jit(solution)/shard_map/ppermute | solution.py:213
  118.0 4.0 %collective-permute-done.2.rest_0_ = bf16[768,256]{1,0:T(8,128)(2,1)} collective-permute-done((bf16[768,256]{1,0:T(8,128)(2,1)}, bf16[768,256]{1,0:T(8,128)(2,1)}, u32[]{:S(2)}, u32[]{:S(2)}) %collective-permute-start.2) | collective-permute-done | bytes 393248 | tf_op jit(solution)/shard_map/ppermute | solution.py:207
  122.0 4.2 %collective-permute-done.3.rest_1_ = bf16[768,256]{1,0:T(8,128)(2,1)} collective-permute-done((bf16[768,256]{1,0:T(8,128)(2,1)}, bf16[768,256]{1,0:T(8,128)(2,1)}, u32[]{:S(2)}, u32[]{:S(2)}) %collective-permute-start.3) | collective-permute-done | bytes 393248 | tf_op jit(solution)/shard_map/ppermute | solution.py:207
  126.3 2.2 %finish_keys.1 = (bf16[768,128]{1,0:T(8,128)(2,1)}, bf16[768,128]{1,0:T(8,128)(2,1)}) custom-call(f32[2,64,768]{2,1,0:T(8,128)S(1)} %pad_maximum_fusion.1.tab_ref, f32[2,384,256]{2,1,0:T(8,128)S(1)} %get-tuple-element.16.kv0_ref, bf16[768,256]{1,0:T(8,128)(2,1)} %collective-permute-done.2.rest_0_, bf16[768,256]{1,0:T(8,128)(2,1)} %collective-permute-done.3.rest_1_), custom_call_target="tpu_custom_call" | custom-call | tf_op jit(solution)/shard_map/finish_keys/pallas_call | solution.py:283
  128.4 1.0 fusion
  129.4 1.6 %collective-permute-start.5 = (bf16[384,256]{1,0:T(8,128)(2,1)S(1)}, bf16[384,256]{1,0:T(8,128)(2,1)S(1)}, u32[]{:S(2)}, u32[]{:S(2)}) collective-permute-start(bf16[384,256]{1,0:T(8,128)(2,1)S(1)} %fusion), channel_id=1, source_target_pairs={{0,1},{1,0},{2,3},{3,2},{4,5},{5,4},{6,7},{7,6},{8,9},{9,8},{10,11... | collective-permute-start | bytes 589832 | tf_op jit(solution)/shard_map/ppermute | solution.py:213
  131.0 1.0 constant_dynamic-slice_fusion.4
  131.9 3.2 %collective-permute-done.5.kvo = bf16[384,256]{1,0:T(8,128)(2,1)S(1)} collective-permute-done((bf16[384,256]{1,0:T(8,128)(2,1)S(1)}, bf16[384,256]{1,0:T(8,128)(2,1)S(1)}, u32[]{:S(2)}, u32[]{:S(2)}) %collective-permute-start.5) | collective-permute-done | bytes 196640 | tf_op jit(solution)/shard_map/ppermute | solution.py:213
  135.1 9.6 %project.1 = bf16[384,4096]{1,0:T(8,128)(2,1)} custom-call(s32[1]{0:T(128)} %bitcast.r_ref, bf16[384,512]{1,0:T(8,128)(2,1)S(1)} %get-tuple-element.22.qg, bf16[384,128]{1,0:T(8,128)(2,1)S(1)} %get-tuple-element.26.kg, bf16[384,128]{1,0:T(8,128)(2,1)S(1)} %get-tuple-element.25.vg, bf16[384,512]{1,0:T(8,128)(2,1)S(1)} %collective-permute-done.4.qo, ...), custom_call_target="tpu_custom_call" | custom-call | tf_op jit(solution)/shard_map/project/pallas_call | solution.py:298
  (39 shorter events, 4.4 us)
Async XLA Ops:
  0.6 1.5 %copy-start = (bf16[4096,128]{1,0:T(8,128)(2,1)S(1)}, bf16[4096,128]{1,0:T(8,128)(2,1)}, u32[]{:S(2)}) copy-start(bf16[4096,128]{1,0:T(8,128)(2,1)} %wk.1) | copy-start | bytes 3145732
  0.6 1.8 %copy-start.1 = (bf16[4096,128]{1,0:T(8,128)(2,1)S(1)}, bf16[4096,128]{1,0:T(8,128)(2,1)}, u32[]{:S(2)}) copy-start(bf16[4096,128]{1,0:T(8,128)(2,1)} %wv.1) | copy-start | bytes 3145732
  2.5 39.4 %copy-start.3 = (bf16[768,128]{1,0:T(8,128)(2,1)S(1)}, bf16[768,128]{1,0:T(8,128)(2,1)}, u32[]{:S(2)}) copy-start(bf16[768,128]{1,0:T(8,128)(2,1)} %k_ref.1) | copy-start | bytes 589828
  2.5 40.1 %copy-start.4 = (bf16[768,128]{1,0:T(8,128)(2,1)S(1)}, bf16[768,128]{1,0:T(8,128)(2,1)}, u32[]{:S(2)}) copy-start(bf16[768,128]{1,0:T(8,128)(2,1)} %v_ref.1) | copy-start | bytes 589828
  2.6 41.1 %copy-start.11 = (s32[16,2]{0,1:T(2,128)S(1)}, s32[16,2]{0,1:T(2,128)}, u32[]{:S(2)}) copy-start(s32[16,2]{0,1:T(2,128)} %param.16) | copy-start | bytes 388
  2.7 87.0 %copy-start.10 = (f32[4,768]{1,0:T(4,128)S(1)}, f32[4,768]{1,0:T(4,128)}, u32[]{:S(2)}) copy-start(f32[4,768]{1,0:T(4,128)} %ln_ref.1) | copy-start | bytes 36868
  2.7 37.5 %collective-permute-start.6 = (bf16[1024,768]{1,0:T(8,128)(2,1)S(1)}, bf16[1024,768]{1,0:T(8,128)(2,1)}, u32[]{:S(2)}, u32[]{:S(2)}) collective-permute-start(bf16[1024,768]{1,0:T(8,128)(2,1)S(1)} %pad_maximum_fusion), channel_id=1, source_target_pairs={{0,1},{1,0},{2,3},{3,2},{4,5},{5,4},{6,7},{7,6},{8,9},{9,8},{10,11... | collective-permute-start | bytes 4718600 | tf_op jit(solution)/shard_map/ppermute | solution.py:213
  40.2 48.5 %collective-permute-start.8 = (bf16[1024,768]{1,0:T(8,128)(2,1)}, bf16[1024,768]{1,0:T(8,128)(2,1)}, u32[]{:S(2)}, u32[]{:S(2)}) collective-permute-start(bf16[1024,768]{1,0:T(8,128)(2,1)} %collective-permute-done.6.p0), channel_id=1, source_target_pairs={{0,4},{2,6},{4,0},{6,2},{8,12},{10,14},{12,8},{14,10},{16,20},{18,... | collective-permute-start | bytes 4718600 | tf_op jit(solution)/shard_map/ppermute | solution.py:210
  43.3 56.5 %collective-permute-start = (bf16[768,256]{1,0:T(8,128)(2,1)}, bf16[768,256]{1,0:T(8,128)(2,1)}, u32[]{:S(2)}, u32[]{:S(2)}) collective-permute-start(bf16[768,256]{1,0:T(8,128)(2,1)} %constant_dynamic-update-slice_fusion), channel_id=1, source_target_pairs={{0,2},{2,4},{4,6},{6,8},{8,10},{10,12},{12,14},{14,16},{16,18},{18... | collective-permute-start | bytes 1179656 | tf_op jit(solution)/shard_map/ppermute | solution.py:207
  43.3 56.5 %collective-permute-start.1 = (bf16[768,256]{1,0:T(8,128)(2,1)}, bf16[768,256]{1,0:T(8,128)(2,1)}, u32[]{:S(2)}, u32[]{:S(2)}) collective-permute-start(bf16[768,256]{1,0:T(8,128)(2,1)} %constant_dynamic-update-slice_fusion), channel_id=1, source_target_pairs={{0,4},{2,6},{4,8},{6,10},{8,12},{10,14},{12,16},{14,18},{16,20},{1... | collective-permute-start | bytes 1179656 | tf_op jit(solution)/shard_map/ppermute | solution.py:207
  44.0 91.2 %collective-permute-start.7 = (bf16[1024,768]{1,0:T(8,128)(2,1)}, bf16[1024,768]{1,0:T(8,128)(2,1)}, u32[]{:S(2)}, u32[]{:S(2)}) collective-permute-start(bf16[1024,768]{1,0:T(8,128)(2,1)} %collective-permute-done.6.p0), channel_id=1, source_target_pairs={{0,2},{2,0},{4,6},{6,4},{8,10},{10,8},{12,14},{14,12},{16,18},{18,... | collective-permute-start | bytes 4718600 | tf_op jit(solution)/shard_map/ppermute | solution.py:210
  88.8 46.4 %collective-permute-start.9 = (bf16[1024,768]{1,0:T(8,128)(2,1)}, bf16[1024,768]{1,0:T(8,128)(2,1)}, u32[]{:S(2)}, u32[]{:S(2)}) collective-permute-start(bf16[1024,768]{1,0:T(8,128)(2,1)} %collective-permute-done.8.p2), channel_id=1, source_target_pairs={{0,2},{2,0},{4,6},{6,4},{8,10},{10,8},{12,14},{14,12},{16,18},{18,... | collective-permute-start | bytes 4718600 | tf_op jit(solution)/shard_map/ppermute | solution.py:210
  89.7 0.9 copy-start.5
  90.6 1.1 copy-start.6
  91.8 1.1 copy-start.7
  92.9 1.1 copy-start.8
  94.0 5.8 %copy-start.9 = (bf16[768,512]{1,0:T(8,128)(2,1)S(1)}, bf16[768,512]{1,0:T(8,128)(2,1)}, u32[]{:S(2)}) copy-start(bf16[768,512]{1,0:T(8,128)(2,1)} %do_ref.3) | copy-start | bytes 2359300
  109.3 0.9 copy-start.2
  110.2 11.9 %collective-permute-start.2 = (bf16[768,256]{1,0:T(8,128)(2,1)}, bf16[768,256]{1,0:T(8,128)(2,1)}, u32[]{:S(2)}, u32[]{:S(2)}) collective-permute-start(bf16[768,256]{1,0:T(8,128)(2,1)} %get-tuple-element.17), channel_id=1, source_target_pairs={{0,30},{2,0},{4,2},{6,4},{8,6},{10,8},{12,10},{14,12},{16,14},{18,... | collective-permute-start | bytes 1179656 | tf_op jit(solution)/shard_map/ppermute | solution.py:207
  112.7 13.5 %collective-permute-start.3 = (bf16[768,256]{1,0:T(8,128)(2,1)}, bf16[768,256]{1,0:T(8,128)(2,1)}, u32[]{:S(2)}, u32[]{:S(2)}) collective-permute-start(bf16[768,256]{1,0:T(8,128)(2,1)} %get-tuple-element.18), channel_id=1, source_target_pairs={{0,28},{2,30},{4,0},{6,2},{8,4},{10,6},{12,8},{14,10},{16,12},{18,... | collective-permute-start | bytes 1179656 | tf_op jit(solution)/shard_map/ppermute | solution.py:207
  116.4 15.5 %collective-permute-start.4 = (bf16[384,512]{1,0:T(8,128)(2,1)S(1)}, bf16[384,512]{1,0:T(8,128)(2,1)S(1)}, u32[]{:S(2)}, u32[]{:S(2)}) collective-permute-start(bf16[384,512]{1,0:T(8,128)(2,1)S(1)} %get-tuple-element.21), channel_id=1, source_target_pairs={{0,1},{1,0},{2,3},{3,2},{4,5},{5,4},{6,7},{7,6},{8,9},{9,8},{10,11... | collective-permute-start | bytes 1179656 | tf_op jit(solution)/shard_map/ppermute | solution.py:213
  129.4 5.7 %collective-permute-start.5 = (bf16[384,256]{1,0:T(8,128)(2,1)S(1)}, bf16[384,256]{1,0:T(8,128)(2,1)S(1)}, u32[]{:S(2)}, u32[]{:S(2)}) collective-permute-start(bf16[384,256]{1,0:T(8,128)(2,1)S(1)} %fusion), channel_id=1, source_target_pairs={{0,1},{1,0},{2,3},{3,2},{4,5},{5,4},{6,7},{7,6},{8,9},{9,8},{10,11... | collective-permute-start | bytes 589832 | tf_op jit(solution)/shard_map/ppermute | solution.py:213

commit v2 on v1

--- a/solution.py
+++ b/solution.py
@@ -151,21 +151,21 @@
         vg_ref[rows, :] = total[:, hd:].astype(BF16)
 
 
-def project_kernel(others, slots, r_ref, qg, kg, vg, qo, kvo, wq, wk, wv, p0, p1, p2, p3, out_ref, buf, sem):
+def project_kernel(others, slots, r_ref, qg, kg, vg, qo, kvo, wq, wk, wv, *rest):
     j = pl.program_id(0)
-    pieces = (p0, p1, p2, p3)
+    pieces, (out_ref, buf, sem) = rest[:8], rest[8:]
     qw, kw = qg.shape[1], kg.shape[1]
 
     def copy(i):
         return pltpu.make_async_copy(pieces[i], buf.at[i % slots], sem.at[i])
 
-    for i in range(4):
+    for i in range(8):
         @pl.when(j == max(0, i - slots + 1))
         def _(i=i):
             copy(i).start()
 
     total = dot(qg[...], wq[...], NT) + dot(kg[...], wk[...], NT) + dot(vg[...], wv[...], NT)
-    for i in range(4):
+    for i in range(8):
         @pl.when(j == i)
         def _(i=i):
             copy(i).wait()
@@ -184,6 +184,22 @@
     out_ref[...] = total.astype(BF16)
 
 
+def tie_kernel(*refs):
+    pass
+
+
+def tie(arrays, after):
+    hbm = pl.BlockSpec(memory_space=pl.ANY)
+    return pl.pallas_call(
+        tie_kernel,
+        out_shape=tuple(jax.ShapeDtypeStruct(x.shape, x.dtype) for x in arrays),
+        in_specs=[hbm] * (len(arrays) + 1),
+        out_specs=(hbm,) * len(arrays),
+        input_output_aliases={i: i for i in range(len(arrays))},
+        name="tie",
+    )(*arrays, after)
+
+
 def params(**kw):
     return pltpu.CompilerParams(vmem_limit_bytes=VMEM_LIMIT, **kw)
 
@@ -200,8 +216,8 @@
     d_model = q_weight.shape[0]
     me = lax.axis_index("seq")
     my_head = lax.axis_index("head")
-    quarter = d_model // 4
-    part = lax.rem(me, 4)
+    eighth = d_model // 8
+    part = lax.rem(me, 8)
 
     def shift_seq(x, by):
         return lax.ppermute(x, "seq", [(i, (i + by) % seq_count) for i in range(seq_count)])
@@ -215,15 +231,18 @@
     kv = jnp.concatenate([k_rot, values], axis=1)
     kvs = [shift_seq(kv, stop) for stop in range(1, STOPS)]
 
-    def rows_of(w):
-        return lax.dynamic_slice_in_dim(w, part * quarter, quarter, 0)
-
-    mine = jnp.concatenate([rows_of(q_weight), rows_of(k_weight), rows_of(v_weight)], axis=1)
-    got = [from_head(mine, s) for s in range(1, head_axis)]
-    piece0 = got[0] if len(got) == 1 else jnp.concatenate(got, axis=1)
-    piece2 = swap_seq(piece0, 2)
-    piece1 = swap_seq(piece0, 1)
-    piece3 = swap_seq(piece2, 1)
+    def piece_of(which):
+        def rows_of(w):
+            return lax.dynamic_slice_in_dim(w, which * eighth, eighth, 0)
+
+        return jnp.concatenate([rows_of(q_weight), rows_of(k_weight), rows_of(v_weight)], axis=1)
+
+    def fetch(x):
+        got = [from_head(x, s) for s in range(1, head_axis)]
+        return got[0] if len(got) == 1 else jnp.concatenate(got, axis=1)
+
+    near = fetch(piece_of(part))
+    later = piece_of(part ^ 6)
 
     own_ids = lax.dynamic_index_in_dim(stretch_ids, me, 0, keepdims=False)
     offsets = jnp.arange(half, dtype=jnp.int32)
@@ -250,6 +269,12 @@
         name="own_stop",
     )(stretch_ids, q_rot, k_rot, values, attn_out, out_grad, log_norm)
 
+    near, later = tie((near, later), norm)
+    over_x = swap_seq(near, 2)
+    over_z = swap_seq(near, 4)
+    over_y = fetch(later)
+    near_twin = swap_seq(near, 1)
+
     query_grad, *homes = pl.pallas_call(
         functools.partial(far_kernel, seq_count),
         out_shape=(jax.ShapeDtypeStruct((tok, col_width), BF16),)
@@ -267,6 +292,9 @@
         name="far_stops",
     )(stretch_ids, q_rot, out_grad, norm, delta, dq0, tables, *kvs)
 
+    over_x, over_z, over_y = tie((over_x, over_z, over_y), homes[0])
+    pieces = [near, over_x, over_z, over_y, near_twin]
+    pieces += [swap_seq(x, 1) for x in (over_x, over_z, over_y)]
     homes = [shift_seq(x, -(i + 1)) for i, x in enumerate(homes)]
     out_rows = tok // head_axis
 
@@ -291,16 +319,17 @@
     kv_other = exchange(jnp.concatenate([key_grad, value_grad], axis=1))
 
     others = head_axis - 1
-    slots = 4 if others == 1 else 2
+    slots = 8 if others == 1 else 2
     full = lambda shape: pl.BlockSpec(shape, lambda j, r: (0, 0))
-    wspec = lambda cols: pl.BlockSpec((quarter, cols), lambda j, r: (r[0] ^ j, 0))
+    which = lambda j, r: r[0] ^ (2 * (j % 4) + j // 4)
+    wspec = lambda cols: pl.BlockSpec((eighth, cols), lambda j, r: (which(j, r), 0))
     hbm = pl.BlockSpec(memory_space=pl.ANY)
     d_input = pl.pallas_call(
         functools.partial(project_kernel, others, slots),
         out_shape=jax.ShapeDtypeStruct((out_rows, d_model), BF16),
         grid_spec=pltpu.PrefetchScalarGridSpec(
             num_scalar_prefetch=1,
-            grid=(4,),
+            grid=(8,),
             in_specs=[
                 full((out_rows, col_width)),
                 full((out_rows, hd)),
@@ -310,15 +339,12 @@
                 wspec(col_width),
                 wspec(hd),
                 wspec(hd),
-                hbm,
-                hbm,
-                hbm,
-                hbm,
-            ],
-            out_specs=pl.BlockSpec((out_rows, quarter), lambda j, r: (0, r[0] ^ j)),
+            ]
+            + [hbm] * 8,
+            out_specs=pl.BlockSpec((out_rows, eighth), lambda j, r: (0, which(j, r))),
             scratch_shapes=[
-                pltpu.VMEM((slots, quarter, (col_width + 2 * hd) * others), BF16),
-                pltpu.SemaphoreType.DMA((4,)),
+                pltpu.VMEM((slots, eighth, (col_width + 2 * hd) * others), BF16),
+                pltpu.SemaphoreType.DMA((8,)),
             ],
         ),
         compiler_params=params(),
@@ -333,10 +359,7 @@
         q_weight,
         k_weight,
         v_weight,
-        piece0,
-        piece1,
-        piece2,
-        piece3,
+        *pieces,
     )
     return (d_input, key_grad, value_grad)
 

time: 145 us -> 97.5 us (0.67)
  waiting for transfers between devices: 88.3 us -> 26 us
  local copies, waits for them, and re-layouts: 10.7 us -> 21.6 us
  other arithmetic: 2.15 us -> 5.7 us
  starting transfers between devices: 15.9 us -> 13.6 us
  Pallas kernels: 26.9 us -> 28.6 us
    ppermute x3 -> x6, waiting for transfers between devices: 42.3 us -> 0.02 us  [swap_seq(): return lax.ppermute(x, 'seq', [(i, i ^ bit) for i in range(seq_count)])]
    ppermute x3 -> x4, waiting for transfers between devices: 37.7 us -> 17.6 us  [from_head(): lax.ppermute(x, 'head', [(i, (i - by) % head_axis) for i in range(head_ax...]
    unnamed x26 -> x60, local copies, waits for them, and re-layouts: 6.39 us -> 15.4 us
    ppermute x3 -> x4, starting transfers between devices: 6.18 us -> 4.05 us  [from_head(): lax.ppermute(x, 'head', [(i, (i - by) % head_axis) for i in range(head_ax...]
    concatenate x1 -> x2, other arithmetic: 0.13 us -> 1.92 us  [piece_of(): jnp.concatenate([rows_of(q_weight), rows_of(k_weight), rows_of(v_weight)]...]
    pallas_call x1, Pallas kernels: 9.55 us -> 11.1 us  [local(): pl.pallas_call(functools.partial(project_kernel, others, slots), out_shap...]
    ppermute x3 -> x6, starting transfers between devices: 4.24 us -> 3.77 us  [swap_seq(): return lax.ppermute(x, 'seq', [(i, i ^ bit) for i in range(seq_count)])]
  transfers between devices with their start and end apart: 10 -> 14, of which waited for: 5 -> 5; matrix products, arithmetic and copies ran while one was open for 4% -> 11% of each run, Pallas kernels for 12% -> 18%
where the time goes in v2:
time: 97.5 us; the launch traced here: 96.6 us
  Pallas kernels  28.6 us (29%)
  waiting for transfers between devices  26 us (27%)
  local copies, waits for them, and re-layouts  21.6 us (22%)
  starting transfers between devices  13.6 us (14%)
  other arithmetic  5.7 us (6%)
  between operations  1.07 us (1%)
    ppermute x4, waiting for transfers between devices, from_head(): lax.ppermute(x, 'head', [(i, (i - by) % head_axis) for i in range(head_ax...  17.6 us
    unnamed x60, local copies, waits for them, and re-layouts  15.4 us
    pallas_call x1, Pallas kernels, local(): pl.pallas_call(functools.partial(project_kernel, others, slots), out_shap...  11.1 us
    pallas_call x1, Pallas kernels, local(): pl.pallas_call(functools.partial(far_kernel, seq_count), out_shape=(jax.S...  9.57 us
    ppermute x4, waiting for transfers between devices, shift_seq(): lax.ppermute(x, 'seq', [(i, (i + by) % seq_count) for i in range(seq_coun...  8.43 us
    ppermute x4, starting transfers between devices, shift_seq(): lax.ppermute(x, 'seq', [(i, (i + by) % seq_count) for i in range(seq_coun...  5.78 us
    pallas_call x1, Pallas kernels, local(): pl.pallas_call(functools.partial(own_kernel, seq_count), out_shape=(jax.S...  5.76 us
    ppermute x4, starting transfers between devices, from_head(): lax.ppermute(x, 'head', [(i, (i - by) % head_axis) for i in range(head_ax...  4.05 us
  transfers between devices with their start and end apart: 14, of which 5 were waited for; matrix products, arithmetic and copies ran while one was open for 11% of the time, Pallas kernels for 18%

profile of v2, /device:TPU:0, one launch (start us, length us, event | category | flops | bytes accessed | tf_op | source)
XLA Modules:
  0.0 96.6 jit_solution(627236819797967168)
XLA Ops:
  0.6 1.7 %constant_dynamic-update-slice_fusion.1 = bf16[768,256]{1,0:T(8,128)(2,1)} fusion(bf16[768,128]{1,0:T(8,128)(2,1)} %k_ref.1), kind=kLoop, calls=%fused_computation.9 | loop fusion | bytes 393216
  2.3 1.7 %constant_dynamic-update-slice_fusion = bf16[768,256]{1,0:T(8,128)(2,1)} fusion(bf16[768,256]{1,0:T(8,128)(2,1)} %constant_dynamic-update-slice_fusion.1, bf16[768,128]{1,0:T(8,128)(2,1)} %v_ref.1), kind=kLoop, calls=%fused_computation.8 | loop fusion | bytes 393216 | tf_op jit(solution)/shard_map/concatenate | solution.py:231
  4.0 2.9 %collective-permute-start.1 = (bf16[768,256]{1,0:T(8,128)(2,1)}, bf16[768,256]{1,0:T(8,128)(2,1)}, u32[]{:S(2)}, u32[]{:S(2)}) collective-permute-start(bf16[768,256]{1,0:T(8,128)(2,1)} %constant_dynamic-update-slice_fusion), channel_id=1, source_target_pairs={{0,4},{2,6},{4,8},{6,10},{8,12},{10,14},{12,16},{14,18},{16,20},{1... | collective-permute-start | bytes 1179656 | tf_op jit(solution)/shard_map/ppermute | solution.py:223
  6.9 1.3 %constant_dynamic-slice_fusion.2 = (bf16[512,512]{1,0:T(8,128)(2,1)S(1)}, bf16[512,512]{1,0:T(8,128)(2,1)S(1)}) fusion(bf16[4096,512]{1,0:T(8,128)(2,1)} %wq.1, s32[]{:T(128)S(6)} %select_n.27, s32[]{:T(128)S(6)} %select_n.26), kind=kLoop, calls=%fused_computation.12 | loop fusion | bytes 2097160 | tf_op jit(solution)/shard_map/dynamic_slice | solution.py:236
  8.2 1.1 %constant_dynamic-slice_fusion = (bf16[512,128]{1,0:T(8,128)(2,1)S(1)}, bf16[512,128]{1,0:T(8,128)(2,1)S(1)}, bf16[512,128]{1,0:T(8,128)(2,1)S(1)}, bf16[512,128]{1,0:T(8,128)(2,1)S(1)}) fusion(bf16[4096,128]{1,0:T(8,128)(2,1)} %wv.1, s32[]{:T(128)S(6)} %select_n.27, s32[]{:T(128)S(6)} %select_n.26, bf16[4096,128]{1,0:T(8,128)(2,1)} %wk.1), kind=kLoop, calls=%fused_computation.10 | loop fusion | bytes 1048584 | tf_op jit(solution)/shard_map/dynamic_slice | solution.py:236
  10.4 1.5 %collective-permute-start.6 = (bf16[512,768]{1,0:T(8,128)(2,1)}, bf16[512,768]{1,0:T(8,128)(2,1)S(1)}, u32[]{:S(2)}, u32[]{:S(2)}) collective-permute-start(bf16[512,768]{1,0:T(8,128)(2,1)} %pad_maximum_fusion), channel_id=1, source_target_pairs={{0,1},{1,0},{2,3},{3,2},{4,5},{5,4},{6,7},{7,6},{8,9},{9,8},{10,11... | collective-permute-start | bytes 2359304 | tf_op jit(solution)/shard_map/ppermute | solution.py:229
  13.9 5.8 %own_stop.1 = (f32[2,512,384]{2,1,0:T(8,128)S(1)}, f32[2,384,256]{2,1,0:T(8,128)S(1)}, f32[2,4,384]{2,1,0:T(4,128)S(1)}, f32[2,4,384]{2,1,0:T(4,128)S(1)}) custom-call(s32[16,2]{1,0:T(8,128)S(1)} %copy.19.ids_ref, bf16[768,512]{1,0:T(8,128)(2,1)S(1)} %copy-done.18, bf16[768,128]{1,0:T(8,128)(2,1)S(1)} %copy-done.11, bf16[768,128]{1,0:T(8,128)(2,1)S(1)} %copy-done.12, ...), custom_call_target="tpu_custom_call" | custom-call | flops 2264924160 | bytes 5242880 | tf_op jit(solution)/shard_map/own_stop/pallas_call | solution.py:255
  21.2 1.1 %copy-done.23 = f32[2,512,384]{2,1,0:T(8,128)} copy-done((f32[2,512,384]{2,1,0:T(8,128)}, f32[2,512,384]{2,1,0:T(8,128)S(1)}, u32[]{:S(2)}) %copy-start.23) | copy-done | bytes 1572888
  23.0 1.5 %multiply_cosine_fusion = (f32[1,64,768]{2,1,0:T(8,128)}, f32[1,64,768]{2,1,0:T(8,128)}) fusion(f32[768]{0:T(1024)S(1)} %convert_element_type.11, f32[64]{0:T(128)S(1)} %multiply_exponential_fusion), kind=kLoop, calls=%fused_computation.6 | loop fusion | flops 49152 | bytes 396544 | tf_op jit(solution)/shard_map/cos | solution.py:30
  24.5 5.9 %collective-permute-done.6.refs_0_ = bf16[512,768]{1,0:T(8,128)(2,1)S(1)} collective-permute-done((bf16[512,768]{1,0:T(8,128)(2,1)}, bf16[512,768]{1,0:T(8,128)(2,1)S(1)}, u32[]{:S(2)}, u32[]{:S(2)}) %collective-permute-start.6) | collective-permute-done | bytes 786464 | tf_op jit(solution)/shard_map/ppermute | solution.py:229
  31.3 1.6 %collective-permute-start.8 = (bf16[512,768]{1,0:T(8,128)(2,1)}, bf16[512,768]{1,0:T(8,128)(2,1)S(1)}, u32[]{:S(2)}, u32[]{:S(2)}) collective-permute-start(bf16[512,768]{1,0:T(8,128)(2,1)} %get-tuple-element.26.rest_0_), channel_id=1, source_target_pairs={{0,8},{2,10},{4,12},{6,14},{8,0},{10,2},{12,4},{14,6},{16,24},{18,... | collective-permute-start | bytes 2359304 | tf_op jit(solution)/shard_map/ppermute | solution.py:226
  32.8 1.6 %collective-permute-start.7 = (bf16[512,768]{1,0:T(8,128)(2,1)}, bf16[512,768]{1,0:T(8,128)(2,1)S(1)}, u32[]{:S(2)}, u32[]{:S(2)}) collective-permute-start(bf16[512,768]{1,0:T(8,128)(2,1)} %get-tuple-element.26.rest_0_), channel_id=1, source_target_pairs={{0,4},{2,6},{4,0},{6,2},{8,12},{10,14},{12,8},{14,10},{16,20},{18,... | collective-permute-start | bytes 2359304 | tf_op jit(solution)/shard_map/ppermute | solution.py:226
  34.4 1.5 %collective-permute-start.9 = (bf16[512,768]{1,0:T(8,128)(2,1)}, bf16[512,768]{1,0:T(8,128)(2,1)S(1)}, u32[]{:S(2)}, u32[]{:S(2)}) collective-permute-start(bf16[512,768]{1,0:T(8,128)(2,1)} %get-tuple-element.27), channel_id=1, source_target_pairs={{0,1},{1,0},{2,3},{3,2},{4,5},{5,4},{6,7},{7,6},{8,9},{9,8},{10,11... | collective-permute-start | bytes 2359304 | tf_op jit(solution)/shard_map/ppermute | solution.py:229
  37.7 1.1 %copy-done.19 = bf16[768,512]{1,0:T(8,128)(2,1)S(1)} copy-done((bf16[768,512]{1,0:T(8,128)(2,1)S(1)}, bf16[768,512]{1,0:T(8,128)(2,1)}, u32[]{:S(2)}) %copy-start.19) | copy-done | bytes 786456
  40.0 1.4 %copy-done.24 = f32[2,512,384]{2,1,0:T(8,128)S(1)} copy-done((f32[2,512,384]{2,1,0:T(8,128)S(1)}, f32[2,512,384]{2,1,0:T(8,128)}, u32[]{:S(2)}) %copy-start.24) | copy-done | bytes 1572888
  42.1 9.6 %far_stops.1 = (bf16[768,512]{1,0:T(8,128)(2,1)S(1)}, bf16[768,256]{1,0:T(8,128)(2,1)}, bf16[768,256]{1,0:T(8,128)(2,1)}) custom-call(s32[16,2]{1,0:T(8,128)S(1)} %copy-done.16, bf16[768,512]{1,0:T(8,128)(2,1)S(1)} %copy-done.19, bf16[768,512]{1,0:T(8,128)(2,1)S(1)} %copy-done.21, f32[2,4,384]{2,1,0:T(4,128)S(1)} %copy-done.14, f32[2,4,384]{2,1,0:T(4,128)S(1)} %copy-done.26, ...), custom_call_target="tpu_custom_call" | custom-call | flops 3019898880 | bytes 6291456 | tf_op jit(solution)/shard_map/far_stops/pallas_call | solution.py:278
  52.6 2.3 %collective-permute-start.3 = (bf16[768,256]{1,0:T(8,128)(2,1)}, bf16[768,256]{1,0:T(8,128)(2,1)}, u32[]{:S(2)}, u32[]{:S(2)}) collective-permute-start(bf16[768,256]{1,0:T(8,128)(2,1)} %get-tuple-element.23), channel_id=1, source_target_pairs={{0,28},{2,30},{4,0},{6,2},{8,4},{10,6},{12,8},{14,10},{16,12},{18,... | collective-permute-start | bytes 1179656 | tf_op jit(solution)/shard_map/ppermute | solution.py:223
  58.0 5.5 %collective-permute-done.3.rest_1_ = bf16[768,256]{1,0:T(8,128)(2,1)} collective-permute-done((bf16[768,256]{1,0:T(8,128)(2,1)}, bf16[768,256]{1,0:T(8,128)(2,1)}, u32[]{:S(2)}, u32[]{:S(2)}) %collective-permute-start.3) | collective-permute-done | bytes 393248 | tf_op jit(solution)/shard_map/ppermute | solution.py:223
  63.5 1.2 %constant_dynamic-slice_fusion.6 = (bf16[384,512]{1,0:T(8,128)(2,1)S(1)}, bf16[384,512]{1,0:T(8,128)(2,1)S(1)}) fusion(bf16[768,512]{1,0:T(8,128)(2,1)} %copy-done.10, s32[]{:T(128)S(6)} %select_n.25, s32[]{:T(128)S(6)} %select_n.24), kind=kLoop, calls=%fused_computation.16 | loop fusion | bytes 1572872 | tf_op jit(solution)/shard_map/dynamic_slice | solution.py:302
  64.7 2.9 %collective-permute-done.2.rest_0_ = bf16[768,256]{1,0:T(8,128)(2,1)} collective-permute-done((bf16[768,256]{1,0:T(8,128)(2,1)}, bf16[768,256]{1,0:T(8,128)(2,1)}, u32[]{:S(2)}, u32[]{:S(2)}) %collective-permute-start.2) | collective-permute-done | bytes 393248 | tf_op jit(solution)/shard_map/ppermute | solution.py:223
  68.1 2.2 %finish_keys.1 = (bf16[768,128]{1,0:T(8,128)(2,1)}, bf16[768,128]{1,0:T(8,128)(2,1)}) custom-call(f32[2,64,768]{2,1,0:T(8,128)S(1)} %pad_maximum_fusion.2.tab_ref, f32[2,384,256]{2,1,0:T(8,128)S(1)} %copy-done.9, bf16[768,256]{1,0:T(8,128)(2,1)} %collective-permute-done.2.rest_0_, bf16[768,256]{1,0:T(8,128)(2,1)} %collective-permute-done.3.rest_1_), custom_call_target="tpu_custom_call" | custom-call | tf_op jit(solution)/shard_map/finish_keys/pallas_call | solution.py:311
  71.3 7.3 %collective-permute-done.4.qo = bf16[384,512]{1,0:T(8,128)(2,1)S(1)} collective-permute-done((bf16[384,512]{1,0:T(8,128)(2,1)S(1)}, bf16[384,512]{1,0:T(8,128)(2,1)S(1)}, u32[]{:S(2)}, u32[]{:S(2)}) %collective-permute-start.4) | collective-permute-done | bytes 393248 | tf_op jit(solution)/shard_map/ppermute | solution.py:229
  80.0 4.4 %collective-permute-done.5.kvo = bf16[384,256]{1,0:T(8,128)(2,1)S(1)} collective-permute-done((bf16[384,256]{1,0:T(8,128)(2,1)S(1)}, bf16[384,256]{1,0:T(8,128)(2,1)S(1)}, u32[]{:S(2)}, u32[]{:S(2)}) %collective-permute-start.5) | collective-permute-done | bytes 196640 | tf_op jit(solution)/shard_map/ppermute | solution.py:229
  85.4 11.1 %project.1 = bf16[384,4096]{1,0:T(8,128)(2,1)} custom-call(s32[1]{0:T(128)} %bitcast.r_ref, bf16[384,512]{1,0:T(8,128)(2,1)S(1)} %get-tuple-element.38.qg, bf16[384,128]{1,0:T(8,128)(2,1)S(1)} %get-tuple-element.42.kg, bf16[384,128]{1,0:T(8,128)(2,1)S(1)} %get-tuple-element.41.vg, bf16[384,512]{1,0:T(8,128)(2,1)S(1)} %collective-permute-done.4.qo, ...), custom_call_target="tpu_custom_call" | custom-call | tf_op jit(solution)/shard_map/project/pallas_call | solution.py:327
  (84 shorter events, 17.3 us)
Async XLA Ops:
  4.0 33.0 %collective-permute-start.1 = (bf16[768,256]{1,0:T(8,128)(2,1)}, bf16[768,256]{1,0:T(8,128)(2,1)}, u32[]{:S(2)}, u32[]{:S(2)}) collective-permute-start(bf16[768,256]{1,0:T(8,128)(2,1)} %constant_dynamic-update-slice_fusion), channel_id=1, source_target_pairs={{0,4},{2,6},{4,8},{6,10},{8,12},{10,14},{12,16},{14,18},{16,20},{1... | collective-permute-start | bytes 1179656 | tf_op jit(solution)/shard_map/ppermute | solution.py:223
  6.9 30.1 %collective-permute-start = (bf16[768,256]{1,0:T(8,128)(2,1)}, bf16[768,256]{1,0:T(8,128)(2,1)}, u32[]{:S(2)}, u32[]{:S(2)}) collective-permute-start(bf16[768,256]{1,0:T(8,128)(2,1)} %constant_dynamic-update-slice_fusion), channel_id=1, source_target_pairs={{0,2},{2,4},{4,6},{6,8},{8,10},{10,12},{12,14},{14,16},{16,18},{18... | collective-permute-start | bytes 1179656 | tf_op jit(solution)/shard_map/ppermute | solution.py:223
  9.4 3.8 %copy-start.11 = (bf16[768,128]{1,0:T(8,128)(2,1)S(1)}, bf16[768,128]{1,0:T(8,128)(2,1)}, u32[]{:S(2)}) copy-start(bf16[768,128]{1,0:T(8,128)(2,1)} %k_ref.1) | copy-start | bytes 589828
  9.4 3.8 %copy-start.12 = (bf16[768,128]{1,0:T(8,128)(2,1)S(1)}, bf16[768,128]{1,0:T(8,128)(2,1)}, u32[]{:S(2)}) copy-start(bf16[768,128]{1,0:T(8,128)(2,1)} %v_ref.1) | copy-start | bytes 589828
  9.4 3.8 %copy-start.17 = (bf16[768,512]{1,0:T(8,128)(2,1)S(1)}, bf16[768,512]{1,0:T(8,128)(2,1)}, u32[]{:S(2)}) copy-start(bf16[768,512]{1,0:T(8,128)(2,1)} %o_ref.1) | copy-start | bytes 2359300
  10.4 20.0 %collective-permute-start.6 = (bf16[512,768]{1,0:T(8,128)(2,1)}, bf16[512,768]{1,0:T(8,128)(2,1)S(1)}, u32[]{:S(2)}, u32[]{:S(2)}) collective-permute-start(bf16[512,768]{1,0:T(8,128)(2,1)} %pad_maximum_fusion), channel_id=1, source_target_pairs={{0,1},{1,0},{2,3},{3,2},{4,5},{5,4},{6,7},{7,6},{8,9},{9,8},{10,11... | collective-permute-start | bytes 2359304 | tf_op jit(solution)/shard_map/ppermute | solution.py:229
  12.9 6.7 %copy-start.15 = (s32[16,2]{1,0:T(8,128)}, s32[16,2]{1,0:T(8,128)S(1)}, u32[]{:S(2)}) copy-start(s32[16,2]{1,0:T(8,128)S(1)} %copy.19.ids_ref) | copy-start | bytes 388
  23.0 14.1 %copy-start.14 = (f32[2,4,384]{2,1,0:T(4,128)S(1)}, f32[2,4,384]{2,1,0:T(4,128)}, u32[]{:S(2)}) copy-start(f32[2,4,384]{2,1,0:T(4,128)} %copy-done.13) | copy-start | bytes 36868
  31.3 24.3 %collective-permute-start.8 = (bf16[512,768]{1,0:T(8,128)(2,1)}, bf16[512,768]{1,0:T(8,128)(2,1)S(1)}, u32[]{:S(2)}, u32[]{:S(2)}) collective-permute-start(bf16[512,768]{1,0:T(8,128)(2,1)} %get-tuple-element.26.rest_0_), channel_id=1, source_target_pairs={{0,8},{2,10},{4,12},{6,14},{8,0},{10,2},{12,4},{14,6},{16,24},{18,... | collective-permute-start | bytes 2359304 | tf_op jit(solution)/shard_map/ppermute | solution.py:226
  32.8 22.7 %collective-permute-start.7 = (bf16[512,768]{1,0:T(8,128)(2,1)}, bf16[512,768]{1,0:T(8,128)(2,1)S(1)}, u32[]{:S(2)}, u32[]{:S(2)}) collective-permute-start(bf16[512,768]{1,0:T(8,128)(2,1)} %get-tuple-element.26.rest_0_), channel_id=1, source_target_pairs={{0,4},{2,6},{4,0},{6,2},{8,12},{10,14},{12,8},{14,10},{16,20},{18,... | collective-permute-start | bytes 2359304 | tf_op jit(solution)/shard_map/ppermute | solution.py:226
  34.4 21.0 %collective-permute-start.9 = (bf16[512,768]{1,0:T(8,128)(2,1)}, bf16[512,768]{1,0:T(8,128)(2,1)S(1)}, u32[]{:S(2)}, u32[]{:S(2)}) collective-permute-start(bf16[512,768]{1,0:T(8,128)(2,1)} %get-tuple-element.27), channel_id=1, source_target_pairs={{0,1},{1,0},{2,3},{3,2},{4,5},{5,4},{6,7},{7,6},{8,9},{9,8},{10,11... | collective-permute-start | bytes 2359304 | tf_op jit(solution)/shard_map/ppermute | solution.py:229
  42.1 13.3 %copy-start.1 = (bf16[512,768]{1,0:T(8,128)(2,1)S(1)}, bf16[512,768]{1,0:T(8,128)(2,1)}, u32[]{:S(2)}) copy-start(bf16[512,768]{1,0:T(8,128)(2,1)} %get-tuple-element.26.rest_0_) | copy-start | bytes 2359300
  52.6 10.9 %collective-permute-start.3 = (bf16[768,256]{1,0:T(8,128)(2,1)}, bf16[768,256]{1,0:T(8,128)(2,1)}, u32[]{:S(2)}, u32[]{:S(2)}) collective-permute-start(bf16[768,256]{1,0:T(8,128)(2,1)} %get-tuple-element.23), channel_id=1, source_target_pairs={{0,28},{2,30},{4,0},{6,2},{8,4},{10,6},{12,8},{14,10},{16,12},{18,... | collective-permute-start | bytes 1179656 | tf_op jit(solution)/shard_map/ppermute | solution.py:223
  54.9 12.7 %collective-permute-start.2 = (bf16[768,256]{1,0:T(8,128)(2,1)}, bf16[768,256]{1,0:T(8,128)(2,1)}, u32[]{:S(2)}, u32[]{:S(2)}) collective-permute-start(bf16[768,256]{1,0:T(8,128)(2,1)} %get-tuple-element.22.refs_3_), channel_id=1, source_target_pairs={{0,30},{2,0},{4,2},{6,4},{8,6},{10,8},{12,10},{14,12},{16,14},{18,... | collective-permute-start | bytes 1179656 | tf_op jit(solution)/shard_map/ppermute | solution.py:223
  55.4 29.0 %collective-permute-start.10 = (bf16[512,768]{1,0:T(8,128)(2,1)S(1)}, bf16[512,768]{1,0:T(8,128)(2,1)}, u32[]{:S(2)}, u32[]{:S(2)}) collective-permute-start(bf16[512,768]{1,0:T(8,128)(2,1)S(1)} %copy-done.1), channel_id=1, source_target_pairs={{0,2},{2,0},{4,6},{6,4},{8,10},{10,8},{12,14},{14,12},{16,18},{18,... | collective-permute-start | bytes 2359304 | tf_op jit(solution)/shard_map/ppermute | solution.py:226
  57.5 10.6 %copy-start.9 = (f32[2,384,256]{2,1,0:T(8,128)S(1)}, f32[2,384,256]{2,1,0:T(8,128)}, u32[]{:S(2)}) copy-start(f32[2,384,256]{2,1,0:T(8,128)} %copy-done.8) | copy-start | bytes 2359300
  57.5 27.0 %collective-permute-start.11 = (bf16[512,768]{1,0:T(8,128)(2,1)}, bf16[512,768]{1,0:T(8,128)(2,1)S(1)}, u32[]{:S(2)}, u32[]{:S(2)}) collective-permute-start(bf16[512,768]{1,0:T(8,128)(2,1)} %get-tuple-element.28.rest_1_), channel_id=1, source_target_pairs={{0,2},{2,0},{4,6},{6,4},{8,10},{10,8},{12,14},{14,12},{16,18},{18,... | collective-permute-start | bytes 2359304 | tf_op jit(solution)/shard_map/ppermute | solution.py:226
  57.8 26.7 %collective-permute-start.12 = (bf16[512,768]{1,0:T(8,128)(2,1)}, bf16[512,768]{1,0:T(8,128)(2,1)S(1)}, u32[]{:S(2)}, u32[]{:S(2)}) collective-permute-start(bf16[512,768]{1,0:T(8,128)(2,1)} %get-tuple-element.29.rest_2_), channel_id=1, source_target_pairs={{0,2},{2,0},{4,6},{6,4},{8,10},{10,8},{12,14},{14,12},{16,18},{18,... | collective-permute-start | bytes 2359304 | tf_op jit(solution)/shard_map/ppermute | solution.py:226
  63.5 21.0 %collective-permute-start.13 = (bf16[512,768]{1,0:T(8,128)(2,1)}, bf16[512,768]{1,0:T(8,128)(2,1)}, u32[]{:S(2)}, u32[]{:S(2)}) collective-permute-start(bf16[512,768]{1,0:T(8,128)(2,1)} %get-tuple-element.30.rest_3_), channel_id=1, source_target_pairs={{0,2},{2,0},{4,6},{6,4},{8,10},{10,8},{12,14},{14,12},{16,18},{18,... | collective-permute-start | bytes 2359304 | tf_op jit(solution)/shard_map/ppermute | solution.py:226
  64.7 20.7 %copy-start.3 = (bf16[512,768]{1,0:T(8,128)(2,1)S(1)}, bf16[512,768]{1,0:T(8,128)(2,1)}, u32[]{:S(2)}) copy-start(bf16[512,768]{1,0:T(8,128)(2,1)} %get-tuple-element.29.rest_2_) | copy-start | bytes 2359300
  64.7 20.7 %copy-start.5 = (bf16[512,768]{1,0:T(8,128)(2,1)S(1)}, bf16[512,768]{1,0:T(8,128)(2,1)}, u32[]{:S(2)}) copy-start(bf16[512,768]{1,0:T(8,128)(2,1)} %get-tuple-element.28.rest_1_) | copy-start | bytes 2359300
  64.7 20.7 %copy-start.7 = (bf16[512,768]{1,0:T(8,128)(2,1)S(1)}, bf16[512,768]{1,0:T(8,128)(2,1)}, u32[]{:S(2)}) copy-start(bf16[512,768]{1,0:T(8,128)(2,1)} %get-tuple-element.30.rest_3_) | copy-start | bytes 2359300
  67.6 10.9 %collective-permute-start.4 = (bf16[384,512]{1,0:T(8,128)(2,1)S(1)}, bf16[384,512]{1,0:T(8,128)(2,1)S(1)}, u32[]{:S(2)}, u32[]{:S(2)}) collective-permute-start(bf16[384,512]{1,0:T(8,128)(2,1)S(1)} %get-tuple-element.37), channel_id=1, source_target_pairs={{0,1},{1,0},{2,3},{3,2},{4,5},{5,4},{6,7},{7,6},{8,9},{9,8},{10,11... | collective-permute-start | bytes 1179656 | tf_op jit(solution)/shard_map/ppermute | solution.py:229
  78.6 5.9 %collective-permute-start.5 = (bf16[384,256]{1,0:T(8,128)(2,1)S(1)}, bf16[384,256]{1,0:T(8,128)(2,1)S(1)}, u32[]{:S(2)}, u32[]{:S(2)}) collective-permute-start(bf16[384,256]{1,0:T(8,128)(2,1)S(1)} %fusion), channel_id=1, source_target_pairs={{0,1},{1,0},{2,3},{3,2},{4,5},{5,4},{6,7},{7,6},{8,9},{9,8},{10,11... | collective-permute-start | bytes 589832 | tf_op jit(solution)/shard_map/ppermute | solution.py:229
  (19 other events, 25.5 us)

commit v3 on v2

--- a/solution.py
+++ b/solution.py
@@ -14,7 +14,7 @@
 BF16 = jnp.bfloat16
 NT = (((1,), (1,)), ((), ()))
 NN = (((1,), (0,)), ((), ()))
-VMEM_LIMIT = 48 * 1024 * 1024
+VMEM_LIMIT = 127 * 512 * 1024
 
 
 def dot(a, b, dims):
@@ -130,8 +130,8 @@
             qg_ref[a * half : (a + 1) * half, h * hd : (h + 1) * hd] = turned.T.astype(BF16)
 
 
-def finish_kernel(tab_ref, kv0_ref, *rest):
-    home_refs, (kg_ref, vg_ref) = rest[:-2], rest[-2:]
+def finish_kernel(tab_ref, kv0_ref, after_ref, *rest):
+    home_refs, (kg_ref, vg_ref, both_ref) = rest[:-3], rest[-3:]
     half = kv0_ref.shape[1]
     hd = kg_ref.shape[1]
     hh = hd // 2
@@ -147,8 +147,12 @@
         sin = jnp.concatenate([sin, -sin], axis=0).T * scale
         dk = total[:, :hd]
         swapped = jnp.concatenate([dk[:, hh:], dk[:, :hh]], axis=1)
-        kg_ref[rows, :] = (dk * cos + swapped * sin).astype(BF16)
-        vg_ref[rows, :] = total[:, hd:].astype(BF16)
+        key_grad = (dk * cos + swapped * sin).astype(BF16)
+        value_grad = total[:, hd:].astype(BF16)
+        kg_ref[rows, :] = key_grad
+        vg_ref[rows, :] = value_grad
+        both_ref[rows, :hd] = key_grad
+        both_ref[rows, hd:] = value_grad
 
 
 def project_kernel(others, slots, r_ref, qg, kg, vg, qo, kvo, wq, wk, wv, *rest):
@@ -164,7 +168,8 @@
         def _(i=i):
             copy(i).start()
 
-    total = dot(qg[...], wq[...], NT) + dot(kg[...], wk[...], NT) + dot(vg[...], wv[...], NT)
+    own = jnp.concatenate([wq[...], wk[...], wv[...]], axis=1)
+    total = dot(jnp.concatenate([qg[...], kg[...], vg[...]], axis=1), own, NT)
     for i in range(8):
         @pl.when(j == i)
         def _(i=i):
@@ -173,15 +178,26 @@
     slot = lax.rem(j, slots)
     width = qw + 2 * kw
     for s in range(others):
-        total = total + dot(
-            qo[:, s * qw : (s + 1) * qw], buf[slot, :, s * width : s * width + qw], NT
+        grads = jnp.concatenate(
+            [qo[:, s * qw : (s + 1) * qw], kvo[:, s * 2 * kw : (s + 1) * 2 * kw]], axis=1
         )
-        total = total + dot(
-            kvo[:, s * 2 * kw : (s + 1) * 2 * kw],
-            buf[slot, :, s * width + qw : (s + 1) * width],
-            NT,
-        )
+        total = total + dot(grads, buf[slot, :, s * width : (s + 1) * width], NT)
     out_ref[...] = total.astype(BF16)
+
+
+def prep_kernel(r_ref, k, v, q0, k0, v0, q1, k1, v1, kv, near, later):
+    hd = k.shape[1]
+    qw = q0.shape[1]
+    kv[:, :hd] = k[...]
+    kv[:, hd:] = v[...]
+    for out, (a, b, c) in ((near, (q0, k0, v0)), (later, (q1, k1, v1))):
+        out[:, :qw] = a[...]
+        out[:, qw : qw + hd] = b[...]
+        out[:, qw + hd :] = c[...]
+
+
+def whole(shape):
+    return pl.BlockSpec(shape, lambda *_: (0,) * len(shape))
 
 
 def tie_kernel(*refs):
@@ -189,13 +205,14 @@
 
 
 def tie(arrays, after):
-    hbm = pl.BlockSpec(memory_space=pl.ANY)
+    hbm = pl.BlockSpec(memory_space=pltpu.HBM)
     return pl.pallas_call(
         tie_kernel,
         out_shape=tuple(jax.ShapeDtypeStruct(x.shape, x.dtype) for x in arrays),
         in_specs=[hbm] * (len(arrays) + 1),
         out_specs=(hbm,) * len(arrays),
         input_output_aliases={i: i for i in range(len(arrays))},
+        compiler_params=params(),
         name="tie",
     )(*arrays, after)
 
@@ -228,21 +245,31 @@
     def from_head(x, by):
         return lax.ppermute(x, "head", [(i, (i - by) % head_axis) for i in range(head_axis)])
 
-    kv = jnp.concatenate([k_rot, values], axis=1)
-    kvs = [shift_seq(kv, stop) for stop in range(1, STOPS)]
-
-    def piece_of(which):
-        def rows_of(w):
-            return lax.dynamic_slice_in_dim(w, which * eighth, eighth, 0)
-
-        return jnp.concatenate([rows_of(q_weight), rows_of(k_weight), rows_of(v_weight)], axis=1)
+    spot = jnp.stack([part, my_head])
+    wblock = lambda w, flip: pl.BlockSpec((eighth, w.shape[1]), lambda i, r: (r[0] ^ flip, 0))
+    weights = (q_weight, k_weight, v_weight)
+    joined = jax.ShapeDtypeStruct((eighth, col_width + 2 * hd), BF16)
+    kv, near, later = pl.pallas_call(
+        prep_kernel,
+        out_shape=(jax.ShapeDtypeStruct((tok, 2 * hd), BF16), joined, joined),
+        grid_spec=pltpu.PrefetchScalarGridSpec(
+            num_scalar_prefetch=1,
+            grid=(1,),
+            in_specs=[whole(k_rot.shape), whole(values.shape)]
+            + [wblock(w, 0) for w in weights]
+            + [wblock(w, 6) for w in weights],
+            out_specs=(whole((tok, 2 * hd)), whole(joined.shape), whole(joined.shape)),
+        ),
+        compiler_params=params(),
+        name="prep",
+    )(spot, k_rot, values, *weights, *weights)
 
     def fetch(x):
         got = [from_head(x, s) for s in range(1, head_axis)]
         return got[0] if len(got) == 1 else jnp.concatenate(got, axis=1)
 
-    near = fetch(piece_of(part))
-    later = piece_of(part ^ 6)
+    near = fetch(near)
+    kvs = [shift_seq(kv, stop) for stop in range(1, STOPS)]
 
     own_ids = lax.dynamic_index_in_dim(stretch_ids, me, 0, keepdims=False)
     offsets = jnp.arange(half, dtype=jnp.int32)
@@ -250,7 +277,7 @@
     tables = rotary_tables(positions, hd)
 
     smem = pl.BlockSpec(memory_space=pltpu.SMEM)
-    vmem = pl.BlockSpec(memory_space=pltpu.VMEM)
+    hbm = pl.BlockSpec(memory_space=pltpu.HBM)
     unit = 10 * heads * half * half * hd
     dq0, kv0, norm, delta = pl.pallas_call(
         functools.partial(own_kernel, seq_count),
@@ -260,8 +287,15 @@
             jax.ShapeDtypeStruct((2, heads, half), F32),
             jax.ShapeDtypeStruct((2, heads, half), F32),
         ),
-        in_specs=[smem] + [vmem] * 6,
-        out_specs=(vmem,) * 4,
+        grid=(1,),
+        in_specs=[smem]
+        + [whole(x.shape) for x in (q_rot, k_rot, values, attn_out, out_grad, log_norm)],
+        out_specs=(
+            whole((2, col_width, half)),
+            whole((2, half, 2 * hd)),
+            whole((2, heads, half)),
+            whole((2, heads, half)),
+        ),
         compiler_params=params(),
         cost_estimate=pl.CostEstimate(
             flops=3 * unit, bytes_accessed=5 * 2**20, transcendentals=3 * heads * half * half
@@ -279,8 +313,10 @@
         functools.partial(far_kernel, seq_count),
         out_shape=(jax.ShapeDtypeStruct((tok, col_width), BF16),)
         + (jax.ShapeDtypeStruct((tok, 2 * hd), BF16),) * (STOPS - 1),
-        in_specs=[smem] + [vmem] * (6 + STOPS - 1),
-        out_specs=(vmem,) * STOPS,
+        grid=(1,),
+        in_specs=[smem]
+        + [whole(x.shape) for x in (q_rot, out_grad, norm, delta, dq0, tables, *kvs)],
+        out_specs=(whole((tok, col_width)),) + (whole((tok, 2 * hd)),) * (STOPS - 1),
         scratch_shapes=[
             pltpu.VMEM((2, col_width, half), F32),
             pltpu.VMEM((STOPS - 1, 2, half, 2 * hd), F32),
@@ -292,10 +328,6 @@
         name="far_stops",
     )(stretch_ids, q_rot, out_grad, norm, delta, dq0, tables, *kvs)
 
-    over_x, over_z, over_y = tie((over_x, over_z, over_y), homes[0])
-    pieces = [near, over_x, over_z, over_y, near_twin]
-    pieces += [swap_seq(x, 1) for x in (over_x, over_z, over_y)]
-    homes = [shift_seq(x, -(i + 1)) for i, x in enumerate(homes)]
     out_rows = tok // head_axis
 
     def rows_for(x, h):
@@ -308,22 +340,29 @@
         return got[0] if len(got) == 1 else jnp.concatenate(got, axis=1)
 
     q_other = exchange(query_grad)
-    key_grad, value_grad = pl.pallas_call(
+    homes = [shift_seq(x, -(i + 1)) for i, x in enumerate(homes)]
+    over_x, over_z, over_y = tie((over_x, over_z, over_y), homes[0])
+    pieces = [near, over_x, over_z, over_y, near_twin]
+    pieces += [swap_seq(x, 1) for x in (over_x, over_z, over_y)]
+    key_grad, value_grad, both = pl.pallas_call(
         finish_kernel,
-        out_shape=(jax.ShapeDtypeStruct((tok, hd), BF16),) * 2,
-        in_specs=[vmem] * (1 + STOPS),
-        out_specs=(vmem,) * 2,
+        out_shape=(jax.ShapeDtypeStruct((tok, hd), BF16),) * 2
+        + (jax.ShapeDtypeStruct((tok, 2 * hd), BF16),),
+        grid=(1,),
+        in_specs=[whole(tables.shape), whole(kv0.shape), hbm]
+        + [whole(x.shape) for x in homes],
+        out_specs=(whole((tok, hd)), whole((tok, hd)), whole((tok, 2 * hd))),
         compiler_params=params(),
         name="finish_keys",
-    )(tables, kv0, *homes)
-    kv_other = exchange(jnp.concatenate([key_grad, value_grad], axis=1))
+    )(tables, kv0, q_other, *homes)
+    kv_other = exchange(both)
 
     others = head_axis - 1
     slots = 8 if others == 1 else 2
     full = lambda shape: pl.BlockSpec(shape, lambda j, r: (0, 0))
+    mine = lambda shape: pl.BlockSpec(shape, lambda j, r: (r[1], 0))
     which = lambda j, r: r[0] ^ (2 * (j % 4) + j // 4)
     wspec = lambda cols: pl.BlockSpec((eighth, cols), lambda j, r: (which(j, r), 0))
-    hbm = pl.BlockSpec(memory_space=pl.ANY)
     d_input = pl.pallas_call(
         functools.partial(project_kernel, others, slots),
         out_shape=jax.ShapeDtypeStruct((out_rows, d_model), BF16),
@@ -331,9 +370,9 @@
             num_scalar_prefetch=1,
             grid=(8,),
             in_specs=[
-                full((out_rows, col_width)),
-                full((out_rows, hd)),
-                full((out_rows, hd)),
+                mine((out_rows, col_width)),
+                mine((out_rows, hd)),
+                mine((out_rows, hd)),
                 full((out_rows, col_width * others)),
                 full((out_rows, 2 * hd * others)),
                 wspec(col_width),
@@ -350,10 +389,10 @@
         compiler_params=params(),
         name="project",
     )(
-        part.reshape(1),
-        rows_for(query_grad, my_head),
-        rows_for(key_grad, my_head),
-        rows_for(value_grad, my_head),
+        spot,
+        query_grad,
+        key_grad,
+        value_grad,
         q_other,
         kv_other,
         q_weight,

time: 97.5 us -> 91.3 us (0.936)
  local copies, waits for them, and re-layouts: 21.6 us -> 4.82 us
  Pallas kernels: 28.6 us -> 38.5 us
  starting transfers between devices: 13.6 us -> 16.9 us
  other arithmetic: 5.7 us -> 2.43 us
  waiting for transfers between devices: 26 us -> 27.3 us
    unnamed x60 -> x9, local copies, waits for them, and re-layouts: 15.4 us -> 2.11 us
    pallas_call x0 -> x1, Pallas kernels: none -> 3.76 us  [local(): pl.pallas_call(prep_kernel, out_shape=(jax.ShapeDtypeStruct((tok, 2 * hd)...]
    ppermute x4, waiting for transfers between devices: 8.43 us -> 11.9 us  [shift_seq(): lax.ppermute(x, 'seq', [(i, (i + by) % seq_count) for i in range(seq_coun...]
    ppermute x6, starting transfers between devices: 3.77 us -> 6.78 us  [swap_seq(): return lax.ppermute(x, 'seq', [(i, i ^ bit) for i in range(seq_count)])]
    concatenate x3 -> x0, other arithmetic: 2.88 us -> none  [the longest x2 1.92 us: piece_of(): jnp.concatenate([rows_of(q_weight), rows_of(k_weight), rows_of(v_weight)]...]
    pallas_call x1, Pallas kernels: 5.76 us -> 8.25 us  [local(): pl.pallas_call(functools.partial(own_kernel, seq_count), out_shape=(jax.S...]
    dynamic_slice x2 -> x0, local copies, waits for them, and re-layouts: 2.41 us -> none  [rows_of(): return lax.dynamic_slice_in_dim(w, which * eighth, eighth, 0)]
    ppermute x4, waiting for transfers between devices: 17.6 us -> 15.4 us  [from_head(): lax.ppermute(x, 'head', [(i, (i - by) % head_axis) for i in range(head_ax...]
  transfers between devices with their start and end apart: 14 -> 14, of which waited for: 5 -> 5; matrix products, arithmetic and copies ran while one was open for 11% -> 6% of each run, Pallas kernels for 18% -> 24%
where the time goes in v3:
time: 91.3 us; the launch traced here: 90.8 us
  Pallas kernels  38.5 us (42%)
  waiting for transfers between devices  27.3 us (30%)
  starting transfers between devices  16.9 us (19%)
  local copies, waits for them, and re-layouts  4.82 us (5%)
  other arithmetic  2.43 us (3%)
    ppermute x4, waiting for transfers between devices, from_head(): lax.ppermute(x, 'head', [(i, (i - by) % head_axis) for i in range(head_ax...  15.4 us
    pallas_call x1, Pallas kernels, local(): pl.pallas_call(functools.partial(project_kernel, others, slots), out_shap...  12.8 us
    ppermute x4, waiting for transfers between devices, shift_seq(): lax.ppermute(x, 'seq', [(i, (i + by) % seq_count) for i in range(seq_coun...  11.9 us
    pallas_call x1, Pallas kernels, local(): pl.pallas_call(functools.partial(far_kernel, seq_count), out_shape=(jax.S...  10.9 us
    pallas_call x1, Pallas kernels, local(): pl.pallas_call(functools.partial(own_kernel, seq_count), out_shape=(jax.S...  8.25 us
    ppermute x6, starting transfers between devices, swap_seq(): return lax.ppermute(x, 'seq', [(i, i ^ bit) for i in range(seq_count)])  6.78 us
    ppermute x4, starting transfers between devices, from_head(): lax.ppermute(x, 'head', [(i, (i - by) % head_axis) for i in range(head_ax...  6.02 us
    ppermute x4, starting transfers between devices, shift_seq(): lax.ppermute(x, 'seq', [(i, (i + by) % seq_count) for i in range(seq_coun...  4.1 us
  transfers between devices with their start and end apart: 14, of which 5 were waited for; matrix products, arithmetic and copies ran while one was open for 6% of the time, Pallas kernels for 24%

profile of v3, /device:TPU:0, one launch (start us, length us, event | category | flops | bytes accessed | tf_op | source)
XLA Modules:
  0.0 90.8 jit_solution(2679946159713104941)
XLA Ops:
  1.2 3.8 %prep.1 = (bf16[768,256]{1,0:T(8,128)(2,1)}, bf16[512,768]{1,0:T(8,128)(2,1)}, bf16[512,768]{1,0:T(8,128)(2,1)}) custom-call(s32[2]{0:T(128)} %pad_add_fusion.r_ref, bf16[768,128]{1,0:T(8,128)(2,1)} %k.1, bf16[768,128]{1,0:T(8,128)(2,1)} %v.1, bf16[4096,512]{1,0:T(8,128)(2,1)} %wq.1, bf16[4096,128]{1,0:T(8,128)(2,1)} %wk.1, bf16[4096,128]{1,0:T(8,128)(2,1)} %wv.1, ...), custom_call_target="tpu_custom_call" | custom-call | tf_op jit(solution)/shard_map/prep/pallas_call | solution.py:252
  5.0 3.0 %collective-permute-start.6 = (bf16[512,768]{1,0:T(8,128)(2,1)}, bf16[512,768]{1,0:T(8,128)(2,1)}, u32[]{:S(2)}, u32[]{:S(2)}) collective-permute-start(bf16[512,768]{1,0:T(8,128)(2,1)} %get-tuple-element.32), channel_id=1, source_target_pairs={{0,1},{1,0},{2,3},{3,2},{4,5},{5,4},{6,7},{7,6},{8,9},{9,8},{10,11... | collective-permute-start | bytes 2359304 | tf_op jit(solution)/shard_map/ppermute | solution.py:246
  8.0 1.5 %collective-permute-start.1 = (bf16[768,256]{1,0:T(8,128)(2,1)}, bf16[768,256]{1,0:T(8,128)(2,1)}, u32[]{:S(2)}, u32[]{:S(2)}) collective-permute-start(bf16[768,256]{1,0:T(8,128)(2,1)} %get-tuple-element.24), channel_id=1, source_target_pairs={{0,4},{2,6},{4,8},{6,10},{8,12},{10,14},{12,16},{14,18},{16,20},{1... | collective-permute-start | bytes 1179656 | tf_op jit(solution)/shard_map/ppermute | solution.py:240
  10.3 8.3 %own_stop.1 = (f32[2,512,384]{2,1,0:T(8,128)}, f32[2,384,256]{2,1,0:T(8,128)}, f32[2,4,384]{2,1,0:T(4,128)}, f32[2,4,384]{2,1,0:T(4,128)}) custom-call(s32[16,2]{1,0:T(8,128)} %copy.19.ids_ref, bf16[768,512]{1,0:T(8,128)(2,1)} %q_ref.3, bf16[768,128]{1,0:T(8,128)(2,1)} %k.1, bf16[768,128]{1,0:T(8,128)(2,1)} %v.1, bf16[768,512]{1,0:T(8,128)(2,1)} %o_ref.1, ...), custom_call_target="tpu_custom_call" | custom-call | flops 2264924160 | bytes 5242880 | tf_op jit(solution)/shard_map/own_stop/pallas_call | solution.py:282
  18.7 0.8 multiply_cosine_fusion
  19.4 6.4 %collective-permute-done.6.refs_0_ = bf16[512,768]{1,0:T(8,128)(2,1)} collective-permute-done((bf16[512,768]{1,0:T(8,128)(2,1)}, bf16[512,768]{1,0:T(8,128)(2,1)}, u32[]{:S(2)}, u32[]{:S(2)}) %collective-permute-start.6) | collective-permute-done | bytes 786464 | tf_op jit(solution)/shard_map/ppermute | solution.py:246
  25.8 1.8 %collective-permute-start.8 = (bf16[512,768]{1,0:T(8,128)(2,1)}, bf16[512,768]{1,0:T(8,128)(2,1)}, u32[]{:S(2)}, u32[]{:S(2)}) collective-permute-start(bf16[512,768]{1,0:T(8,128)(2,1)} %get-tuple-element.34.rest_0_), channel_id=1, source_target_pairs={{0,8},{2,10},{4,12},{6,14},{8,0},{10,2},{12,4},{14,6},{16,24},{18,... | collective-permute-start | bytes 2359304 | tf_op jit(solution)/shard_map/ppermute | solution.py:243
  27.6 1.5 %collective-permute-start.7 = (bf16[512,768]{1,0:T(8,128)(2,1)}, bf16[512,768]{1,0:T(8,128)(2,1)}, u32[]{:S(2)}, u32[]{:S(2)}) collective-permute-start(bf16[512,768]{1,0:T(8,128)(2,1)} %get-tuple-element.34.rest_0_), channel_id=1, source_target_pairs={{0,4},{2,6},{4,0},{6,2},{8,12},{10,14},{12,8},{14,10},{16,20},{18,... | collective-permute-start | bytes 2359304 | tf_op jit(solution)/shard_map/ppermute | solution.py:243
  29.1 1.5 %collective-permute-start.9 = (bf16[512,768]{1,0:T(8,128)(2,1)}, bf16[512,768]{1,0:T(8,128)(2,1)}, u32[]{:S(2)}, u32[]{:S(2)}) collective-permute-start(bf16[512,768]{1,0:T(8,128)(2,1)} %get-tuple-element.35), channel_id=1, source_target_pairs={{0,1},{1,0},{2,3},{3,2},{4,5},{5,4},{6,7},{7,6},{8,9},{9,8},{10,11... | collective-permute-start | bytes 2359304 | tf_op jit(solution)/shard_map/ppermute | solution.py:246
  30.6 0.8 pad_maximum_fusion.tab_ref
  31.4 10.9 %far_stops.1 = (bf16[768,512]{1,0:T(8,128)(2,1)}, bf16[768,256]{1,0:T(8,128)(2,1)}, bf16[768,256]{1,0:T(8,128)(2,1)}) custom-call(s32[16,2]{1,0:T(8,128)} %copy.19.ids_ref, bf16[768,512]{1,0:T(8,128)(2,1)} %q_ref.3, bf16[768,512]{1,0:T(8,128)(2,1)} %do_ref.3, f32[2,4,384]{2,1,0:T(4,128)} %get-tuple-element.21.norm_ref.refs_2_, ...), custom_call_target="tpu_custom_call" | custom-call | flops 3019898880 | bytes 6291456 | tf_op jit(solution)/shard_map/far_stops/pallas_call | solution.py:312
  42.5 1.8 %constant_dynamic-slice_fusion.1 = bf16[384,512]{1,0:T(8,128)(2,1)} fusion(bf16[768,512]{1,0:T(8,128)(2,1)} %get-tuple-element.25.qg, s32[]{:T(128)S(6)} %select_n.9), kind=kLoop, calls=%fused_computation.6 | loop fusion | bytes 786436 | tf_op jit(solution)/shard_map/dynamic_slice | solution.py:334
  44.8 3.3 %collective-permute-done.3.rest_0_.refs_3_ = bf16[768,256]{1,0:T(8,128)(2,1)S(1)} collective-permute-done((bf16[768,256]{1,0:T(8,128)(2,1)}, bf16[768,256]{1,0:T(8,128)(2,1)S(1)}, u32[]{:S(2)}, u32[]{:S(2)}) %collective-permute-start.3) | collective-permute-done | bytes 393248 | tf_op jit(solution)/shard_map/ppermute | solution.py:240
  48.1 2.3 %collective-permute-start.10 = (bf16[512,768]{1,0:T(8,128)(2,1)}, bf16[512,768]{1,0:T(8,128)(2,1)}, u32[]{:S(2)}, u32[]{:S(2)}) collective-permute-start(bf16[512,768]{1,0:T(8,128)(2,1)} %get-tuple-element.34.rest_0_), channel_id=1, source_target_pairs={{0,2},{2,0},{4,6},{6,4},{8,10},{10,8},{12,14},{14,12},{16,18},{18,... | collective-permute-start | bytes 2359304 | tf_op jit(solution)/shard_map/ppermute | solution.py:243
  50.4 0.7 collective-permute-start.11
  51.6 4.3 %collective-permute-done.2.after_ref.qo = bf16[384,512]{1,0:T(8,128)(2,1)} collective-permute-done((bf16[384,512]{1,0:T(8,128)(2,1)}, bf16[384,512]{1,0:T(8,128)(2,1)}, u32[]{:S(2)}, u32[]{:S(2)}) %collective-permute-start.2) | collective-permute-done | bytes 393248 | tf_op jit(solution)/shard_map/ppermute | solution.py:246
  56.0 2.4 %collective-permute-start.4 = (bf16[768,256]{1,0:T(8,128)(2,1)}, bf16[768,256]{1,0:T(8,128)(2,1)S(1)}, u32[]{:S(2)}, u32[]{:S(2)}) collective-permute-start(bf16[768,256]{1,0:T(8,128)(2,1)} %get-tuple-element.28), channel_id=1, source_target_pairs={{0,28},{2,30},{4,0},{6,2},{8,4},{10,6},{12,8},{14,10},{16,12},{18,... | collective-permute-start | bytes 1179656 | tf_op jit(solution)/shard_map/ppermute | solution.py:240
  58.4 8.6 %collective-permute-done.4.rest_1_ = bf16[768,256]{1,0:T(8,128)(2,1)S(1)} collective-permute-done((bf16[768,256]{1,0:T(8,128)(2,1)}, bf16[768,256]{1,0:T(8,128)(2,1)S(1)}, u32[]{:S(2)}, u32[]{:S(2)}) %collective-permute-start.4) | collective-permute-done | bytes 393248 | tf_op jit(solution)/shard_map/ppermute | solution.py:240
  67.0 0.7 copy-done.1
  67.7 2.7 %finish_keys.1 = (bf16[768,128]{1,0:T(8,128)(2,1)}, bf16[768,128]{1,0:T(8,128)(2,1)}, bf16[768,256]{1,0:T(8,128)(2,1)}) custom-call(f32[2,64,768]{2,1,0:T(8,128)} %pad_maximum_fusion.tab_ref, f32[2,384,256]{2,1,0:T(8,128)} %get-tuple-element.26.kv0_ref, bf16[384,512]{1,0:T(8,128)(2,1)} %collective-permute-done.2.after_ref.qo, bf16[768,256]{1,0:T(8,128)(2,1)} %copy-done, ...), custom_call_target="tpu_custom_call" | custom-call | tf_op jit(solution)/shard_map/finish_keys/pallas_call | solution.py:347
  70.4 0.9 %constant_dynamic-slice_fusion = bf16[384,256]{1,0:T(8,128)(2,1)S(1)} fusion(bf16[768,256]{1,0:T(8,128)(2,1)} %get-tuple-element.31, s32[]{:T(128)S(6)} %select_n.9), kind=kLoop, calls=%fused_computation.5 | loop fusion | bytes 393220 | tf_op jit(solution)/shard_map/dynamic_slice | solution.py:334
  71.4 1.0 %collective-permute-start.5 = (bf16[384,256]{1,0:T(8,128)(2,1)S(1)}, bf16[384,256]{1,0:T(8,128)(2,1)S(1)}, u32[]{:S(2)}, u32[]{:S(2)}) collective-permute-start(bf16[384,256]{1,0:T(8,128)(2,1)S(1)} %constant_dynamic-slice_fusion), channel_id=1, source_target_pairs={{0,1},{1,0},{2,3},{3,2},{4,5},{5,4},{6,7},{7,6},{8,9},{9,8},{10,11... | collective-permute-start | bytes 589832 | tf_op jit(solution)/shard_map/ppermute | solution.py:246
  72.4 4.7 %collective-permute-done.5.kvo = bf16[384,256]{1,0:T(8,128)(2,1)S(1)} collective-permute-done((bf16[384,256]{1,0:T(8,128)(2,1)S(1)}, bf16[384,256]{1,0:T(8,128)(2,1)S(1)}, u32[]{:S(2)}, u32[]{:S(2)}) %collective-permute-start.5) | collective-permute-done | bytes 196640 | tf_op jit(solution)/shard_map/ppermute | solution.py:246
  77.8 12.8 %project.1 = bf16[384,4096]{1,0:T(8,128)(2,1)} custom-call(s32[2]{0:T(128)} %pad_add_fusion.r_ref, bf16[768,512]{1,0:T(8,128)(2,1)} %get-tuple-element.25.qg, bf16[768,128]{1,0:T(8,128)(2,1)} %get-tuple-element.19.kg, bf16[768,128]{1,0:T(8,128)(2,1)} %get-tuple-element.20.vg, bf16[384,512]{1,0:T(8,128)(2,1)} %collective-permute-done.2.after_ref.qo, ...), custom_call_target="tpu_custom_call" | custom-call | tf_op jit(solution)/shard_map/project/pallas_call | solution.py:366
  (29 shorter events, 3.5 us)
Async XLA Ops:
  1.2 8.2 %copy-start.3 = (s32[16,2]{0,1:T(2,128)S(1)}, s32[16,2]{0,1:T(2,128)}, u32[]{:S(2)}) copy-start(s32[16,2]{0,1:T(2,128)} %param.16) | copy-start | bytes 388
  5.0 20.8 %collective-permute-start.6 = (bf16[512,768]{1,0:T(8,128)(2,1)}, bf16[512,768]{1,0:T(8,128)(2,1)}, u32[]{:S(2)}, u32[]{:S(2)}) collective-permute-start(bf16[512,768]{1,0:T(8,128)(2,1)} %get-tuple-element.32), channel_id=1, source_target_pairs={{0,1},{1,0},{2,3},{3,2},{4,5},{5,4},{6,7},{7,6},{8,9},{9,8},{10,11... | collective-permute-start | bytes 2359304 | tf_op jit(solution)/shard_map/ppermute | solution.py:246
  8.0 23.5 %collective-permute-start.1 = (bf16[768,256]{1,0:T(8,128)(2,1)}, bf16[768,256]{1,0:T(8,128)(2,1)}, u32[]{:S(2)}, u32[]{:S(2)}) collective-permute-start(bf16[768,256]{1,0:T(8,128)(2,1)} %get-tuple-element.24), channel_id=1, source_target_pairs={{0,4},{2,6},{4,8},{6,10},{8,12},{10,14},{12,16},{14,18},{16,20},{1... | collective-permute-start | bytes 1179656 | tf_op jit(solution)/shard_map/ppermute | solution.py:240
  9.5 22.0 %collective-permute-start = (bf16[768,256]{1,0:T(8,128)(2,1)}, bf16[768,256]{1,0:T(8,128)(2,1)}, u32[]{:S(2)}, u32[]{:S(2)}) collective-permute-start(bf16[768,256]{1,0:T(8,128)(2,1)} %get-tuple-element.24), channel_id=1, source_target_pairs={{0,2},{2,4},{4,6},{6,8},{8,10},{10,12},{12,14},{14,16},{16,18},{18... | collective-permute-start | bytes 1179656 | tf_op jit(solution)/shard_map/ppermute | solution.py:240
  25.8 24.6 %collective-permute-start.8 = (bf16[512,768]{1,0:T(8,128)(2,1)}, bf16[512,768]{1,0:T(8,128)(2,1)}, u32[]{:S(2)}, u32[]{:S(2)}) collective-permute-start(bf16[512,768]{1,0:T(8,128)(2,1)} %get-tuple-element.34.rest_0_), channel_id=1, source_target_pairs={{0,8},{2,10},{4,12},{6,14},{8,0},{10,2},{12,4},{14,6},{16,24},{18,... | collective-permute-start | bytes 2359304 | tf_op jit(solution)/shard_map/ppermute | solution.py:243
  27.6 22.8 %collective-permute-start.7 = (bf16[512,768]{1,0:T(8,128)(2,1)}, bf16[512,768]{1,0:T(8,128)(2,1)}, u32[]{:S(2)}, u32[]{:S(2)}) collective-permute-start(bf16[512,768]{1,0:T(8,128)(2,1)} %get-tuple-element.34.rest_0_), channel_id=1, source_target_pairs={{0,4},{2,6},{4,0},{6,2},{8,12},{10,14},{12,8},{14,10},{16,20},{18,... | collective-permute-start | bytes 2359304 | tf_op jit(solution)/shard_map/ppermute | solution.py:243
  29.1 21.3 %collective-permute-start.9 = (bf16[512,768]{1,0:T(8,128)(2,1)}, bf16[512,768]{1,0:T(8,128)(2,1)}, u32[]{:S(2)}, u32[]{:S(2)}) collective-permute-start(bf16[512,768]{1,0:T(8,128)(2,1)} %get-tuple-element.35), channel_id=1, source_target_pairs={{0,1},{1,0},{2,3},{3,2},{4,5},{5,4},{6,7},{7,6},{8,9},{9,8},{10,11... | collective-permute-start | bytes 2359304 | tf_op jit(solution)/shard_map/ppermute | solution.py:246
  42.3 5.8 %collective-permute-start.3 = (bf16[768,256]{1,0:T(8,128)(2,1)}, bf16[768,256]{1,0:T(8,128)(2,1)S(1)}, u32[]{:S(2)}, u32[]{:S(2)}) collective-permute-start(bf16[768,256]{1,0:T(8,128)(2,1)} %get-tuple-element.27), channel_id=1, source_target_pairs={{0,30},{2,0},{4,2},{6,4},{8,6},{10,8},{12,10},{14,12},{16,14},{18,... | collective-permute-start | bytes 1179656 | tf_op jit(solution)/shard_map/ppermute | solution.py:240
  44.3 11.7 %collective-permute-start.2 = (bf16[384,512]{1,0:T(8,128)(2,1)}, bf16[384,512]{1,0:T(8,128)(2,1)}, u32[]{:S(2)}, u32[]{:S(2)}) collective-permute-start(bf16[384,512]{1,0:T(8,128)(2,1)} %constant_dynamic-slice_fusion.1), channel_id=1, source_target_pairs={{0,1},{1,0},{2,3},{3,2},{4,5},{5,4},{6,7},{7,6},{8,9},{9,8},{10,11... | collective-permute-start | bytes 1179656 | tf_op jit(solution)/shard_map/ppermute | solution.py:246
  48.1 2.3 %copy-start = (bf16[768,256]{1,0:T(8,128)(2,1)}, bf16[768,256]{1,0:T(8,128)(2,1)S(1)}, u32[]{:S(2)}) copy-start(bf16[768,256]{1,0:T(8,128)(2,1)S(1)} %collective-permute-done.3.rest_0_.refs_3_) | copy-start | bytes 1179652
  48.1 29.0 %collective-permute-start.10 = (bf16[512,768]{1,0:T(8,128)(2,1)}, bf16[512,768]{1,0:T(8,128)(2,1)}, u32[]{:S(2)}, u32[]{:S(2)}) collective-permute-start(bf16[512,768]{1,0:T(8,128)(2,1)} %get-tuple-element.34.rest_0_), channel_id=1, source_target_pairs={{0,2},{2,0},{4,6},{6,4},{8,10},{10,8},{12,14},{14,12},{16,18},{18,... | collective-permute-start | bytes 2359304 | tf_op jit(solution)/shard_map/ppermute | solution.py:243
  50.4 26.7 %collective-permute-start.11 = (bf16[512,768]{1,0:T(8,128)(2,1)}, bf16[512,768]{1,0:T(8,128)(2,1)}, u32[]{:S(2)}, u32[]{:S(2)}) collective-permute-start(bf16[512,768]{1,0:T(8,128)(2,1)} %get-tuple-element.36.rest_1_), channel_id=1, source_target_pairs={{0,2},{2,0},{4,6},{6,4},{8,10},{10,8},{12,14},{14,12},{16,18},{18,... | collective-permute-start | bytes 2359304 | tf_op jit(solution)/shard_map/ppermute | solution.py:243
  51.1 26.0 %collective-permute-start.12 = (bf16[512,768]{1,0:T(8,128)(2,1)}, bf16[512,768]{1,0:T(8,128)(2,1)}, u32[]{:S(2)}, u32[]{:S(2)}) collective-permute-start(bf16[512,768]{1,0:T(8,128)(2,1)} %get-tuple-element.37.rest_2_), channel_id=1, source_target_pairs={{0,2},{2,0},{4,6},{6,4},{8,10},{10,8},{12,14},{14,12},{16,18},{18,... | collective-permute-start | bytes 2359304 | tf_op jit(solution)/shard_map/ppermute | solution.py:243
  51.1 26.0 %collective-permute-start.13 = (bf16[512,768]{1,0:T(8,128)(2,1)}, bf16[512,768]{1,0:T(8,128)(2,1)}, u32[]{:S(2)}, u32[]{:S(2)}) collective-permute-start(bf16[512,768]{1,0:T(8,128)(2,1)} %get-tuple-element.38.rest_3_), channel_id=1, source_target_pairs={{0,2},{2,0},{4,6},{6,4},{8,10},{10,8},{12,14},{14,12},{16,18},{18,... | collective-permute-start | bytes 2359304 | tf_op jit(solution)/shard_map/ppermute | solution.py:243
  56.0 11.0 %collective-permute-start.4 = (bf16[768,256]{1,0:T(8,128)(2,1)}, bf16[768,256]{1,0:T(8,128)(2,1)S(1)}, u32[]{:S(2)}, u32[]{:S(2)}) collective-permute-start(bf16[768,256]{1,0:T(8,128)(2,1)} %get-tuple-element.28), channel_id=1, source_target_pairs={{0,28},{2,30},{4,0},{6,2},{8,4},{10,6},{12,8},{14,10},{16,12},{18,... | collective-permute-start | bytes 1179656 | tf_op jit(solution)/shard_map/ppermute | solution.py:240
  67.0 0.7 copy-start.1
  71.4 5.7 %collective-permute-start.5 = (bf16[384,256]{1,0:T(8,128)(2,1)S(1)}, bf16[384,256]{1,0:T(8,128)(2,1)S(1)}, u32[]{:S(2)}, u32[]{:S(2)}) collective-permute-start(bf16[384,256]{1,0:T(8,128)(2,1)S(1)} %constant_dynamic-slice_fusion), channel_id=1, source_target_pairs={{0,1},{1,0},{2,3},{3,2},{4,5},{5,4},{6,7},{7,6},{8,9},{9,8},{10,11... | collective-permute-start | bytes 589832 | tf_op jit(solution)/shard_map/ppermute | solution.py:246
  77.1 0.7 copy-start.2

commit v4 on v3

--- a/solution.py
+++ b/solution.py
@@ -130,7 +130,7 @@
             qg_ref[a * half : (a + 1) * half, h * hd : (h + 1) * hd] = turned.T.astype(BF16)
 
 
-def finish_kernel(tab_ref, kv0_ref, after_ref, *rest):
+def finish_kernel(tab_ref, kv0_ref, *rest):
     home_refs, (kg_ref, vg_ref, both_ref) = rest[:-3], rest[-3:]
     half = kv0_ref.shape[1]
     hd = kg_ref.shape[1]
@@ -155,33 +155,51 @@
         both_ref[rows, hd:] = value_grad
 
 
-def project_kernel(others, slots, r_ref, qg, kg, vg, qo, kvo, wq, wk, wv, *rest):
+def own_project_kernel(r_ref, qg, wq, out_ref):
+    out_ref[...] = dot(qg[...], wq[...], NT)
+
+
+def project_kernel(others, slots, r_ref, partial, kg, vg, qo, kvo, wk, wv, *rest):
     j = pl.program_id(0)
     pieces, (out_ref, buf, sem) = rest[:8], rest[8:]
-    qw, kw = qg.shape[1], kg.shape[1]
-
-    def copy(i):
-        return pltpu.make_async_copy(pieces[i], buf.at[i % slots], sem.at[i])
-
-    for i in range(8):
+    kw = kg.shape[1]
+    qw = qo.shape[1] // others
+    eighth = pieces[0].shape[0]
+    odd = lax.rem(r_ref[0], 2)
+
+    def copies(i):
+        for twin in range(2):
+            place = pl.multiple_of((odd ^ twin) * eighth, eighth)
+            yield pltpu.make_async_copy(
+                pieces[2 * i + twin],
+                buf.at[i % slots, pl.ds(place, eighth), :],
+                sem.at[2 * i + twin],
+            )
+
+    for i in range(4):
         @pl.when(j == max(0, i - slots + 1))
         def _(i=i):
-            copy(i).start()
-
-    own = jnp.concatenate([wq[...], wk[...], wv[...]], axis=1)
-    total = dot(jnp.concatenate([qg[...], kg[...], vg[...]], axis=1), own, NT)
-    for i in range(8):
+            for copy in copies(i):
+                copy.start()
+
+    total = partial[...] + dot(kg[...], wk[...], NT) + dot(vg[...], wv[...], NT)
+    for i in range(4):
         @pl.when(j == i)
         def _(i=i):
-            copy(i).wait()
+            for copy in copies(i):
+                copy.wait()
 
     slot = lax.rem(j, slots)
     width = qw + 2 * kw
     for s in range(others):
-        grads = jnp.concatenate(
-            [qo[:, s * qw : (s + 1) * qw], kvo[:, s * 2 * kw : (s + 1) * 2 * kw]], axis=1
+        total = total + dot(
+            qo[:, s * qw : (s + 1) * qw], buf[slot, :, s * width : s * width + qw], NT
         )
-        total = total + dot(grads, buf[slot, :, s * width : (s + 1) * width], NT)
+        total = total + dot(
+            kvo[:, s * 2 * kw : (s + 1) * 2 * kw],
+            buf[slot, :, s * width + qw : (s + 1) * width],
+            NT,
+        )
     out_ref[...] = total.astype(BF16)
 
 
@@ -204,17 +222,17 @@
     pass
 
 
-def tie(arrays, after):
+def tie(arrays, *after):
     hbm = pl.BlockSpec(memory_space=pltpu.HBM)
     return pl.pallas_call(
         tie_kernel,
         out_shape=tuple(jax.ShapeDtypeStruct(x.shape, x.dtype) for x in arrays),
-        in_specs=[hbm] * (len(arrays) + 1),
+        in_specs=[hbm] * (len(arrays) + len(after)),
         out_specs=(hbm,) * len(arrays),
         input_output_aliases={i: i for i in range(len(arrays))},
         compiler_params=params(),
         name="tie",
-    )(*arrays, after)
+    )(*arrays, *after)
 
 
 def params(**kw):
@@ -340,49 +358,66 @@
         return got[0] if len(got) == 1 else jnp.concatenate(got, axis=1)
 
     q_other = exchange(query_grad)
+    quarter = 2 * eighth
+    wquarter = lambda cols: pl.BlockSpec((quarter, cols), lambda j, r: ((r[0] // 2) ^ j, 0))
+    column = pl.BlockSpec((out_rows, quarter), lambda j, r: (0, (r[0] // 2) ^ j))
+    mine = lambda shape: pl.BlockSpec(shape, lambda j, r: (r[1], 0))
+    partial = pl.pallas_call(
+        own_project_kernel,
+        out_shape=jax.ShapeDtypeStruct((out_rows, d_model), F32),
+        grid_spec=pltpu.PrefetchScalarGridSpec(
+            num_scalar_prefetch=1,
+            grid=(4,),
+            in_specs=[mine((out_rows, col_width)), wquarter(col_width)],
+            out_specs=column,
+        ),
+        compiler_params=params(),
+        cost_estimate=pl.CostEstimate(
+            flops=2 * out_rows * d_model * col_width, bytes_accessed=11 * 2**20, transcendentals=0
+        ),
+        name="own_project",
+    )(spot, query_grad, q_weight)
     homes = [shift_seq(x, -(i + 1)) for i, x in enumerate(homes)]
-    over_x, over_z, over_y = tie((over_x, over_z, over_y), homes[0])
-    pieces = [near, over_x, over_z, over_y, near_twin]
-    pieces += [swap_seq(x, 1) for x in (over_x, over_z, over_y)]
+    over_x, over_z, over_y = tie((over_x, over_z, over_y), partial, q_other, *homes)
+    pieces = [near, near_twin]
+    for x in (over_x, over_z, over_y):
+        pieces += [x, swap_seq(x, 1)]
     key_grad, value_grad, both = pl.pallas_call(
         finish_kernel,
         out_shape=(jax.ShapeDtypeStruct((tok, hd), BF16),) * 2
         + (jax.ShapeDtypeStruct((tok, 2 * hd), BF16),),
         grid=(1,),
-        in_specs=[whole(tables.shape), whole(kv0.shape), hbm]
+        in_specs=[whole(tables.shape), whole(kv0.shape)]
         + [whole(x.shape) for x in homes],
         out_specs=(whole((tok, hd)), whole((tok, hd)), whole((tok, 2 * hd))),
         compiler_params=params(),
         name="finish_keys",
-    )(tables, kv0, q_other, *homes)
+    )(tables, kv0, *homes)
     kv_other = exchange(both)
 
     others = head_axis - 1
-    slots = 8 if others == 1 else 2
+    slots = 4 if others == 1 else 2
     full = lambda shape: pl.BlockSpec(shape, lambda j, r: (0, 0))
     mine = lambda shape: pl.BlockSpec(shape, lambda j, r: (r[1], 0))
-    which = lambda j, r: r[0] ^ (2 * (j % 4) + j // 4)
-    wspec = lambda cols: pl.BlockSpec((eighth, cols), lambda j, r: (which(j, r), 0))
     d_input = pl.pallas_call(
         functools.partial(project_kernel, others, slots),
         out_shape=jax.ShapeDtypeStruct((out_rows, d_model), BF16),
         grid_spec=pltpu.PrefetchScalarGridSpec(
             num_scalar_prefetch=1,
-            grid=(8,),
+            grid=(4,),
             in_specs=[
-                mine((out_rows, col_width)),
+                column,
                 mine((out_rows, hd)),
                 mine((out_rows, hd)),
                 full((out_rows, col_width * others)),
                 full((out_rows, 2 * hd * others)),
-                wspec(col_width),
-                wspec(hd),
-                wspec(hd),
+                wquarter(hd),
+                wquarter(hd),
             ]
             + [hbm] * 8,
-            out_specs=pl.BlockSpec((out_rows, eighth), lambda j, r: (0, which(j, r))),
+            out_specs=column,
             scratch_shapes=[
-                pltpu.VMEM((slots, eighth, (col_width + 2 * hd) * others), BF16),
+                pltpu.VMEM((slots, quarter, (col_width + 2 * hd) * others), BF16),
                 pltpu.SemaphoreType.DMA((8,)),
             ],
         ),
@@ -390,12 +425,11 @@
         name="project",
     )(
         spot,
-        query_grad,
+        partial,
         key_grad,
         value_grad,
         q_other,
         kv_other,
-        q_weight,
         k_weight,
         v_weight,
         *pieces,

time: 91.3 us -> 93.8 us (1.027)
  Pallas kernels: 38.5 us -> 43.3 us
  starting transfers between devices: 16.9 us -> 13.1 us
  waiting for transfers between devices: 27.3 us -> 29.5 us
    pallas_call x0 -> x1, Pallas kernels: none -> 7.18 us  [local(): pl.pallas_call(own_project_kernel, out_shape=jax.ShapeDtypeStruct((out_ro...]
    ppermute x6, starting transfers between devices: 6.78 us -> 2.85 us  [swap_seq(): return lax.ppermute(x, 'seq', [(i, i ^ bit) for i in range(seq_count)])]
    pallas_call x1, Pallas kernels: 12.8 us -> 10.5 us  [local(): pl.pallas_call(functools.partial(project_kernel, others, slots), out_shap...]
    ppermute x4, waiting for transfers between devices: 11.9 us -> 14.1 us  [shift_seq(): lax.ppermute(x, 'seq', [(i, (i + by) % seq_count) for i in range(seq_coun...]
    ppermute x4, starting transfers between devices: 4.1 us -> 6.13 us  [shift_seq(): lax.ppermute(x, 'seq', [(i, (i + by) % seq_count) for i in range(seq_coun...]
    ppermute x4, starting transfers between devices: 6.02 us -> 4.1 us  [from_head(): lax.ppermute(x, 'head', [(i, (i - by) % head_axis) for i in range(head_ax...]
  transfers between devices with their start and end apart: 14 -> 14, of which waited for: 5 -> 6; matrix products, arithmetic and copies ran while one was open for 6% -> 6% of each run, Pallas kernels for 24% -> 31%
where the time goes in v4:
time: 93.8 us; the launch traced here: 93.3 us
  Pallas kernels  43.3 us (46%)
  waiting for transfers between devices  29.5 us (31%)
  starting transfers between devices  13.1 us (14%)
  local copies, waits for them, and re-layouts  4.06 us (4%)
  other arithmetic  2.47 us (3%)
    ppermute x4, waiting for transfers between devices, from_head(): lax.ppermute(x, 'head', [(i, (i - by) % head_axis) for i in range(head_ax...  15.4 us
    ppermute x4, waiting for transfers between devices, shift_seq(): lax.ppermute(x, 'seq', [(i, (i + by) % seq_count) for i in range(seq_coun...  14.1 us
    pallas_call x1, Pallas kernels, local(): pl.pallas_call(functools.partial(far_kernel, seq_count), out_shape=(jax.S...  10.8 us
    pallas_call x1, Pallas kernels, local(): pl.pallas_call(functools.partial(project_kernel, others, slots), out_shap...  10.5 us
    pallas_call x1, Pallas kernels, local(): pl.pallas_call(functools.partial(own_kernel, seq_count), out_shape=(jax.S...  8.25 us
    pallas_call x1, Pallas kernels, local(): pl.pallas_call(own_project_kernel, out_shape=jax.ShapeDtypeStruct((out_ro...  7.18 us
    ppermute x4, starting transfers between devices, shift_seq(): lax.ppermute(x, 'seq', [(i, (i + by) % seq_count) for i in range(seq_coun...  6.13 us
    ppermute x4, starting transfers between devices, from_head(): lax.ppermute(x, 'head', [(i, (i - by) % head_axis) for i in range(head_ax...  4.1 us
  transfers between devices with their start and end apart: 14, of which 6 were waited for; matrix products, arithmetic and copies ran while one was open for 6% of the time, Pallas kernels for 31%

profile of v4, /device:TPU:0, one launch (start us, length us, event | category | flops | bytes accessed | tf_op | source)
XLA Modules:
  0.0 93.3 jit_solution(14117510367122393511)
XLA Ops:
  0.6 0.7 pad_add_fusion.r_ref
  1.3 3.8 %prep.1 = (bf16[768,256]{1,0:T(8,128)(2,1)}, bf16[512,768]{1,0:T(8,128)(2,1)}, bf16[512,768]{1,0:T(8,128)(2,1)}) custom-call(s32[2]{0:T(128)} %pad_add_fusion.r_ref, bf16[768,128]{1,0:T(8,128)(2,1)} %k.1, bf16[768,128]{1,0:T(8,128)(2,1)} %v.1, bf16[4096,512]{1,0:T(8,128)(2,1)} %wq.1, bf16[4096,128]{1,0:T(8,128)(2,1)} %wk.1, bf16[4096,128]{1,0:T(8,128)(2,1)} %wv.1, ...), custom_call_target="tpu_custom_call" | custom-call | tf_op jit(solution)/shard_map/prep/pallas_call | solution.py:270
  5.1 2.9 %collective-permute-start.1 = (bf16[768,256]{1,0:T(8,128)(2,1)}, bf16[768,256]{1,0:T(8,128)(2,1)S(1)}, u32[]{:S(2)}, u32[]{:S(2)}) collective-permute-start(bf16[768,256]{1,0:T(8,128)(2,1)} %get-tuple-element.24), channel_id=1, source_target_pairs={{0,4},{2,6},{4,8},{6,10},{8,12},{10,14},{12,16},{14,18},{16,20},{1... | collective-permute-start | bytes 1179656 | tf_op jit(solution)/shard_map/ppermute | solution.py:258
  8.0 1.5 %collective-permute-start.6 = (bf16[512,768]{1,0:T(8,128)(2,1)}, bf16[512,768]{1,0:T(8,128)(2,1)}, u32[]{:S(2)}, u32[]{:S(2)}) collective-permute-start(bf16[512,768]{1,0:T(8,128)(2,1)} %get-tuple-element.32), channel_id=1, source_target_pairs={{0,1},{1,0},{2,3},{3,2},{4,5},{5,4},{6,7},{7,6},{8,9},{9,8},{10,11... | collective-permute-start | bytes 2359304 | tf_op jit(solution)/shard_map/ppermute | solution.py:264
  9.9 0.8 multiply_cosine_fusion
  10.6 0.7 copy.19.ids_ref
  11.3 0.8 pad_maximum_fusion.tab_ref
  12.1 8.2 %own_stop.1 = (f32[2,512,384]{2,1,0:T(8,128)}, f32[2,384,256]{2,1,0:T(8,128)}, f32[2,4,384]{2,1,0:T(4,128)}, f32[2,4,384]{2,1,0:T(4,128)}) custom-call(s32[16,2]{1,0:T(8,128)} %copy.19.ids_ref, bf16[768,512]{1,0:T(8,128)(2,1)} %q_ref.3, bf16[768,128]{1,0:T(8,128)(2,1)} %k.1, bf16[768,128]{1,0:T(8,128)(2,1)} %v.1, bf16[768,512]{1,0:T(8,128)(2,1)} %o_ref.1, ...), custom_call_target="tpu_custom_call" | custom-call | flops 2264924160 | bytes 5242880 | tf_op jit(solution)/shard_map/own_stop/pallas_call | solution.py:300
  20.3 0.9 collective-permute-done.1.rest_1_
  21.2 3.5 %collective-permute-done.rest_0_ = bf16[768,256]{1,0:T(8,128)(2,1)} collective-permute-done((bf16[768,256]{1,0:T(8,128)(2,1)}, bf16[768,256]{1,0:T(8,128)(2,1)}, u32[]{:S(2)}, u32[]{:S(2)}) %collective-permute-start) | collective-permute-done | bytes 393248 | tf_op jit(solution)/shard_map/ppermute | solution.py:258
  24.7 10.8 %far_stops.1 = (bf16[768,512]{1,0:T(8,128)(2,1)}, bf16[768,256]{1,0:T(8,128)(2,1)}, bf16[768,256]{1,0:T(8,128)(2,1)}) custom-call(s32[16,2]{1,0:T(8,128)} %copy.19.ids_ref, bf16[768,512]{1,0:T(8,128)(2,1)} %q_ref.3, bf16[768,512]{1,0:T(8,128)(2,1)} %do_ref.3, f32[2,4,384]{2,1,0:T(4,128)} %get-tuple-element.21.norm_ref.refs_2_, ...), custom_call_target="tpu_custom_call" | custom-call | flops 3019898880 | bytes 6291456 | tf_op jit(solution)/shard_map/far_stops/pallas_call | solution.py:330
  35.6 1.8 %constant_dynamic-slice_fusion.1 = bf16[384,512]{1,0:T(8,128)(2,1)} fusion(bf16[768,512]{1,0:T(8,128)(2,1)} %get-tuple-element.25.qg, s32[]{:T(128)S(6)} %select_n.9), kind=kLoop, calls=%fused_computation.6 | loop fusion | bytes 786436 | tf_op jit(solution)/shard_map/dynamic_slice | solution.py:352
  37.3 1.5 %collective-permute-start.4 = (bf16[384,512]{1,0:T(8,128)(2,1)}, bf16[384,512]{1,0:T(8,128)(2,1)}, u32[]{:S(2)}, u32[]{:S(2)}) collective-permute-start(bf16[384,512]{1,0:T(8,128)(2,1)} %constant_dynamic-slice_fusion.1), channel_id=1, source_target_pairs={{0,1},{1,0},{2,3},{3,2},{4,5},{5,4},{6,7},{7,6},{8,9},{9,8},{10,11... | collective-permute-start | bytes 1179656 | tf_op jit(solution)/shard_map/ppermute | solution.py:264
  39.6 1.5 %collective-permute-start.2 = (bf16[768,256]{1,0:T(8,128)(2,1)}, bf16[768,256]{1,0:T(8,128)(2,1)S(1)}, u32[]{:S(2)}, u32[]{:S(2)}) collective-permute-start(bf16[768,256]{1,0:T(8,128)(2,1)} %get-tuple-element.27), channel_id=1, source_target_pairs={{0,30},{2,0},{4,2},{6,4},{8,6},{10,8},{12,10},{14,12},{16,14},{18,... | collective-permute-start | bytes 1179656 | tf_op jit(solution)/shard_map/ppermute | solution.py:258
  41.1 8.6 %collective-permute-done.4.refs_4_.qo = bf16[384,512]{1,0:T(8,128)(2,1)} collective-permute-done((bf16[384,512]{1,0:T(8,128)(2,1)}, bf16[384,512]{1,0:T(8,128)(2,1)}, u32[]{:S(2)}, u32[]{:S(2)}) %collective-permute-start.4) | collective-permute-done | bytes 393248 | tf_op jit(solution)/shard_map/ppermute | solution.py:264
  49.7 1.7 %collective-permute-start.3 = (bf16[768,256]{1,0:T(8,128)(2,1)}, bf16[768,256]{1,0:T(8,128)(2,1)}, u32[]{:S(2)}, u32[]{:S(2)}) collective-permute-start(bf16[768,256]{1,0:T(8,128)(2,1)} %get-tuple-element.28), channel_id=1, source_target_pairs={{0,28},{2,30},{4,0},{6,2},{8,4},{10,6},{12,8},{14,10},{16,12},{18,... | collective-permute-start | bytes 1179656 | tf_op jit(solution)/shard_map/ppermute | solution.py:258
  51.4 7.2 %own_project.1.refs_3_.partial = f32[384,4096]{1,0:T(8,128)} custom-call(s32[2]{0:T(128)} %pad_add_fusion.r_ref, bf16[768,512]{1,0:T(8,128)(2,1)} %get-tuple-element.25.qg, bf16[4096,512]{1,0:T(8,128)(2,1)} %wq.1), custom_call_target="tpu_custom_call" | custom-call | flops 1610612736 | bytes 11534336 | tf_op jit(solution)/shard_map/own_project/pallas_call | solution.py:365
  58.6 5.2 %collective-permute-done.2.rest_0_.refs_5_ = bf16[768,256]{1,0:T(8,128)(2,1)S(1)} collective-permute-done((bf16[768,256]{1,0:T(8,128)(2,1)}, bf16[768,256]{1,0:T(8,128)(2,1)S(1)}, u32[]{:S(2)}, u32[]{:S(2)}) %collective-permute-start.2) | collective-permute-done | bytes 393248 | tf_op jit(solution)/shard_map/ppermute | solution.py:258
  63.8 1.9 %collective-permute-start.7 = (bf16[512,768]{1,0:T(8,128)(2,1)}, bf16[512,768]{1,0:T(8,128)(2,1)}, u32[]{:S(2)}, u32[]{:S(2)}) collective-permute-start(bf16[512,768]{1,0:T(8,128)(2,1)} %get-tuple-element.34.rest_0_), channel_id=1, source_target_pairs={{0,2},{2,0},{4,6},{6,4},{8,10},{10,8},{12,14},{14,12},{16,18},{18,... | collective-permute-start | bytes 2359304 | tf_op jit(solution)/shard_map/ppermute | solution.py:261
  65.8 4.5 %collective-permute-done.3.rest_1_.refs_6_ = bf16[768,256]{1,0:T(8,128)(2,1)} collective-permute-done((bf16[768,256]{1,0:T(8,128)(2,1)}, bf16[768,256]{1,0:T(8,128)(2,1)}, u32[]{:S(2)}, u32[]{:S(2)}) %collective-permute-start.3) | collective-permute-done | bytes 393248 | tf_op jit(solution)/shard_map/ppermute | solution.py:258
  71.0 2.7 %finish_keys.1 = (bf16[768,128]{1,0:T(8,128)(2,1)}, bf16[768,128]{1,0:T(8,128)(2,1)}, bf16[768,256]{1,0:T(8,128)(2,1)}) custom-call(f32[2,64,768]{2,1,0:T(8,128)} %pad_maximum_fusion.tab_ref, f32[2,384,256]{2,1,0:T(8,128)} %get-tuple-element.26.kv0_ref, bf16[768,256]{1,0:T(8,128)(2,1)} %copy-done, bf16[768,256]{1,0:T(8,128)(2,1)} %collective-permute-done.3.rest_1_.refs_6_), custom_call_target="tpu_custom_call" | custom-call | tf_op jit(solution)/shard_map/finish_keys/pallas_call | solution.py:385
  73.6 0.9 %constant_dynamic-slice_fusion = bf16[384,256]{1,0:T(8,128)(2,1)S(1)} fusion(bf16[768,256]{1,0:T(8,128)(2,1)} %get-tuple-element.31, s32[]{:T(128)S(6)} %select_n.9), kind=kLoop, calls=%fused_computation.5 | loop fusion | bytes 393220 | tf_op jit(solution)/shard_map/dynamic_slice | solution.py:352
  75.1 6.8 %collective-permute-done.5.kvo = bf16[384,256]{1,0:T(8,128)(2,1)S(1)} collective-permute-done((bf16[384,256]{1,0:T(8,128)(2,1)S(1)}, bf16[384,256]{1,0:T(8,128)(2,1)S(1)}, u32[]{:S(2)}, u32[]{:S(2)}) %collective-permute-start.5) | collective-permute-done | bytes 196640 | tf_op jit(solution)/shard_map/ppermute | solution.py:264
  82.6 10.5 %project.1 = bf16[384,4096]{1,0:T(8,128)(2,1)} custom-call(s32[2]{0:T(128)} %pad_add_fusion.r_ref, f32[384,4096]{1,0:T(8,128)} %own_project.1.refs_3_.partial, bf16[768,128]{1,0:T(8,128)(2,1)} %get-tuple-element.19.kg, bf16[768,128]{1,0:T(8,128)(2,1)} %get-tuple-element.20.vg, bf16[384,512]{1,0:T(8,128)(2,1)} %collective-permute-done.4.refs_4_.qo, ...), custom_call_target="tpu_custom_call" | custom-call | tf_op jit(solution)/shard_map/project/pallas_call | solution.py:402
  (30 shorter events, 3.0 us)
Async XLA Ops:
  1.3 8.3 %copy-start.2 = (s32[16,2]{0,1:T(2,128)S(1)}, s32[16,2]{0,1:T(2,128)}, u32[]{:S(2)}) copy-start(s32[16,2]{0,1:T(2,128)} %param.16) | copy-start | bytes 388
  5.1 16.1 %collective-permute-start.1 = (bf16[768,256]{1,0:T(8,128)(2,1)}, bf16[768,256]{1,0:T(8,128)(2,1)S(1)}, u32[]{:S(2)}, u32[]{:S(2)}) collective-permute-start(bf16[768,256]{1,0:T(8,128)(2,1)} %get-tuple-element.24), channel_id=1, source_target_pairs={{0,4},{2,6},{4,8},{6,10},{8,12},{10,14},{12,16},{14,18},{16,20},{1... | collective-permute-start | bytes 1179656 | tf_op jit(solution)/shard_map/ppermute | solution.py:258
  8.0 16.7 %collective-permute-start = (bf16[768,256]{1,0:T(8,128)(2,1)}, bf16[768,256]{1,0:T(8,128)(2,1)}, u32[]{:S(2)}, u32[]{:S(2)}) collective-permute-start(bf16[768,256]{1,0:T(8,128)(2,1)} %get-tuple-element.24), channel_id=1, source_target_pairs={{0,2},{2,4},{4,6},{6,8},{8,10},{10,12},{12,14},{14,16},{16,18},{18... | collective-permute-start | bytes 1179656 | tf_op jit(solution)/shard_map/ppermute | solution.py:258
  8.0 30.8 %collective-permute-start.6 = (bf16[512,768]{1,0:T(8,128)(2,1)}, bf16[512,768]{1,0:T(8,128)(2,1)}, u32[]{:S(2)}, u32[]{:S(2)}) collective-permute-start(bf16[512,768]{1,0:T(8,128)(2,1)} %get-tuple-element.32), channel_id=1, source_target_pairs={{0,1},{1,0},{2,3},{3,2},{4,5},{5,4},{6,7},{7,6},{8,9},{9,8},{10,11... | collective-permute-start | bytes 2359304 | tf_op jit(solution)/shard_map/ppermute | solution.py:264
  21.2 3.5 %copy-start.3 = (bf16[768,256]{1,0:T(8,128)(2,1)}, bf16[768,256]{1,0:T(8,128)(2,1)S(1)}, u32[]{:S(2)}) copy-start(bf16[768,256]{1,0:T(8,128)(2,1)S(1)} %collective-permute-done.1.rest_1_) | copy-start | bytes 1179652
  37.3 12.4 %collective-permute-start.4 = (bf16[384,512]{1,0:T(8,128)(2,1)}, bf16[384,512]{1,0:T(8,128)(2,1)}, u32[]{:S(2)}, u32[]{:S(2)}) collective-permute-start(bf16[384,512]{1,0:T(8,128)(2,1)} %constant_dynamic-slice_fusion.1), channel_id=1, source_target_pairs={{0,1},{1,0},{2,3},{3,2},{4,5},{5,4},{6,7},{7,6},{8,9},{9,8},{10,11... | collective-permute-start | bytes 1179656 | tf_op jit(solution)/shard_map/ppermute | solution.py:264
  38.9 31.4 %collective-permute-start.10 = (bf16[512,768]{1,0:T(8,128)(2,1)}, bf16[512,768]{1,0:T(8,128)(2,1)}, u32[]{:S(2)}, u32[]{:S(2)}) collective-permute-start(bf16[512,768]{1,0:T(8,128)(2,1)} %get-tuple-element.35), channel_id=1, source_target_pairs={{0,1},{1,0},{2,3},{3,2},{4,5},{5,4},{6,7},{7,6},{8,9},{9,8},{10,11... | collective-permute-start | bytes 2359304 | tf_op jit(solution)/shard_map/ppermute | solution.py:264
  39.4 30.9 %collective-permute-start.9 = (bf16[512,768]{1,0:T(8,128)(2,1)}, bf16[512,768]{1,0:T(8,128)(2,1)}, u32[]{:S(2)}, u32[]{:S(2)}) collective-permute-start(bf16[512,768]{1,0:T(8,128)(2,1)} %get-tuple-element.34.rest_0_), channel_id=1, source_target_pairs={{0,8},{2,10},{4,12},{6,14},{8,0},{10,2},{12,4},{14,6},{16,24},{18,... | collective-permute-start | bytes 2359304 | tf_op jit(solution)/shard_map/ppermute | solution.py:261
  39.4 30.9 %collective-permute-start.8 = (bf16[512,768]{1,0:T(8,128)(2,1)}, bf16[512,768]{1,0:T(8,128)(2,1)}, u32[]{:S(2)}, u32[]{:S(2)}) collective-permute-start(bf16[512,768]{1,0:T(8,128)(2,1)} %get-tuple-element.34.rest_0_), channel_id=1, source_target_pairs={{0,4},{2,6},{4,0},{6,2},{8,12},{10,14},{12,8},{14,10},{16,20},{18,... | collective-permute-start | bytes 2359304 | tf_op jit(solution)/shard_map/ppermute | solution.py:261
  39.6 24.2 %collective-permute-start.2 = (bf16[768,256]{1,0:T(8,128)(2,1)}, bf16[768,256]{1,0:T(8,128)(2,1)S(1)}, u32[]{:S(2)}, u32[]{:S(2)}) collective-permute-start(bf16[768,256]{1,0:T(8,128)(2,1)} %get-tuple-element.27), channel_id=1, source_target_pairs={{0,30},{2,0},{4,2},{6,4},{8,6},{10,8},{12,10},{14,12},{16,14},{18,... | collective-permute-start | bytes 1179656 | tf_op jit(solution)/shard_map/ppermute | solution.py:258
  49.7 20.6 %collective-permute-start.3 = (bf16[768,256]{1,0:T(8,128)(2,1)}, bf16[768,256]{1,0:T(8,128)(2,1)}, u32[]{:S(2)}, u32[]{:S(2)}) collective-permute-start(bf16[768,256]{1,0:T(8,128)(2,1)} %get-tuple-element.28), channel_id=1, source_target_pairs={{0,28},{2,30},{4,0},{6,2},{8,4},{10,6},{12,8},{14,10},{16,12},{18,... | collective-permute-start | bytes 1179656 | tf_op jit(solution)/shard_map/ppermute | solution.py:258
  63.8 6.4 %copy-start = (bf16[768,256]{1,0:T(8,128)(2,1)}, bf16[768,256]{1,0:T(8,128)(2,1)S(1)}, u32[]{:S(2)}) copy-start(bf16[768,256]{1,0:T(8,128)(2,1)S(1)} %collective-permute-done.2.rest_0_.refs_5_) | copy-start | bytes 1179652
  63.8 18.0 %collective-permute-start.7 = (bf16[512,768]{1,0:T(8,128)(2,1)}, bf16[512,768]{1,0:T(8,128)(2,1)}, u32[]{:S(2)}, u32[]{:S(2)}) collective-permute-start(bf16[512,768]{1,0:T(8,128)(2,1)} %get-tuple-element.34.rest_0_), channel_id=1, source_target_pairs={{0,2},{2,0},{4,6},{6,4},{8,10},{10,8},{12,14},{14,12},{16,18},{18,... | collective-permute-start | bytes 2359304 | tf_op jit(solution)/shard_map/ppermute | solution.py:261
  70.3 11.6 %collective-permute-start.11 = (bf16[512,768]{1,0:T(8,128)(2,1)}, bf16[512,768]{1,0:T(8,128)(2,1)}, u32[]{:S(2)}, u32[]{:S(2)}) collective-permute-start(bf16[512,768]{1,0:T(8,128)(2,1)} %get-tuple-element.36.rest_2_), channel_id=1, source_target_pairs={{0,2},{2,0},{4,6},{6,4},{8,10},{10,8},{12,14},{14,12},{16,18},{18,... | collective-permute-start | bytes 2359304 | tf_op jit(solution)/shard_map/ppermute | solution.py:261
  70.4 11.5 %collective-permute-start.12 = (bf16[512,768]{1,0:T(8,128)(2,1)}, bf16[512,768]{1,0:T(8,128)(2,1)}, u32[]{:S(2)}, u32[]{:S(2)}) collective-permute-start(bf16[512,768]{1,0:T(8,128)(2,1)} %get-tuple-element.37.rest_4_), channel_id=1, source_target_pairs={{0,2},{2,0},{4,6},{6,4},{8,10},{10,8},{12,14},{14,12},{16,18},{18,... | collective-permute-start | bytes 2359304 | tf_op jit(solution)/shard_map/ppermute | solution.py:261
  70.9 11.0 %collective-permute-start.13 = (bf16[512,768]{1,0:T(8,128)(2,1)}, bf16[512,768]{1,0:T(8,128)(2,1)}, u32[]{:S(2)}, u32[]{:S(2)}) collective-permute-start(bf16[512,768]{1,0:T(8,128)(2,1)} %get-tuple-element.38.rest_6_), channel_id=1, source_target_pairs={{0,2},{2,0},{4,6},{6,4},{8,10},{10,8},{12,14},{14,12},{16,18},{18,... | collective-permute-start | bytes 2359304 | tf_op jit(solution)/shard_map/ppermute | solution.py:261
  74.6 7.3 %collective-permute-start.5 = (bf16[384,256]{1,0:T(8,128)(2,1)S(1)}, bf16[384,256]{1,0:T(8,128)(2,1)S(1)}, u32[]{:S(2)}, u32[]{:S(2)}) collective-permute-start(bf16[384,256]{1,0:T(8,128)(2,1)S(1)} %constant_dynamic-slice_fusion), channel_id=1, source_target_pairs={{0,1},{1,0},{2,3},{3,2},{4,5},{5,4},{6,7},{7,6},{8,9},{9,8},{10,11... | collective-permute-start | bytes 589832 | tf_op jit(solution)/shard_map/ppermute | solution.py:264
  81.9 0.7 copy-start.1

commit v5 on v4

--- a/solution.py
+++ b/solution.py
@@ -155,11 +155,7 @@
         both_ref[rows, hd:] = value_grad
 
 
-def own_project_kernel(r_ref, qg, wq, out_ref):
-    out_ref[...] = dot(qg[...], wq[...], NT)
-
-
-def project_kernel(others, slots, r_ref, partial, kg, vg, qo, kvo, wk, wv, *rest):
+def project_kernel(others, slots, r_ref, qg, kg, vg, qo, kvo, wq, wk, wv, *rest):
     j = pl.program_id(0)
     pieces, (out_ref, buf, sem) = rest[:8], rest[8:]
     kw = kg.shape[1]
@@ -182,7 +178,7 @@
             for copy in copies(i):
                 copy.start()
 
-    total = partial[...] + dot(kg[...], wk[...], NT) + dot(vg[...], wv[...], NT)
+    total = dot(qg[...], wq[...], NT) + dot(kg[...], wk[...], NT) + dot(vg[...], wv[...], NT)
     for i in range(4):
         @pl.when(j == i)
         def _(i=i):
@@ -321,11 +317,10 @@
         name="own_stop",
     )(stretch_ids, q_rot, k_rot, values, attn_out, out_grad, log_norm)
 
-    near, later = tie((near, later), norm)
+    near, later, norm = tie((near, later, norm))
     over_x = swap_seq(near, 2)
     over_z = swap_seq(near, 4)
     over_y = fetch(later)
-    near_twin = swap_seq(near, 1)
 
     query_grad, *homes = pl.pallas_call(
         functools.partial(far_kernel, seq_count),
@@ -362,25 +357,9 @@
     wquarter = lambda cols: pl.BlockSpec((quarter, cols), lambda j, r: ((r[0] // 2) ^ j, 0))
     column = pl.BlockSpec((out_rows, quarter), lambda j, r: (0, (r[0] // 2) ^ j))
     mine = lambda shape: pl.BlockSpec(shape, lambda j, r: (r[1], 0))
-    partial = pl.pallas_call(
-        own_project_kernel,
-        out_shape=jax.ShapeDtypeStruct((out_rows, d_model), F32),
-        grid_spec=pltpu.PrefetchScalarGridSpec(
-            num_scalar_prefetch=1,
-            grid=(4,),
-            in_specs=[mine((out_rows, col_width)), wquarter(col_width)],
-            out_specs=column,
-        ),
-        compiler_params=params(),
-        cost_estimate=pl.CostEstimate(
-            flops=2 * out_rows * d_model * col_width, bytes_accessed=11 * 2**20, transcendentals=0
-        ),
-        name="own_project",
-    )(spot, query_grad, q_weight)
     homes = [shift_seq(x, -(i + 1)) for i, x in enumerate(homes)]
-    over_x, over_z, over_y = tie((over_x, over_z, over_y), partial, q_other, *homes)
-    pieces = [near, near_twin]
-    for x in (over_x, over_z, over_y):
+    pieces = []
+    for x in tie((near, over_x, over_z, over_y), q_other, *homes):
         pieces += [x, swap_seq(x, 1)]
     key_grad, value_grad, both = pl.pallas_call(
         finish_kernel,
@@ -406,11 +385,12 @@
             num_scalar_prefetch=1,
             grid=(4,),
             in_specs=[
-                column,
+                mine((out_rows, col_width)),
                 mine((out_rows, hd)),
                 mine((out_rows, hd)),
                 full((out_rows, col_width * others)),
                 full((out_rows, 2 * hd * others)),
+                wquarter(col_width),
                 wquarter(hd),
                 wquarter(hd),
             ]
@@ -425,11 +405,12 @@
         name="project",
     )(
         spot,
-        partial,
+        query_grad,
         key_grad,
         value_grad,
         q_other,
         kv_other,
+        q_weight,
         k_weight,
         v_weight,
         *pieces,

time: 93.8 us -> 101 us (1.077)
  waiting for transfers between devices: 29.5 us -> 39.2 us
  Pallas kernels: 43.3 us -> 36.9 us
  starting transfers between devices: 13.1 us -> 16.7 us
    pallas_call x1 -> x0, Pallas kernels: 7.18 us -> none  [local(): pl.pallas_call(own_project_kernel, out_shape=jax.ShapeDtypeStruct((out_ro...]
    ppermute x4, waiting for transfers between devices: 14.1 us -> 20.7 us  [shift_seq(): lax.ppermute(x, 'seq', [(i, (i + by) % seq_count) for i in range(seq_coun...]
    ppermute x4, waiting for transfers between devices: 15.4 us -> 18.5 us  [from_head(): lax.ppermute(x, 'head', [(i, (i - by) % head_axis) for i in range(head_ax...]
    ppermute x6, starting transfers between devices: 2.85 us -> 4.31 us  [swap_seq(): return lax.ppermute(x, 'seq', [(i, i ^ bit) for i in range(seq_count)])]
    ppermute x4, starting transfers between devices: 4.1 us -> 5.19 us  [from_head(): lax.ppermute(x, 'head', [(i, (i - by) % head_axis) for i in range(head_ax...]
    ppermute x4, starting transfers between devices: 6.13 us -> 7.21 us  [shift_seq(): lax.ppermute(x, 'seq', [(i, (i + by) % seq_count) for i in range(seq_coun...]
    unnamed x9 -> x11, local copies, waits for them, and re-layouts: 1.34 us -> 2.12 us
  transfers between devices with their start and end apart: 14 -> 14, of which waited for: 6 -> 5; matrix products, arithmetic and copies ran while one was open for 6% -> 3% of each run, Pallas kernels for 31% -> 11%
where the time goes in v5:
time: 101 us; the launch traced here: 100 us
  waiting for transfers between devices  39.2 us (39%)
  Pallas kernels  36.9 us (37%)
  starting transfers between devices  16.7 us (17%)
  local copies, waits for them, and re-layouts  4.09 us (4%)
  other arithmetic  2.45 us (2%)
    ppermute x4, waiting for transfers between devices, shift_seq(): lax.ppermute(x, 'seq', [(i, (i + by) % seq_count) for i in range(seq_coun...  20.7 us
    ppermute x4, waiting for transfers between devices, from_head(): lax.ppermute(x, 'head', [(i, (i - by) % head_axis) for i in range(head_ax...  18.5 us
    pallas_call x1, Pallas kernels, local(): pl.pallas_call(functools.partial(project_kernel, others, slots), out_shap...  11.3 us
    pallas_call x1, Pallas kernels, local(): pl.pallas_call(functools.partial(far_kernel, seq_count), out_shape=(jax.S...  10.9 us
    pallas_call x1, Pallas kernels, local(): pl.pallas_call(functools.partial(own_kernel, seq_count), out_shape=(jax.S...  8.25 us
    ppermute x4, starting transfers between devices, shift_seq(): lax.ppermute(x, 'seq', [(i, (i + by) % seq_count) for i in range(seq_coun...  7.21 us
    ppermute x4, starting transfers between devices, from_head(): lax.ppermute(x, 'head', [(i, (i - by) % head_axis) for i in range(head_ax...  5.19 us
    ppermute x6, starting transfers between devices, swap_seq(): return lax.ppermute(x, 'seq', [(i, i ^ bit) for i in range(seq_count)])  4.31 us
  transfers between devices with their start and end apart: 14, of which 5 were waited for; matrix products, arithmetic and copies ran while one was open for 3% of the time, Pallas kernels for 11%

profile of v5, /device:TPU:0, one launch (start us, length us, event | category | flops | bytes accessed | tf_op | source)
XLA Modules:
  0.0 100.3 jit_solution(9185236971976678900)
XLA Ops:
  1.2 3.8 %prep.1 = (bf16[768,256]{1,0:T(8,128)(2,1)}, bf16[512,768]{1,0:T(8,128)(2,1)}, bf16[512,768]{1,0:T(8,128)(2,1)}) custom-call(s32[2]{0:T(128)} %pad_add_fusion.r_ref, bf16[768,128]{1,0:T(8,128)(2,1)} %k_ref.1, bf16[768,128]{1,0:T(8,128)(2,1)} %v_ref.1, bf16[4096,512]{1,0:T(8,128)(2,1)} %wq.1, bf16[4096,128]{1,0:T(8,128)(2,1)} %wk.1, bf16[4096,128]{1,0:T(8,128)(2,1)} %wv.1, ...), custom_call_target="tpu_custom_call" | custom-call | tf_op jit(solution)/shard_map/prep/pallas_call | solution.py:266
  5.0 2.9 %collective-permute-start.2 = (bf16[768,256]{1,0:T(8,128)(2,1)}, bf16[768,256]{1,0:T(8,128)(2,1)S(1)}, u32[]{:S(2)}, u32[]{:S(2)}) collective-permute-start(bf16[768,256]{1,0:T(8,128)(2,1)} %get-tuple-element.29), channel_id=1, source_target_pairs={{0,4},{2,6},{4,8},{6,10},{8,12},{10,14},{12,16},{14,18},{16,20},{1... | collective-permute-start | bytes 1179656 | tf_op jit(solution)/shard_map/ppermute | solution.py:254
  7.9 1.5 %collective-permute-start = (bf16[512,768]{1,0:T(8,128)(2,1)}, bf16[512,768]{1,0:T(8,128)(2,1)}, u32[]{:S(2)}, u32[]{:S(2)}) collective-permute-start(bf16[512,768]{1,0:T(8,128)(2,1)} %get-tuple-element.23), channel_id=1, source_target_pairs={{0,1},{1,0},{2,3},{3,2},{4,5},{5,4},{6,7},{7,6},{8,9},{9,8},{10,11... | collective-permute-start | bytes 2359304 | tf_op jit(solution)/shard_map/ppermute | solution.py:260
  9.7 0.8 multiply_cosine_fusion
  11.2 0.8 pad_maximum_fusion.tab_ref
  12.0 8.3 %own_stop.1 = (f32[2,512,384]{2,1,0:T(8,128)}, f32[2,384,256]{2,1,0:T(8,128)}, f32[2,4,384]{2,1,0:T(4,128)}, f32[2,4,384]{2,1,0:T(4,128)}) custom-call(s32[16,2]{1,0:T(8,128)} %copy.21.ids_ref, bf16[768,512]{1,0:T(8,128)(2,1)} %q_ref.3, bf16[768,128]{1,0:T(8,128)(2,1)} %k_ref.1, bf16[768,128]{1,0:T(8,128)(2,1)} %v_ref.1, bf16[768,512]{1,0:T(8,128)(2,1)} %o_ref.1, ...), custom_call_target="tpu_custom_call" | custom-call | flops 2264924160 | bytes 5242880 | tf_op jit(solution)/shard_map/own_stop/pallas_call | solution.py:296
  20.3 7.8 %collective-permute-done.refs_0_ = bf16[512,768]{1,0:T(8,128)(2,1)} collective-permute-done((bf16[512,768]{1,0:T(8,128)(2,1)}, bf16[512,768]{1,0:T(8,128)(2,1)}, u32[]{:S(2)}, u32[]{:S(2)}) %collective-permute-start) | collective-permute-done | bytes 786464 | tf_op jit(solution)/shard_map/ppermute | solution.py:260
  28.0 0.7 copy-done.4
  28.8 10.9 %far_stops.1 = (bf16[768,512]{1,0:T(8,128)(2,1)}, bf16[768,256]{1,0:T(8,128)(2,1)}, bf16[768,256]{1,0:T(8,128)(2,1)}) custom-call(s32[16,2]{1,0:T(8,128)} %copy.21.ids_ref, bf16[768,512]{1,0:T(8,128)(2,1)} %q_ref.3, bf16[768,512]{1,0:T(8,128)(2,1)} %do_ref.3, f32[2,4,384]{2,1,0:T(4,128)} %get-tuple-element.26.norm_ref, ...), custom_call_target="tpu_custom_call" | custom-call | flops 3019898880 | bytes 6291456 | tf_op jit(solution)/shard_map/far_stops/pallas_call | solution.py:325
  39.7 1.0 %constant_dynamic-slice_fusion.1 = bf16[384,512]{1,0:T(8,128)(2,1)S(1)} fusion(bf16[768,512]{1,0:T(8,128)(2,1)} %get-tuple-element.30.qg, s32[]{:T(128)S(6)} %select_n.9), kind=kLoop, calls=%fused_computation.6 | loop fusion | bytes 786436 | tf_op jit(solution)/shard_map/dynamic_slice | solution.py:347
  40.7 1.6 %collective-permute-start.5 = (bf16[384,512]{1,0:T(8,128)(2,1)S(1)}, bf16[384,512]{1,0:T(8,128)(2,1)S(1)}, u32[]{:S(2)}, u32[]{:S(2)}) collective-permute-start(bf16[384,512]{1,0:T(8,128)(2,1)S(1)} %constant_dynamic-slice_fusion.1), channel_id=1, source_target_pairs={{0,1},{1,0},{2,3},{3,2},{4,5},{5,4},{6,7},{7,6},{8,9},{9,8},{10,11... | collective-permute-start | bytes 1179656 | tf_op jit(solution)/shard_map/ppermute | solution.py:260
  42.8 1.6 %collective-permute-start.8 = (bf16[512,768]{1,0:T(8,128)(2,1)}, bf16[512,768]{1,0:T(8,128)(2,1)}, u32[]{:S(2)}, u32[]{:S(2)}) collective-permute-start(bf16[512,768]{1,0:T(8,128)(2,1)} %get-tuple-element.37.refs_0_), channel_id=1, source_target_pairs={{0,8},{2,10},{4,12},{6,14},{8,0},{10,2},{12,4},{14,6},{16,24},{18,... | collective-permute-start | bytes 2359304 | tf_op jit(solution)/shard_map/ppermute | solution.py:257
  44.4 1.7 %collective-permute-start.7 = (bf16[512,768]{1,0:T(8,128)(2,1)}, bf16[512,768]{1,0:T(8,128)(2,1)}, u32[]{:S(2)}, u32[]{:S(2)}) collective-permute-start(bf16[512,768]{1,0:T(8,128)(2,1)} %get-tuple-element.37.refs_0_), channel_id=1, source_target_pairs={{0,4},{2,6},{4,0},{6,2},{8,12},{10,14},{12,8},{14,10},{16,20},{18,... | collective-permute-start | bytes 2359304 | tf_op jit(solution)/shard_map/ppermute | solution.py:257
  46.0 1.2 %collective-permute-start.3 = (bf16[768,256]{1,0:T(8,128)(2,1)}, bf16[768,256]{1,0:T(8,128)(2,1)S(1)}, u32[]{:S(2)}, u32[]{:S(2)}) collective-permute-start(bf16[768,256]{1,0:T(8,128)(2,1)} %get-tuple-element.32), channel_id=1, source_target_pairs={{0,30},{2,0},{4,2},{6,4},{8,6},{10,8},{12,10},{14,12},{16,14},{18,... | collective-permute-start | bytes 1179656 | tf_op jit(solution)/shard_map/ppermute | solution.py:254
  47.2 5.4 %collective-permute-done.5.refs_4_.qo = bf16[384,512]{1,0:T(8,128)(2,1)S(1)} collective-permute-done((bf16[384,512]{1,0:T(8,128)(2,1)S(1)}, bf16[384,512]{1,0:T(8,128)(2,1)S(1)}, u32[]{:S(2)}, u32[]{:S(2)}) %collective-permute-start.5) | collective-permute-done | bytes 393248 | tf_op jit(solution)/shard_map/ppermute | solution.py:260
  52.7 3.0 %collective-permute-start.4 = (bf16[768,256]{1,0:T(8,128)(2,1)}, bf16[768,256]{1,0:T(8,128)(2,1)}, u32[]{:S(2)}, u32[]{:S(2)}) collective-permute-start(bf16[768,256]{1,0:T(8,128)(2,1)} %get-tuple-element.33), channel_id=1, source_target_pairs={{0,28},{2,30},{4,0},{6,2},{8,4},{10,6},{12,8},{14,10},{16,12},{18,... | collective-permute-start | bytes 1179656 | tf_op jit(solution)/shard_map/ppermute | solution.py:254
  55.7 14.3 %collective-permute-done.3.rest_0_.refs_5_ = bf16[768,256]{1,0:T(8,128)(2,1)S(1)} collective-permute-done((bf16[768,256]{1,0:T(8,128)(2,1)}, bf16[768,256]{1,0:T(8,128)(2,1)S(1)}, u32[]{:S(2)}, u32[]{:S(2)}) %collective-permute-start.3) | collective-permute-done | bytes 393248 | tf_op jit(solution)/shard_map/ppermute | solution.py:254
  70.0 6.4 %collective-permute-done.4.rest_1_.refs_6_ = bf16[768,256]{1,0:T(8,128)(2,1)} collective-permute-done((bf16[768,256]{1,0:T(8,128)(2,1)}, bf16[768,256]{1,0:T(8,128)(2,1)}, u32[]{:S(2)}, u32[]{:S(2)}) %collective-permute-start.4) | collective-permute-done | bytes 393248 | tf_op jit(solution)/shard_map/ppermute | solution.py:254
  77.5 2.7 %finish_keys.1 = (bf16[768,128]{1,0:T(8,128)(2,1)}, bf16[768,128]{1,0:T(8,128)(2,1)}, bf16[768,256]{1,0:T(8,128)(2,1)}) custom-call(f32[2,64,768]{2,1,0:T(8,128)} %pad_maximum_fusion.tab_ref, f32[2,384,256]{2,1,0:T(8,128)} %get-tuple-element.31.kv0_ref, bf16[768,256]{1,0:T(8,128)(2,1)} %copy-done, bf16[768,256]{1,0:T(8,128)(2,1)} %collective-permute-done.4.rest_1_.refs_6_), custom_call_target="tpu_custom_call" | custom-call | tf_op jit(solution)/shard_map/finish_keys/pallas_call | solution.py:364
  80.2 0.9 constant_dynamic-slice_fusion
  81.1 1.6 %collective-permute-start.6 = (bf16[384,256]{1,0:T(8,128)(2,1)S(1)}, bf16[384,256]{1,0:T(8,128)(2,1)S(1)}, u32[]{:S(2)}, u32[]{:S(2)}) collective-permute-start(bf16[384,256]{1,0:T(8,128)(2,1)S(1)} %constant_dynamic-slice_fusion), channel_id=1, source_target_pairs={{0,1},{1,0},{2,3},{3,2},{4,5},{5,4},{6,7},{7,6},{8,9},{9,8},{10,11... | collective-permute-start | bytes 589832 | tf_op jit(solution)/shard_map/ppermute | solution.py:260
  82.7 5.4 %collective-permute-done.6.kvo = bf16[384,256]{1,0:T(8,128)(2,1)S(1)} collective-permute-done((bf16[384,256]{1,0:T(8,128)(2,1)S(1)}, bf16[384,256]{1,0:T(8,128)(2,1)S(1)}, u32[]{:S(2)}, u32[]{:S(2)}) %collective-permute-start.6) | collective-permute-done | bytes 196640 | tf_op jit(solution)/shard_map/ppermute | solution.py:260
  88.1 0.7 copy-done.2
  88.8 11.3 %project.1 = bf16[384,4096]{1,0:T(8,128)(2,1)} custom-call(s32[2]{0:T(128)} %pad_add_fusion.r_ref, bf16[768,512]{1,0:T(8,128)(2,1)} %get-tuple-element.30.qg, bf16[768,128]{1,0:T(8,128)(2,1)} %get-tuple-element.21.kg, bf16[768,128]{1,0:T(8,128)(2,1)} %get-tuple-element.22.vg, bf16[384,512]{1,0:T(8,128)(2,1)} %copy-done.1, bf16[384,256]{1,0:T(8,128)(2,1)} %copy-done.2, ...), custom_call_target="tpu_custom_call" | custom-call | tf_op jit(solution)/shard_map/project/pallas_call | solution.py:381
  (31 shorter events, 3.2 us)
Async XLA Ops:
  1.2 8.2 %copy-start.3 = (s32[16,2]{0,1:T(2,128)S(1)}, s32[16,2]{0,1:T(2,128)}, u32[]{:S(2)}) copy-start(s32[16,2]{0,1:T(2,128)} %param.16) | copy-start | bytes 388
  5.0 23.0 %collective-permute-start.2 = (bf16[768,256]{1,0:T(8,128)(2,1)}, bf16[768,256]{1,0:T(8,128)(2,1)S(1)}, u32[]{:S(2)}, u32[]{:S(2)}) collective-permute-start(bf16[768,256]{1,0:T(8,128)(2,1)} %get-tuple-element.29), channel_id=1, source_target_pairs={{0,4},{2,6},{4,8},{6,10},{8,12},{10,14},{12,16},{14,18},{16,20},{1... | collective-permute-start | bytes 1179656 | tf_op jit(solution)/shard_map/ppermute | solution.py:254
  7.9 20.1 %collective-permute-start.1 = (bf16[768,256]{1,0:T(8,128)(2,1)}, bf16[768,256]{1,0:T(8,128)(2,1)}, u32[]{:S(2)}, u32[]{:S(2)}) collective-permute-start(bf16[768,256]{1,0:T(8,128)(2,1)} %get-tuple-element.29), channel_id=1, source_target_pairs={{0,2},{2,4},{4,6},{6,8},{8,10},{10,12},{12,14},{14,16},{16,18},{18... | collective-permute-start | bytes 1179656 | tf_op jit(solution)/shard_map/ppermute | solution.py:254
  7.9 20.1 %collective-permute-start = (bf16[512,768]{1,0:T(8,128)(2,1)}, bf16[512,768]{1,0:T(8,128)(2,1)}, u32[]{:S(2)}, u32[]{:S(2)}) collective-permute-start(bf16[512,768]{1,0:T(8,128)(2,1)} %get-tuple-element.23), channel_id=1, source_target_pairs={{0,1},{1,0},{2,3},{3,2},{4,5},{5,4},{6,7},{7,6},{8,9},{9,8},{10,11... | collective-permute-start | bytes 2359304 | tf_op jit(solution)/shard_map/ppermute | solution.py:260
  28.0 0.7 copy-start.4
  40.7 12.0 %collective-permute-start.5 = (bf16[384,512]{1,0:T(8,128)(2,1)S(1)}, bf16[384,512]{1,0:T(8,128)(2,1)S(1)}, u32[]{:S(2)}, u32[]{:S(2)}) collective-permute-start(bf16[384,512]{1,0:T(8,128)(2,1)S(1)} %constant_dynamic-slice_fusion.1), channel_id=1, source_target_pairs={{0,1},{1,0},{2,3},{3,2},{4,5},{5,4},{6,7},{7,6},{8,9},{9,8},{10,11... | collective-permute-start | bytes 1179656 | tf_op jit(solution)/shard_map/ppermute | solution.py:260
  42.3 34.1 %collective-permute-start.9 = (bf16[512,768]{1,0:T(8,128)(2,1)}, bf16[512,768]{1,0:T(8,128)(2,1)}, u32[]{:S(2)}, u32[]{:S(2)}) collective-permute-start(bf16[512,768]{1,0:T(8,128)(2,1)} %get-tuple-element.38), channel_id=1, source_target_pairs={{0,1},{1,0},{2,3},{3,2},{4,5},{5,4},{6,7},{7,6},{8,9},{9,8},{10,11... | collective-permute-start | bytes 2359304 | tf_op jit(solution)/shard_map/ppermute | solution.py:260
  42.8 33.6 %collective-permute-start.8 = (bf16[512,768]{1,0:T(8,128)(2,1)}, bf16[512,768]{1,0:T(8,128)(2,1)}, u32[]{:S(2)}, u32[]{:S(2)}) collective-permute-start(bf16[512,768]{1,0:T(8,128)(2,1)} %get-tuple-element.37.refs_0_), channel_id=1, source_target_pairs={{0,8},{2,10},{4,12},{6,14},{8,0},{10,2},{12,4},{14,6},{16,24},{18,... | collective-permute-start | bytes 2359304 | tf_op jit(solution)/shard_map/ppermute | solution.py:257
  44.4 32.0 %collective-permute-start.7 = (bf16[512,768]{1,0:T(8,128)(2,1)}, bf16[512,768]{1,0:T(8,128)(2,1)}, u32[]{:S(2)}, u32[]{:S(2)}) collective-permute-start(bf16[512,768]{1,0:T(8,128)(2,1)} %get-tuple-element.37.refs_0_), channel_id=1, source_target_pairs={{0,4},{2,6},{4,0},{6,2},{8,12},{10,14},{12,8},{14,10},{16,20},{18,... | collective-permute-start | bytes 2359304 | tf_op jit(solution)/shard_map/ppermute | solution.py:257
  46.0 24.0 %collective-permute-start.3 = (bf16[768,256]{1,0:T(8,128)(2,1)}, bf16[768,256]{1,0:T(8,128)(2,1)S(1)}, u32[]{:S(2)}, u32[]{:S(2)}) collective-permute-start(bf16[768,256]{1,0:T(8,128)(2,1)} %get-tuple-element.32), channel_id=1, source_target_pairs={{0,30},{2,0},{4,2},{6,4},{8,6},{10,8},{12,10},{14,12},{16,14},{18,... | collective-permute-start | bytes 1179656 | tf_op jit(solution)/shard_map/ppermute | solution.py:254
  52.7 17.3 %copy-start.1 = (bf16[384,512]{1,0:T(8,128)(2,1)}, bf16[384,512]{1,0:T(8,128)(2,1)S(1)}, u32[]{:S(2)}) copy-start(bf16[384,512]{1,0:T(8,128)(2,1)S(1)} %collective-permute-done.5.refs_4_.qo) | copy-start | bytes 1179652
  52.7 23.7 %collective-permute-start.4 = (bf16[768,256]{1,0:T(8,128)(2,1)}, bf16[768,256]{1,0:T(8,128)(2,1)}, u32[]{:S(2)}, u32[]{:S(2)}) collective-permute-start(bf16[768,256]{1,0:T(8,128)(2,1)} %get-tuple-element.33), channel_id=1, source_target_pairs={{0,28},{2,30},{4,0},{6,2},{8,4},{10,6},{12,8},{14,10},{16,12},{18,... | collective-permute-start | bytes 1179656 | tf_op jit(solution)/shard_map/ppermute | solution.py:254
  70.0 6.4 %copy-start = (bf16[768,256]{1,0:T(8,128)(2,1)}, bf16[768,256]{1,0:T(8,128)(2,1)S(1)}, u32[]{:S(2)}) copy-start(bf16[768,256]{1,0:T(8,128)(2,1)S(1)} %collective-permute-done.3.rest_0_.refs_5_) | copy-start | bytes 1179652
  76.4 11.7 %collective-permute-start.10 = (bf16[512,768]{1,0:T(8,128)(2,1)}, bf16[512,768]{1,0:T(8,128)(2,1)}, u32[]{:S(2)}, u32[]{:S(2)}) collective-permute-start(bf16[512,768]{1,0:T(8,128)(2,1)} %get-tuple-element.39.rest_0_), channel_id=1, source_target_pairs={{0,2},{2,0},{4,6},{6,4},{8,10},{10,8},{12,14},{14,12},{16,18},{18,... | collective-permute-start | bytes 2359304 | tf_op jit(solution)/shard_map/ppermute | solution.py:257
  76.5 11.6 %collective-permute-start.11 = (bf16[512,768]{1,0:T(8,128)(2,1)}, bf16[512,768]{1,0:T(8,128)(2,1)}, u32[]{:S(2)}, u32[]{:S(2)}) collective-permute-start(bf16[512,768]{1,0:T(8,128)(2,1)} %get-tuple-element.40.rest_2_), channel_id=1, source_target_pairs={{0,2},{2,0},{4,6},{6,4},{8,10},{10,8},{12,14},{14,12},{16,18},{18,... | collective-permute-start | bytes 2359304 | tf_op jit(solution)/shard_map/ppermute | solution.py:257
  77.0 11.1 %collective-permute-start.12 = (bf16[512,768]{1,0:T(8,128)(2,1)}, bf16[512,768]{1,0:T(8,128)(2,1)}, u32[]{:S(2)}, u32[]{:S(2)}) collective-permute-start(bf16[512,768]{1,0:T(8,128)(2,1)} %get-tuple-element.41.rest_4_), channel_id=1, source_target_pairs={{0,2},{2,0},{4,6},{6,4},{8,10},{10,8},{12,14},{14,12},{16,18},{18,... | collective-permute-start | bytes 2359304 | tf_op jit(solution)/shard_map/ppermute | solution.py:257
  77.1 11.0 %collective-permute-start.13 = (bf16[512,768]{1,0:T(8,128)(2,1)}, bf16[512,768]{1,0:T(8,128)(2,1)}, u32[]{:S(2)}, u32[]{:S(2)}) collective-permute-start(bf16[512,768]{1,0:T(8,128)(2,1)} %get-tuple-element.42.rest_6_), channel_id=1, source_target_pairs={{0,2},{2,0},{4,6},{6,4},{8,10},{10,8},{12,14},{14,12},{16,18},{18,... | collective-permute-start | bytes 2359304 | tf_op jit(solution)/shard_map/ppermute | solution.py:257
  81.1 7.0 %collective-permute-start.6 = (bf16[384,256]{1,0:T(8,128)(2,1)S(1)}, bf16[384,256]{1,0:T(8,128)(2,1)S(1)}, u32[]{:S(2)}, u32[]{:S(2)}) collective-permute-start(bf16[384,256]{1,0:T(8,128)(2,1)S(1)} %constant_dynamic-slice_fusion), channel_id=1, source_target_pairs={{0,1},{1,0},{2,3},{3,2},{4,5},{5,4},{6,7},{7,6},{8,9},{9,8},{10,11... | collective-permute-start | bytes 589832 | tf_op jit(solution)/shard_map/ppermute | solution.py:260
  88.1 0.7 copy-start.2

commit v6 on v3

--- a/solution.py
+++ b/solution.py
@@ -168,8 +168,7 @@
         def _(i=i):
             copy(i).start()
 
-    own = jnp.concatenate([wq[...], wk[...], wv[...]], axis=1)
-    total = dot(jnp.concatenate([qg[...], kg[...], vg[...]], axis=1), own, NT)
+    total = dot(qg[...], wq[...], NT) + dot(kg[...], wk[...], NT) + dot(vg[...], wv[...], NT)
     for i in range(8):
         @pl.when(j == i)
         def _(i=i):
@@ -178,10 +177,14 @@
     slot = lax.rem(j, slots)
     width = qw + 2 * kw
     for s in range(others):
-        grads = jnp.concatenate(
-            [qo[:, s * qw : (s + 1) * qw], kvo[:, s * 2 * kw : (s + 1) * 2 * kw]], axis=1
+        total = total + dot(
+            qo[:, s * qw : (s + 1) * qw], buf[slot, :, s * width : s * width + qw], NT
         )
-        total = total + dot(grads, buf[slot, :, s * width : (s + 1) * width], NT)
+        total = total + dot(
+            kvo[:, s * 2 * kw : (s + 1) * 2 * kw],
+            buf[slot, :, s * width + qw : (s + 1) * width],
+            NT,
+        )
     out_ref[...] = total.astype(BF16)
 
 

time: 91.3 us -> 91.4 us (level)
  no operation moved by 1% of the time
where the time goes in v6:
time: 91.4 us; the launch traced here: 90.9 us
  Pallas kernels  38.6 us (42%)
  waiting for transfers between devices  27.3 us (30%)
  starting transfers between devices  16.9 us (18%)
  local copies, waits for them, and re-layouts  4.82 us (5%)
  other arithmetic  2.43 us (3%)
    ppermute x4, waiting for transfers between devices, from_head(): lax.ppermute(x, 'head', [(i, (i - by) % head_axis) for i in range(head_ax...  15.4 us
    pallas_call x1, Pallas kernels, local(): pl.pallas_call(functools.partial(project_kernel, others, slots), out_shap...  12.9 us
    ppermute x4, waiting for transfers between devices, shift_seq(): lax.ppermute(x, 'seq', [(i, (i + by) % seq_count) for i in range(seq_coun...  11.9 us
    pallas_call x1, Pallas kernels, local(): pl.pallas_call(functools.partial(far_kernel, seq_count), out_shape=(jax.S...  10.9 us
    pallas_call x1, Pallas kernels, local(): pl.pallas_call(functools.partial(own_kernel, seq_count), out_shape=(jax.S...  8.25 us
    ppermute x6, starting transfers between devices, swap_seq(): return lax.ppermute(x, 'seq', [(i, i ^ bit) for i in range(seq_count)])  6.78 us
    ppermute x4, starting transfers between devices, from_head(): lax.ppermute(x, 'head', [(i, (i - by) % head_axis) for i in range(head_ax...  6.01 us
    ppermute x4, starting transfers between devices, shift_seq(): lax.ppermute(x, 'seq', [(i, (i + by) % seq_count) for i in range(seq_coun...  4.11 us
  transfers between devices with their start and end apart: 14, of which 5 were waited for; matrix products, arithmetic and copies ran while one was open for 6% of the time, Pallas kernels for 24%

profile of v6, /device:TPU:0, one launch (start us, length us, event | category | flops | bytes accessed | tf_op | source)
XLA Modules:
  0.0 90.9 jit_solution(16075732426420807366)
XLA Ops:
  1.2 3.8 %prep.1 = (bf16[768,256]{1,0:T(8,128)(2,1)}, bf16[512,768]{1,0:T(8,128)(2,1)}, bf16[512,768]{1,0:T(8,128)(2,1)}) custom-call(s32[2]{0:T(128)} %pad_add_fusion.r_ref, bf16[768,128]{1,0:T(8,128)(2,1)} %k.1, bf16[768,128]{1,0:T(8,128)(2,1)} %v.1, bf16[4096,512]{1,0:T(8,128)(2,1)} %wq.1, bf16[4096,128]{1,0:T(8,128)(2,1)} %wk.1, bf16[4096,128]{1,0:T(8,128)(2,1)} %wv.1, ...), custom_call_target="tpu_custom_call" | custom-call | tf_op jit(solution)/shard_map/prep/pallas_call | solution.py:255
  5.0 3.0 %collective-permute-start.6 = (bf16[512,768]{1,0:T(8,128)(2,1)}, bf16[512,768]{1,0:T(8,128)(2,1)}, u32[]{:S(2)}, u32[]{:S(2)}) collective-permute-start(bf16[512,768]{1,0:T(8,128)(2,1)} %get-tuple-element.32), channel_id=1, source_target_pairs={{0,1},{1,0},{2,3},{3,2},{4,5},{5,4},{6,7},{7,6},{8,9},{9,8},{10,11... | collective-permute-start | bytes 2359304 | tf_op jit(solution)/shard_map/ppermute | solution.py:249
  8.0 1.5 %collective-permute-start.1 = (bf16[768,256]{1,0:T(8,128)(2,1)}, bf16[768,256]{1,0:T(8,128)(2,1)}, u32[]{:S(2)}, u32[]{:S(2)}) collective-permute-start(bf16[768,256]{1,0:T(8,128)(2,1)} %get-tuple-element.24), channel_id=1, source_target_pairs={{0,4},{2,6},{4,8},{6,10},{8,12},{10,14},{12,16},{14,18},{16,20},{1... | collective-permute-start | bytes 1179656 | tf_op jit(solution)/shard_map/ppermute | solution.py:243
  10.3 8.3 %own_stop.1 = (f32[2,512,384]{2,1,0:T(8,128)}, f32[2,384,256]{2,1,0:T(8,128)}, f32[2,4,384]{2,1,0:T(4,128)}, f32[2,4,384]{2,1,0:T(4,128)}) custom-call(s32[16,2]{1,0:T(8,128)} %copy.19.ids_ref, bf16[768,512]{1,0:T(8,128)(2,1)} %q_ref.3, bf16[768,128]{1,0:T(8,128)(2,1)} %k.1, bf16[768,128]{1,0:T(8,128)(2,1)} %v.1, bf16[768,512]{1,0:T(8,128)(2,1)} %o_ref.1, ...), custom_call_target="tpu_custom_call" | custom-call | flops 2264924160 | bytes 5242880 | tf_op jit(solution)/shard_map/own_stop/pallas_call | solution.py:285
  18.7 0.8 multiply_cosine_fusion
  19.4 6.4 %collective-permute-done.6.refs_0_ = bf16[512,768]{1,0:T(8,128)(2,1)} collective-permute-done((bf16[512,768]{1,0:T(8,128)(2,1)}, bf16[512,768]{1,0:T(8,128)(2,1)}, u32[]{:S(2)}, u32[]{:S(2)}) %collective-permute-start.6) | collective-permute-done | bytes 786464 | tf_op jit(solution)/shard_map/ppermute | solution.py:249
  25.8 1.8 %collective-permute-start.8 = (bf16[512,768]{1,0:T(8,128)(2,1)}, bf16[512,768]{1,0:T(8,128)(2,1)}, u32[]{:S(2)}, u32[]{:S(2)}) collective-permute-start(bf16[512,768]{1,0:T(8,128)(2,1)} %get-tuple-element.34.rest_0_), channel_id=1, source_target_pairs={{0,8},{2,10},{4,12},{6,14},{8,0},{10,2},{12,4},{14,6},{16,24},{18,... | collective-permute-start | bytes 2359304 | tf_op jit(solution)/shard_map/ppermute | solution.py:246
  27.6 1.5 %collective-permute-start.7 = (bf16[512,768]{1,0:T(8,128)(2,1)}, bf16[512,768]{1,0:T(8,128)(2,1)}, u32[]{:S(2)}, u32[]{:S(2)}) collective-permute-start(bf16[512,768]{1,0:T(8,128)(2,1)} %get-tuple-element.34.rest_0_), channel_id=1, source_target_pairs={{0,4},{2,6},{4,0},{6,2},{8,12},{10,14},{12,8},{14,10},{16,20},{18,... | collective-permute-start | bytes 2359304 | tf_op jit(solution)/shard_map/ppermute | solution.py:246
  29.1 1.5 %collective-permute-start.9 = (bf16[512,768]{1,0:T(8,128)(2,1)}, bf16[512,768]{1,0:T(8,128)(2,1)}, u32[]{:S(2)}, u32[]{:S(2)}) collective-permute-start(bf16[512,768]{1,0:T(8,128)(2,1)} %get-tuple-element.35), channel_id=1, source_target_pairs={{0,1},{1,0},{2,3},{3,2},{4,5},{5,4},{6,7},{7,6},{8,9},{9,8},{10,11... | collective-permute-start | bytes 2359304 | tf_op jit(solution)/shard_map/ppermute | solution.py:249
  30.6 0.8 pad_maximum_fusion.tab_ref
  31.4 10.9 %far_stops.1 = (bf16[768,512]{1,0:T(8,128)(2,1)}, bf16[768,256]{1,0:T(8,128)(2,1)}, bf16[768,256]{1,0:T(8,128)(2,1)}) custom-call(s32[16,2]{1,0:T(8,128)} %copy.19.ids_ref, bf16[768,512]{1,0:T(8,128)(2,1)} %q_ref.3, bf16[768,512]{1,0:T(8,128)(2,1)} %do_ref.3, f32[2,4,384]{2,1,0:T(4,128)} %get-tuple-element.21.norm_ref.refs_2_, ...), custom_call_target="tpu_custom_call" | custom-call | flops 3019898880 | bytes 6291456 | tf_op jit(solution)/shard_map/far_stops/pallas_call | solution.py:315
  42.5 1.8 %constant_dynamic-slice_fusion.1 = bf16[384,512]{1,0:T(8,128)(2,1)} fusion(bf16[768,512]{1,0:T(8,128)(2,1)} %get-tuple-element.25.qg, s32[]{:T(128)S(6)} %select_n.9), kind=kLoop, calls=%fused_computation.6 | loop fusion | bytes 786436 | tf_op jit(solution)/shard_map/dynamic_slice | solution.py:337
  44.8 3.3 %collective-permute-done.3.rest_0_.refs_3_ = bf16[768,256]{1,0:T(8,128)(2,1)S(1)} collective-permute-done((bf16[768,256]{1,0:T(8,128)(2,1)}, bf16[768,256]{1,0:T(8,128)(2,1)S(1)}, u32[]{:S(2)}, u32[]{:S(2)}) %collective-permute-start.3) | collective-permute-done | bytes 393248 | tf_op jit(solution)/shard_map/ppermute | solution.py:243
  48.1 2.3 %collective-permute-start.10 = (bf16[512,768]{1,0:T(8,128)(2,1)}, bf16[512,768]{1,0:T(8,128)(2,1)}, u32[]{:S(2)}, u32[]{:S(2)}) collective-permute-start(bf16[512,768]{1,0:T(8,128)(2,1)} %get-tuple-element.34.rest_0_), channel_id=1, source_target_pairs={{0,2},{2,0},{4,6},{6,4},{8,10},{10,8},{12,14},{14,12},{16,18},{18,... | collective-permute-start | bytes 2359304 | tf_op jit(solution)/shard_map/ppermute | solution.py:246
  50.4 0.7 collective-permute-start.11
  51.6 4.3 %collective-permute-done.2.after_ref.qo = bf16[384,512]{1,0:T(8,128)(2,1)} collective-permute-done((bf16[384,512]{1,0:T(8,128)(2,1)}, bf16[384,512]{1,0:T(8,128)(2,1)}, u32[]{:S(2)}, u32[]{:S(2)}) %collective-permute-start.2) | collective-permute-done | bytes 393248 | tf_op jit(solution)/shard_map/ppermute | solution.py:249
  56.0 2.5 %collective-permute-start.4 = (bf16[768,256]{1,0:T(8,128)(2,1)}, bf16[768,256]{1,0:T(8,128)(2,1)S(1)}, u32[]{:S(2)}, u32[]{:S(2)}) collective-permute-start(bf16[768,256]{1,0:T(8,128)(2,1)} %get-tuple-element.28), channel_id=1, source_target_pairs={{0,28},{2,30},{4,0},{6,2},{8,4},{10,6},{12,8},{14,10},{16,12},{18,... | collective-permute-start | bytes 1179656 | tf_op jit(solution)/shard_map/ppermute | solution.py:243
  58.4 8.6 %collective-permute-done.4.rest_1_ = bf16[768,256]{1,0:T(8,128)(2,1)S(1)} collective-permute-done((bf16[768,256]{1,0:T(8,128)(2,1)}, bf16[768,256]{1,0:T(8,128)(2,1)S(1)}, u32[]{:S(2)}, u32[]{:S(2)}) %collective-permute-start.4) | collective-permute-done | bytes 393248 | tf_op jit(solution)/shard_map/ppermute | solution.py:243
  67.0 0.7 copy-done.1
  67.7 2.7 %finish_keys.1 = (bf16[768,128]{1,0:T(8,128)(2,1)}, bf16[768,128]{1,0:T(8,128)(2,1)}, bf16[768,256]{1,0:T(8,128)(2,1)}) custom-call(f32[2,64,768]{2,1,0:T(8,128)} %pad_maximum_fusion.tab_ref, f32[2,384,256]{2,1,0:T(8,128)} %get-tuple-element.26.kv0_ref, bf16[384,512]{1,0:T(8,128)(2,1)} %collective-permute-done.2.after_ref.qo, bf16[768,256]{1,0:T(8,128)(2,1)} %copy-done, ...), custom_call_target="tpu_custom_call" | custom-call | tf_op jit(solution)/shard_map/finish_keys/pallas_call | solution.py:350
  70.5 0.9 %constant_dynamic-slice_fusion = bf16[384,256]{1,0:T(8,128)(2,1)S(1)} fusion(bf16[768,256]{1,0:T(8,128)(2,1)} %get-tuple-element.31, s32[]{:T(128)S(6)} %select_n.9), kind=kLoop, calls=%fused_computation.5 | loop fusion | bytes 393220 | tf_op jit(solution)/shard_map/dynamic_slice | solution.py:337
  71.4 1.0 %collective-permute-start.5 = (bf16[384,256]{1,0:T(8,128)(2,1)S(1)}, bf16[384,256]{1,0:T(8,128)(2,1)S(1)}, u32[]{:S(2)}, u32[]{:S(2)}) collective-permute-start(bf16[384,256]{1,0:T(8,128)(2,1)S(1)} %constant_dynamic-slice_fusion), channel_id=1, source_target_pairs={{0,1},{1,0},{2,3},{3,2},{4,5},{5,4},{6,7},{7,6},{8,9},{9,8},{10,11... | collective-permute-start | bytes 589832 | tf_op jit(solution)/shard_map/ppermute | solution.py:249
  72.4 4.7 %collective-permute-done.5.kvo = bf16[384,256]{1,0:T(8,128)(2,1)S(1)} collective-permute-done((bf16[384,256]{1,0:T(8,128)(2,1)S(1)}, bf16[384,256]{1,0:T(8,128)(2,1)S(1)}, u32[]{:S(2)}, u32[]{:S(2)}) %collective-permute-start.5) | collective-permute-done | bytes 196640 | tf_op jit(solution)/shard_map/ppermute | solution.py:249
  77.8 12.9 %project.1 = bf16[384,4096]{1,0:T(8,128)(2,1)} custom-call(s32[2]{0:T(128)} %pad_add_fusion.r_ref, bf16[768,512]{1,0:T(8,128)(2,1)} %get-tuple-element.25.qg, bf16[768,128]{1,0:T(8,128)(2,1)} %get-tuple-element.19.kg, bf16[768,128]{1,0:T(8,128)(2,1)} %get-tuple-element.20.vg, bf16[384,512]{1,0:T(8,128)(2,1)} %collective-permute-done.2.after_ref.qo, ...), custom_call_target="tpu_custom_call" | custom-call | tf_op jit(solution)/shard_map/project/pallas_call | solution.py:369
  (29 shorter events, 3.5 us)
Async XLA Ops:
  1.2 8.2 %copy-start.3 = (s32[16,2]{0,1:T(2,128)S(1)}, s32[16,2]{0,1:T(2,128)}, u32[]{:S(2)}) copy-start(s32[16,2]{0,1:T(2,128)} %param.16) | copy-start | bytes 388
  5.0 20.8 %collective-permute-start.6 = (bf16[512,768]{1,0:T(8,128)(2,1)}, bf16[512,768]{1,0:T(8,128)(2,1)}, u32[]{:S(2)}, u32[]{:S(2)}) collective-permute-start(bf16[512,768]{1,0:T(8,128)(2,1)} %get-tuple-element.32), channel_id=1, source_target_pairs={{0,1},{1,0},{2,3},{3,2},{4,5},{5,4},{6,7},{7,6},{8,9},{9,8},{10,11... | collective-permute-start | bytes 2359304 | tf_op jit(solution)/shard_map/ppermute | solution.py:249
  8.0 23.5 %collective-permute-start.1 = (bf16[768,256]{1,0:T(8,128)(2,1)}, bf16[768,256]{1,0:T(8,128)(2,1)}, u32[]{:S(2)}, u32[]{:S(2)}) collective-permute-start(bf16[768,256]{1,0:T(8,128)(2,1)} %get-tuple-element.24), channel_id=1, source_target_pairs={{0,4},{2,6},{4,8},{6,10},{8,12},{10,14},{12,16},{14,18},{16,20},{1... | collective-permute-start | bytes 1179656 | tf_op jit(solution)/shard_map/ppermute | solution.py:243
  9.5 22.0 %collective-permute-start = (bf16[768,256]{1,0:T(8,128)(2,1)}, bf16[768,256]{1,0:T(8,128)(2,1)}, u32[]{:S(2)}, u32[]{:S(2)}) collective-permute-start(bf16[768,256]{1,0:T(8,128)(2,1)} %get-tuple-element.24), channel_id=1, source_target_pairs={{0,2},{2,4},{4,6},{6,8},{8,10},{10,12},{12,14},{14,16},{16,18},{18... | collective-permute-start | bytes 1179656 | tf_op jit(solution)/shard_map/ppermute | solution.py:243
  25.8 24.6 %collective-permute-start.8 = (bf16[512,768]{1,0:T(8,128)(2,1)}, bf16[512,768]{1,0:T(8,128)(2,1)}, u32[]{:S(2)}, u32[]{:S(2)}) collective-permute-start(bf16[512,768]{1,0:T(8,128)(2,1)} %get-tuple-element.34.rest_0_), channel_id=1, source_target_pairs={{0,8},{2,10},{4,12},{6,14},{8,0},{10,2},{12,4},{14,6},{16,24},{18,... | collective-permute-start | bytes 2359304 | tf_op jit(solution)/shard_map/ppermute | solution.py:246
  27.6 22.8 %collective-permute-start.7 = (bf16[512,768]{1,0:T(8,128)(2,1)}, bf16[512,768]{1,0:T(8,128)(2,1)}, u32[]{:S(2)}, u32[]{:S(2)}) collective-permute-start(bf16[512,768]{1,0:T(8,128)(2,1)} %get-tuple-element.34.rest_0_), channel_id=1, source_target_pairs={{0,4},{2,6},{4,0},{6,2},{8,12},{10,14},{12,8},{14,10},{16,20},{18,... | collective-permute-start | bytes 2359304 | tf_op jit(solution)/shard_map/ppermute | solution.py:246
  29.1 21.3 %collective-permute-start.9 = (bf16[512,768]{1,0:T(8,128)(2,1)}, bf16[512,768]{1,0:T(8,128)(2,1)}, u32[]{:S(2)}, u32[]{:S(2)}) collective-permute-start(bf16[512,768]{1,0:T(8,128)(2,1)} %get-tuple-element.35), channel_id=1, source_target_pairs={{0,1},{1,0},{2,3},{3,2},{4,5},{5,4},{6,7},{7,6},{8,9},{9,8},{10,11... | collective-permute-start | bytes 2359304 | tf_op jit(solution)/shard_map/ppermute | solution.py:249
  42.3 5.8 %collective-permute-start.3 = (bf16[768,256]{1,0:T(8,128)(2,1)}, bf16[768,256]{1,0:T(8,128)(2,1)S(1)}, u32[]{:S(2)}, u32[]{:S(2)}) collective-permute-start(bf16[768,256]{1,0:T(8,128)(2,1)} %get-tuple-element.27), channel_id=1, source_target_pairs={{0,30},{2,0},{4,2},{6,4},{8,6},{10,8},{12,10},{14,12},{16,14},{18,... | collective-permute-start | bytes 1179656 | tf_op jit(solution)/shard_map/ppermute | solution.py:243
  44.3 11.7 %collective-permute-start.2 = (bf16[384,512]{1,0:T(8,128)(2,1)}, bf16[384,512]{1,0:T(8,128)(2,1)}, u32[]{:S(2)}, u32[]{:S(2)}) collective-permute-start(bf16[384,512]{1,0:T(8,128)(2,1)} %constant_dynamic-slice_fusion.1), channel_id=1, source_target_pairs={{0,1},{1,0},{2,3},{3,2},{4,5},{5,4},{6,7},{7,6},{8,9},{9,8},{10,11... | collective-permute-start | bytes 1179656 | tf_op jit(solution)/shard_map/ppermute | solution.py:249
  48.1 2.3 %copy-start = (bf16[768,256]{1,0:T(8,128)(2,1)}, bf16[768,256]{1,0:T(8,128)(2,1)S(1)}, u32[]{:S(2)}) copy-start(bf16[768,256]{1,0:T(8,128)(2,1)S(1)} %collective-permute-done.3.rest_0_.refs_3_) | copy-start | bytes 1179652
  48.1 29.0 %collective-permute-start.10 = (bf16[512,768]{1,0:T(8,128)(2,1)}, bf16[512,768]{1,0:T(8,128)(2,1)}, u32[]{:S(2)}, u32[]{:S(2)}) collective-permute-start(bf16[512,768]{1,0:T(8,128)(2,1)} %get-tuple-element.34.rest_0_), channel_id=1, source_target_pairs={{0,2},{2,0},{4,6},{6,4},{8,10},{10,8},{12,14},{14,12},{16,18},{18,... | collective-permute-start | bytes 2359304 | tf_op jit(solution)/shard_map/ppermute | solution.py:246
  50.4 26.7 %collective-permute-start.11 = (bf16[512,768]{1,0:T(8,128)(2,1)}, bf16[512,768]{1,0:T(8,128)(2,1)}, u32[]{:S(2)}, u32[]{:S(2)}) collective-permute-start(bf16[512,768]{1,0:T(8,128)(2,1)} %get-tuple-element.36.rest_1_), channel_id=1, source_target_pairs={{0,2},{2,0},{4,6},{6,4},{8,10},{10,8},{12,14},{14,12},{16,18},{18,... | collective-permute-start | bytes 2359304 | tf_op jit(solution)/shard_map/ppermute | solution.py:246
  51.1 26.0 %collective-permute-start.12 = (bf16[512,768]{1,0:T(8,128)(2,1)}, bf16[512,768]{1,0:T(8,128)(2,1)}, u32[]{:S(2)}, u32[]{:S(2)}) collective-permute-start(bf16[512,768]{1,0:T(8,128)(2,1)} %get-tuple-element.37.rest_2_), channel_id=1, source_target_pairs={{0,2},{2,0},{4,6},{6,4},{8,10},{10,8},{12,14},{14,12},{16,18},{18,... | collective-permute-start | bytes 2359304 | tf_op jit(solution)/shard_map/ppermute | solution.py:246
  51.1 26.0 %collective-permute-start.13 = (bf16[512,768]{1,0:T(8,128)(2,1)}, bf16[512,768]{1,0:T(8,128)(2,1)}, u32[]{:S(2)}, u32[]{:S(2)}) collective-permute-start(bf16[512,768]{1,0:T(8,128)(2,1)} %get-tuple-element.38.rest_3_), channel_id=1, source_target_pairs={{0,2},{2,0},{4,6},{6,4},{8,10},{10,8},{12,14},{14,12},{16,18},{18,... | collective-permute-start | bytes 2359304 | tf_op jit(solution)/shard_map/ppermute | solution.py:246
  56.0 11.0 %collective-permute-start.4 = (bf16[768,256]{1,0:T(8,128)(2,1)}, bf16[768,256]{1,0:T(8,128)(2,1)S(1)}, u32[]{:S(2)}, u32[]{:S(2)}) collective-permute-start(bf16[768,256]{1,0:T(8,128)(2,1)} %get-tuple-element.28), channel_id=1, source_target_pairs={{0,28},{2,30},{4,0},{6,2},{8,4},{10,6},{12,8},{14,10},{16,12},{18,... | collective-permute-start | bytes 1179656 | tf_op jit(solution)/shard_map/ppermute | solution.py:243
  67.0 0.7 copy-start.1
  71.4 5.7 %collective-permute-start.5 = (bf16[384,256]{1,0:T(8,128)(2,1)S(1)}, bf16[384,256]{1,0:T(8,128)(2,1)S(1)}, u32[]{:S(2)}, u32[]{:S(2)}) collective-permute-start(bf16[384,256]{1,0:T(8,128)(2,1)S(1)} %constant_dynamic-slice_fusion), channel_id=1, source_target_pairs={{0,1},{1,0},{2,3},{3,2},{4,5},{5,4},{6,7},{7,6},{8,9},{9,8},{10,11... | collective-permute-start | bytes 589832 | tf_op jit(solution)/shard_map/ppermute | solution.py:249
  77.1 0.7 copy-start.2
